TPU v7x, 32 devices: a whole 2x2x4 slice. The times are simulated.
32 devices in a mesh: gx: 4 (over y, x), gy: 8 (over z, core).
Axes of the slice: x: 2, y: 2, z: 4, core: 2. Of those that a mesh axis runs over, the one named last changes fastest.
Arguments:
- initial_state: float32 [3, 128, 24576], P(None, 'gx', 'gy'), may hold values from -6 to 6
- beam_dir: float32 [3, 128], P(None, ('gx', 'gy')), may hold values from -4 to 4
- gate_obs: float32 [3, 32, 32, 128], P(None, ('gx', 'gy')), may hold values from -6 to 6
- slot_beam: int32 [32, 32, 128], P(('gx', 'gy')), may hold values from -1 to 3, as said below
- slot_cell: int32 [32, 32, 128], P(('gx', 'gy')), may hold values from 0 to 98303, as said below
Outputs:
- gradient: float32 [3, 128, 24576], P(None, 'gx', 'gy')
Inputs may be any that keep to these rules, and one draw needn't show every extreme that they name: `slot_beam`: each of an owner's 4 beams fills exactly 512 slots over all of that owner's lists. In every list the used slots come first. Each owner's list for one common tile is full, so that tile receives 128 used slots from every owner. `slot_cell`: A cell index within the tile, of 32 x 32 x 96 cells with the streamwise index slowest and the vertical fastest; empty slots also hold a valid index.
All inputs are finite; a program needn't handle non-finite values.
Results may differ from a plain program's by a relative error of at most 0.00015.
Values sent between devices are 32-bit elements; how exact they have to be, the bound alone decides.
No kernel may reach another device: no remote copies, remote signals or barrier semaphores. Data moves between devices by JAX's collectives and lax.ppermute only.
A program may use at most 128 MiB of HBM per device.

v0:
```python
import functools

import jax
import jax.numpy as jnp
from jax import lax
from jax.experimental import pallas as pl
from jax.experimental.pallas import tpu as pltpu
from jax.sharding import PartitionSpec as P

NZ = 96
GATES = 512
STEPS = 3
LANES = 128
CX = 32
CY = 32
COLUMNS = CX * CY
RIM = 5
PAD = 8
XH = CX + 2 * PAD
YH = CY + 2 * RIM
PACKED = CX * NZ // LANES
FRIM = 3
FH = CY + 2 * FRIM
FIELDS = 3 * STEPS
BLOCK = 512
F32 = jnp.float32
BF16 = jnp.bfloat16
AXES = ("gx", "gy")
VMEM_LIMIT = 60 * 1024 * 1024


def call(kernel, outs, scratch=(), flops=0):
    return pl.pallas_call(
        kernel,
        out_shape=outs,
        scratch_shapes=list(scratch),
        compiler_params=pltpu.CompilerParams(vmem_limit_bytes=VMEM_LIMIT),
        cost_estimate=pl.CostEstimate(flops=flops, bytes_accessed=1 << 20, transcendentals=0),
    )


def shape(*dims):
    return jax.ShapeDtypeStruct(dims, F32)


def lane_of(rows=8):
    return lax.broadcasted_iota(jnp.int32, (rows, LANES), 1)


def pack(put, block):
    lane = lane_of()
    last = block[24:32]
    for j in range(3):
        tail = pltpu.roll(last, 96 - 32 * j, axis=1)
        put(8 * j, jnp.where(lane < NZ, block[8 * j : 8 * j + 8], tail))


def unpack(rows):
    lane = lane_of()
    last = jnp.zeros((8, LANES), F32)
    parts = []
    for j in range(3):
        piece = rows[8 * j : 8 * j + 8]
        parts.append(jnp.where(lane < NZ, piece, 0.0))
        moved = pltpu.roll(piece, (32 * j - 96) % LANES, axis=1)
        last = jnp.where((lane >= 32 * j) & (lane < 32 * j + 32), moved, last)
    return jnp.concatenate(parts + [last], axis=0)


def column_block(ref, comp, y):
    return ref[comp, :, NZ * y : NZ * y + NZ]


def widen(block):
    return jnp.concatenate([block, jnp.zeros((block.shape[0], LANES - NZ), F32)], axis=1)


def corner_rows(rim):
    rows, out = 0, []
    for comp in range(3):
        for dist in range(1, rim):
            out.append((comp, dist, rows, rim - dist))
            rows += 2 * (rim - dist)
    return out, rows


STATE_CORNERS, STATE_CORNER_ROWS = corner_rows(RIM)
STATE_PIECE = 3 * RIM * PACKED + 64
FORCE_BLOCKS = [(n, c, i) for n in range(STEPS) for c in range(3) for i in range(n + 1)]
FORCE_CORNERS = [
    (n, c, dist, side, k)
    for n in range(STEPS)
    for c in range(3)
    for dist in range(1, n + 1)
    for side in range(2)
    for k in range(1, n + 2 - dist)
]
FORCE_PIECE = len(FORCE_BLOCKS) * PACKED + 24


def prepare_kernel(state, beam_dir, obs, beam, cell, slots, first_rows, last_rows):
    beams = beam_dir.shape[1]
    owned = beam[0]
    used = owned >= 0
    masks = [owned == k for k in range(beams)]

    def spread(values):
        total = jnp.zeros(owned.shape, F32)
        for k in range(beams):
            total = jnp.where(masks[k], values[k], total)
        return total

    slots[:, 0, :] = cell[0].astype(F32)
    slots[:, 1, :] = owned.astype(F32)
    for n in range(STEPS):
        seen = obs[n, 0]
        means = [jnp.sum(jnp.where(m, seen, 0.0), keepdims=True) / GATES for m in masks]
        slots[:, 2 + n, :] = jnp.where(used, seen - spread(means), 0.0)
    for c in range(3):
        slots[:, 5 + c, :] = spread([beam_dir[c : c + 1, k : k + 1] for k in range(beams)])
    for c in range(3):
        first_rows[RIM * c : RIM * c + RIM, :] = state[c, 0:RIM, :]
        last_rows[RIM * c : RIM * c + RIM, :] = state[c, CX - RIM : CX, :]
    first_rows[3 * RIM : 16, :] = jnp.zeros((1, CY * NZ), F32)
    last_rows[3 * RIM : 16, :] = jnp.zeros((1, CY * NZ), F32)


def state_rim_kernel(state, before, after, first_layers, last_layers):
    for out, layer_of in ((first_layers, lambda d: d - 1), (last_layers, lambda d: CY - d)):
        for c in range(3):
            for dist in range(1, RIM + 1):
                base = (c * RIM + dist - 1) * PACKED

                def put(row, rows, base=base, out=out):
                    out[base + row : base + row + 8, :] = rows

                pack(put, widen(column_block(state, c, layer_of(dist))))
        base = 3 * RIM * PACKED
        out[base : base + 64, :] = jnp.zeros((64, LANES), F32)
        for c, dist, row, side in STATE_CORNERS:
            lanes = slice(NZ * layer_of(dist), NZ * layer_of(dist) + NZ)
            out[base + row : base + row + side, 0:NZ] = before[RIM * c + dist : RIM * c + RIM, lanes]
            out[base + row + side : base + row + 2 * side, 0:NZ] = after[RIM * c : RIM * c + side, lanes]


def row_mask(x_place, x_count):
    row = lax.broadcasted_iota(jnp.int32, (XH, LANES), 0)
    lane = lax.broadcasted_iota(jnp.int32, (XH, LANES), 1)
    low = jnp.where(x_place == 0, PAD, 0)
    high = jnp.where(x_place == x_count - 1, PAD + CX, XH)
    return jnp.where((row >= low) & (row < high) & (lane < NZ), 1.0, 0.0).astype(F32)


def layer_mask(y, y_place, y_count):
    outside = ((y < 0) & (y_place == 0)) | ((y >= CY) & (y_place == y_count - 1))
    return jnp.where(outside, 0.0, 1.0).astype(F32)


def next_row(v):
    return pltpu.roll(v, v.shape[0] - 1, axis=0)


def last_row(v):
    return pltpu.roll(v, 1, axis=0)


def next_level(v):
    return pltpu.roll(v, LANES - 1, axis=1)


def last_level(v):
    return pltpu.roll(v, 1, axis=1)


def step_forward(src, dst, low, high, mask, places):
    def layer(i, carry):
        y = i + low
        centre = [src[c, y + RIM] for c in range(3)]
        plus = [0.1 - 0.1 * v for v in centre]
        minus = [0.1 + 0.1 * v for v in centre]
        keep = mask * layer_mask(y, places[2], places[3])
        for c in range(3):
            v = centre[c]
            total = 0.4 * v
            total = total + plus[0] * next_row(v) + minus[0] * last_row(v)
            total = total + plus[1] * src[c, y + RIM + 1] + minus[1] * src[c, y + RIM - 1]
            total = total + plus[2] * next_level(v) + minus[2] * last_level(v)
            dst[c, y + RIM] = total * keep
        return carry

    lax.fori_loop(0, high - low, layer, 0)


def mesh_places():
    return (
        lax.axis_index("gx"),
        lax.axis_size("gx"),
        lax.axis_index("gy"),
        lax.axis_size("gy"),
    )


def slot_columns(slots, row):
    cell = slots[row, 0:1, :]
    x = ((cell + 0.5) * (1.0 / (CY * NZ))).astype(jnp.int32)
    rest = cell.astype(jnp.int32) - x * (CY * NZ)
    y = ((rest.astype(F32) + 0.5) * (1.0 / NZ)).astype(jnp.int32)
    return y * CX + x, rest - y * NZ


def column_hits(columns):
    place = lax.broadcasted_iota(jnp.int32, (COLUMNS, columns.shape[1]), 0)
    return jnp.where(place == columns, 1.0, 0.0).astype(BF16)


def block_places(slots, block):
    rows = [slot_columns(slots, block * (BLOCK // LANES) + r) for r in range(BLOCK // LANES)]
    columns = jnp.concatenate([r[0] for r in rows], axis=1)
    level = jnp.concatenate([r[1] for r in rows], axis=1)
    here = lax.broadcasted_iota(jnp.int32, (NZ, BLOCK), 0) == level
    return column_hits(columns), here


def block_values(slots, block, which):
    rows = [slots[block * (BLOCK // LANES) + r, which : which + 1, :] for r in range(BLOCK // LANES)]
    return jnp.concatenate(rows, axis=1)


def forward_kernel(
    beams, per_row, state, before, after, below, above, slots, seen, sums, s0, s1, s2, s3, table
):
    places = mesh_places()
    mask = row_mask(places[0], places[1])
    s0[...] = jnp.zeros(s0.shape, F32)
    for c in range(3):
        for y in range(CY):
            lanes = slice(NZ * y, NZ * y + NZ)
            s0[c, RIM + y, PAD : PAD + CX, 0:NZ] = state[c, :, lanes]
            s0[c, RIM + y, PAD - RIM : PAD, 0:NZ] = before[RIM * c : RIM * c + RIM, lanes]
            s0[c, RIM + y, PAD + CX : PAD + CX + RIM, 0:NZ] = after[RIM * c : RIM * c + RIM, lanes]
    for piece, layer_of in ((above, lambda d: RIM + CY - 1 + d), (below, lambda d: RIM - d)):
        for c in range(3):
            for dist in range(1, RIM + 1):
                base = (c * RIM + dist - 1) * PACKED
                s0[c, layer_of(dist), PAD : PAD + CX, :] = unpack(piece[base : base + PACKED, :])
        base = 3 * RIM * PACKED
        for c, dist, row, side in STATE_CORNERS:
            s0[c, layer_of(dist), PAD - side : PAD, :] = piece[base + row : base + row + side, :]
            s0[c, layer_of(dist), PAD + CX : PAD + CX + side, :] = piece[
                base + row + side : base + row + 2 * side, :
            ]
    step_forward(s0, s1, -4, CY + 4, mask, places)
    step_forward(s1, s2, -3, CY + 3, mask, places)
    step_forward(s2, s3, 0, CY, mask, places)

    half = FIELDS * NZ
    for n, field in enumerate((s1, s2, s3)):
        for c in range(3):
            tile = field[c, RIM : RIM + CY, PAD : PAD + CX, :].reshape(COLUMNS, LANES)
            turned = tile.T[0:NZ]
            high = turned.astype(BF16)
            base = (3 * n + c) * NZ
            table[base : base + NZ, :] = high
            table[half + base : half + base + NZ, :] = (turned - high.astype(F32)).astype(BF16)

    def gather(block, carry):
        hits, here = block_places(slots, block)
        found = jnp.dot(table[...], hits, preferred_element_type=F32)
        weights = [block_values(slots, block, 5 + c) for c in range(3)]
        for n in range(STEPS):
            total = jnp.zeros((1, BLOCK), F32)
            for c in range(3):
                base = (3 * n + c) * NZ
                both = found[base : base + NZ] + found[half + base : half + base + NZ]
                value = jnp.sum(jnp.where(here, both, 0.0), axis=0, keepdims=True)
                total = total + weights[c] * value
            for r in range(BLOCK // LANES):
                seen[n, pl.ds(block * (BLOCK // LANES) + r, 1), :] = total[:, LANES * r : LANES * r + LANES]
        return carry

    rows = slots.shape[0]
    lax.fori_loop(0, rows * LANES // BLOCK, gather, 0)

    beam = row_beam(beams, per_row, slots)
    lane = lax.broadcasted_iota(jnp.int32, (rows, LANES), 1)
    partial = jnp.zeros((rows, LANES), F32)
    for n in range(STEPS):
        values = seen[n]
        for k in range(per_row):
            one = jnp.sum(jnp.where(beam == k, values, 0.0), axis=1, keepdims=True)
            partial = jnp.where(lane == n * per_row + k, one, partial)
    turned = jnp.concatenate([partial, jnp.zeros((LANES - rows, LANES), F32)], axis=0).T
    per_line = LANES // rows
    sums[...] = jnp.zeros(sums.shape, F32)
    for line in range(STEPS * per_row // per_line):
        total = turned[line * per_line : line * per_line + 1]
        for k in range(1, per_line):
            one = turned[line * per_line + k : line * per_line + k + 1]
            total = total + pltpu.roll(one, rows * k, axis=1)
        sums[:, line : line + 1, :] = jnp.broadcast_to(total[None], (sums.shape[0], 1, LANES))


def row_beam(beams, per_row, slots):
    group = per_row // beams
    lane = lax.broadcasted_iota(jnp.int32, (slots.shape[0], LANES), 1)
    beam = slots[:, 1, :].astype(jnp.int32)
    for g in range(1, group):
        beam = beam + jnp.where(lane >= g * (LANES // group), beams, 0)
    return beam


def force_kernel(beams, per_row, slots, seen, sums, force, first_rows, last_rows, total, weight):
    rows = slots.shape[0]
    per_line = LANES // rows
    lines = jnp.sum(sums[...], axis=0) / GATES
    count = STEPS * per_row
    spread = []
    for k in range(count):
        line = lines[k // per_line : k // per_line + 1]
        spread.append(pltpu.roll(line, (-rows * (k % per_line)) % LANES, axis=1))
    spread.append(jnp.zeros((LANES - count, LANES), F32))
    means = jnp.concatenate(spread, axis=0).T[0:rows]
    beam = row_beam(beams, per_row, slots)
    misfit = []
    for n in range(STEPS):
        mean = jnp.zeros((rows, LANES), F32)
        for k in range(per_row):
            one = means[:, n * per_row + k : n * per_row + k + 1]
            mean = jnp.where(beam == k, one, mean)
        misfit.append(seen[n] - mean - slots[:, 2 + n, :])
    for n in range(STEPS):
        for c in range(3):
            weight[3 * n + c] = slots[:, 5 + c, :] * misfit[n]

    total[...] = jnp.zeros(total.shape, F32)

    def scatter(block, carry):
        hits, here = block_places(slots, block)
        high_rows, low_rows = [], []
        for f in range(FIELDS):
            value = jnp.concatenate(
                [weight[f, pl.ds(block * (BLOCK // LANES) + r, 1), :] for r in range(BLOCK // LANES)],
                axis=1,
            )
            high = value.astype(BF16).astype(F32)
            high_rows.append(jnp.where(here, high, 0.0).astype(BF16))
            low_rows.append(jnp.where(here, value - high, 0.0).astype(BF16))
        table = jnp.concatenate(high_rows + low_rows, axis=0)
        added = lax.dot_general(table, hits, (((1,), (1,)), ((), ())), preferred_element_type=F32)
        for f in range(FIELDS):
            half = FIELDS * NZ
            total[f, 0:NZ, :] += added[NZ * f : NZ * f + NZ] + added[half + NZ * f : half + NZ * f + NZ]
        return carry

    lax.fori_loop(0, rows * LANES // BLOCK, scatter, 0)
    for f in range(FIELDS):
        force[f] = total[f].T.reshape(CY, CX, LANES)
    for out, row_of in ((first_rows, lambda i: i), (last_rows, lambda i: CX - 1 - i)):
        for b, (n, c, i) in enumerate(FORCE_BLOCKS):

            def put(row, rows, b=b, out=out):
                out[b, row : row + 8, :] = rows

            pack(put, force[3 * n + c, :, row_of(i), :])


def rim_rows(piece, which):
    return unpack(piece[which])


def force_rim_kernel(force, before, after, first_layers, last_layers):
    index = {key: b for b, key in enumerate(FORCE_BLOCKS)}
    for out, layer_of in ((first_layers, lambda d: d - 1), (last_layers, lambda d: CY - d)):
        for b, (n, c, i) in enumerate(FORCE_BLOCKS):

            def put(row, rows, b=b, out=out):
                out[b * PACKED + row : b * PACKED + row + 8, :] = rows

            pack(put, force[3 * n + c, layer_of(i + 1)])
        base = len(FORCE_BLOCKS) * PACKED
        for row, (n, c, dist, side, k) in enumerate(FORCE_CORNERS):
            piece = (before, after)[side]
            block = unpack(piece[index[(n, c, k - 1)]])
            y = layer_of(dist)
            out[base + row : base + row + 1, :] = block[y : y + 1]


def backward_kernel(force, before, after, below, above, s0, s1, s2, out, a3, a2, a1, a0):
    places = mesh_places()
    mask = row_mask(places[0], places[1])
    adjoints = (a1, a2, a3)
    for n in range(STEPS):
        adjoints[n][...] = jnp.zeros(adjoints[n].shape, F32)
        for c in range(3):
            adjoints[n][c, FRIM : FRIM + CY, PAD : PAD + CX, :] = force[3 * n + c]
    for b, (n, c, i) in enumerate(FORCE_BLOCKS):
        adjoints[n][c, FRIM : FRIM + CY, PAD - 1 - i, :] = unpack(before[b])
        adjoints[n][c, FRIM : FRIM + CY, PAD + CX + i, :] = unpack(after[b])
    for piece, layer_of in ((above, lambda d: FRIM + CY - 1 + d), (below, lambda d: FRIM - d)):
        for b, (n, c, i) in enumerate(FORCE_BLOCKS):
            adjoints[n][c, layer_of(i + 1), PAD : PAD + CX, :] = unpack(piece[b * PACKED : b * PACKED + PACKED, :])
        base = len(FORCE_BLOCKS) * PACKED
        for row, (n, c, dist, side, k) in enumerate(FORCE_CORNERS):
            x = (PAD - k, PAD + CX - 1 + k)[side]
            adjoints[n][c, layer_of(dist), x : x + 1, :] = piece[base + row : base + row + 1, :]

    def pull(field, source, target, low, high, add):
        def layer(i, carry):
            y = i + low
            v = [field[c, y + RIM] for c in range(3)]
            v_next = [field[c, y + RIM + 1] for c in range(3)]
            v_last = [field[c, y + RIM - 1] for c in range(3)]
            a = [source[c, y + FRIM] for c in range(3)]
            slopes = [
                [next_row(f) - last_row(f) for f in v],
                [n - p for n, p in zip(v_next, v_last)],
                [next_level(f) - last_level(f) for f in v],
            ]
            keep = mask * layer_mask(y, places[2], places[3])
            from_next = [0.1 + 0.1 * f for f in v]
            from_last = [0.1 - 0.1 * f for f in v]
            y_next = 0.1 + 0.1 * v_next[1]
            y_last = 0.1 - 0.1 * v_last[1]
            for c in range(3):
                bend = slopes[c][0] * a[0] + slopes[c][1] * a[1] + slopes[c][2] * a[2]
                total = 0.4 * a[c] - 0.1 * bend
                total = total + next_row(from_next[0] * a[c]) + last_row(from_last[0] * a[c])
                total = total + y_next * source[c, y + FRIM + 1] + y_last * source[c, y + FRIM - 1]
                total = total + next_level(from_next[2] * a[c]) + last_level(from_last[2] * a[c])
                if add:
                    total = total + target[c, y + FRIM]
                target[c, y + FRIM] = total * keep
            return carry

        lax.fori_loop(0, high - low, layer, 0)

    pull(s2, a3, a2, -2, CY + 2, True)
    pull(s1, a2, a1, -1, CY + 1, True)
    pull(s0, a1, a0, 0, CY, False)
    for c in range(3):
        for y in range(CY):
            out[c, :, NZ * y : NZ * y + NZ] = a0[c, FRIM + y, PAD : PAD + CX, 0:NZ]


def shift(values, axis, by):
    count = lax.axis_size(axis)
    return lax.ppermute(values, axis, [(i, i + by) for i in range(count) if 0 <= i + by < count])


def local(initial_state, beam_dir, gate_obs, slot_beam, slot_cell):
    peers, capacity = slot_beam.shape[1:]
    group = LANES // capacity
    beams = beam_dir.shape[1]
    per_row = group * beams
    rows = peers // group
    rim_rows_shape = shape(16, CY * NZ)
    slots, first_rows, last_rows = call(
        prepare_kernel, (shape(peers, 8, capacity), rim_rows_shape, rim_rows_shape)
    )(initial_state, beam_dir, gate_obs, slot_beam, slot_cell)
    after = shift(first_rows, "gx", -1)
    before = shift(last_rows, "gx", 1)
    slots = lax.all_to_all(slots, AXES, split_axis=0, concat_axis=0, tiled=True)
    if group > 1:
        slots = slots.reshape(rows, group, 8, capacity).transpose(0, 2, 1, 3).reshape(rows, 8, LANES)
    piece = shape(STATE_PIECE, LANES)
    first_layers, last_layers = call(state_rim_kernel, (piece, piece))(initial_state, before, after)
    above = shift(first_layers, "gy", -1)
    below = shift(last_layers, "gy", 1)
    lines = -(-STEPS * per_row * rows // LANES // 8) * 8
    field = shape(3, YH, XH, LANES)
    seen, sums, s0, s1, s2 = call(
        functools.partial(forward_kernel, beams, per_row),
        (shape(STEPS, rows, LANES), shape(peers, lines, LANES), field, field, field),
        [pltpu.VMEM(field.shape, F32), pltpu.VMEM((2 * FIELDS * NZ, COLUMNS), BF16)],
    )(initial_state, before, after, below, above, slots)
    sums = lax.all_to_all(sums, AXES, split_axis=0, concat_axis=0, tiled=True)
    rim = shape(len(FORCE_BLOCKS), PACKED, LANES)
    force, first_rows, last_rows = call(
        functools.partial(force_kernel, beams, per_row),
        (shape(FIELDS, CY, CX, LANES), rim, rim),
        [pltpu.VMEM((FIELDS, LANES, COLUMNS), F32), pltpu.VMEM((FIELDS, rows, LANES), F32)],
    )(slots, seen, sums)
    after = shift(first_rows, "gx", -1)
    before = shift(last_rows, "gx", 1)
    piece = shape(FORCE_PIECE, LANES)
    first_layers, last_layers = call(force_rim_kernel, (piece, piece))(force, before, after)
    above = shift(first_layers, "gy", -1)
    below = shift(last_layers, "gy", 1)
    padded = pltpu.VMEM((3, FH, XH, LANES), F32)
    return call(backward_kernel, shape(*initial_state.shape), [padded] * 4)(
        force, before, after, below, above, s0, s1, s2
    )


def solution(mesh):
    in_specs = (
        P(None, "gx", "gy"),
        P(None, ("gx", "gy")),
        P(None, ("gx", "gy"), None, None),
        P(("gx", "gy"), None, None),
        P(("gx", "gy"), None, None),
    )
    out_specs = P(None, "gx", "gy")
    return jax.shard_map(local, mesh=mesh, in_specs=in_specs, out_specs=out_specs, check_vma=False)
```

profile of v0, /device:TPU:1, one launch (start us, length us, event | category | flops | bytes accessed | tf_op | source)
XLA Modules:
  0.0 153.6 jit_solution(451399012076668642)
XLA Ops:
  0.0 2.3 %shard_map.55 = (f32[32,8,128]{2,1,0:T(8,128)}, f32[16,3072]{1,0:T(8,128)}, f32[16,3072]{1,0:T(8,128)}) custom-call(f32[3,32,3072]{2,1,0:T(8,128)} %state.5, f32[3,4]{1,0:T(4,128)} %beam_dir.1, f32[3,1,32,128]{3,2,1,0:T(8,128)} %obs.1, s32[1,32,128]{2,1,0:T(8,128)} %beam.1, s32[1,32,128]{2,1,0:T(8,128)} %cell.1), custom_call_target="tpu_custom_call" | custom-call | bytes 1048576 | tf_op jit(solution)/shard_map/pallas_call | solution.py:457
  2.3 3.9 %collective-permute-start = (f32[16,3072]{1,0:T(8,128)}, f32[16,3072]{1,0:T(8,128)S(1)}, u32[]{:S(2)}, u32[]{:S(2)}) collective-permute-start(f32[16,3072]{1,0:T(8,128)} %get-tuple-element.21), channel_id=1, source_target_pairs={{0,8},{8,16},{16,24},{1,9},{9,17},{17,25},{2,10},{10,18},{18,26},{... | collective-permute-start | bytes 589832 | tf_op jit(solution)/shard_map/ppermute | solution.py:447
  6.3 1.3 collective-permute-start.1
  7.6 7.7 %all-to-all-start = ((f32[32,8,128]{2,1,0:T(8,128)}), f32[32,8,128]{2,1,0:T(8,128)S(1)}, u32[]{:S(2)}, u32[]{:S(2)}) async-start(f32[32,8,128]{2,1,0:T(8,128)} %get-tuple-element.20), calls=%async_computation | async-start | bytes 262144 | tf_op jit(solution)/shard_map/all_to_all | solution.py:462
  15.3 0.0 collective-permute-done.before
  15.3 0.0 copy-start.3
  15.3 0.9 collective-permute-done.1.after
  16.2 0.0 copy-done.3
  16.2 0.0 copy-start.4
  16.2 0.7 copy-done.4
  16.9 3.4 %shard_map.56 = (f32[424,128]{1,0:T(8,128)}, f32[424,128]{1,0:T(8,128)}) custom-call(f32[3,32,3072]{2,1,0:T(8,128)} %state.5, f32[16,3072]{1,0:T(8,128)} %copy-done.3, f32[16,3072]{1,0:T(8,128)} %copy-done.4), custom_call_target="tpu_custom_call" | custom-call | bytes 1048576 | tf_op jit(solution)/shard_map/pallas_call | solution.py:466
  20.2 4.6 %collective-permute-start.2 = (f32[424,128]{1,0:T(8,128)}, f32[424,128]{1,0:T(8,128)S(1)}, u32[]{:S(2)}, u32[]{:S(2)}) collective-permute-start(f32[424,128]{1,0:T(8,128)} %get-tuple-element.23), channel_id=1, source_target_pairs={{0,1},{1,2},{2,3},{3,4},{4,5},{5,6},{6,7},{8,9},{9,10},{10,11},{11... | collective-permute-start | bytes 651272 | tf_op jit(solution)/shard_map/ppermute | solution.py:447
  24.9 1.9 %collective-permute-start.3 = (f32[424,128]{1,0:T(8,128)}, f32[424,128]{1,0:T(8,128)S(1)}, u32[]{:S(2)}, u32[]{:S(2)}) collective-permute-start(f32[424,128]{1,0:T(8,128)} %get-tuple-element.24), channel_id=1, source_target_pairs={{1,0},{2,1},{3,2},{4,3},{5,4},{6,5},{7,6},{9,8},{10,9},{11,10},{12... | collective-permute-start | bytes 651272 | tf_op jit(solution)/shard_map/ppermute | solution.py:447
  26.8 0.0 all-to-all-done.slots
  26.8 0.0 copy-start
  26.8 1.2 collective-permute-done.2.below
  28.0 0.0 copy-start.7
  28.0 4.3 %collective-permute-done.3.above = f32[424,128]{1,0:T(8,128)S(1)} collective-permute-done((f32[424,128]{1,0:T(8,128)}, f32[424,128]{1,0:T(8,128)S(1)}, u32[]{:S(2)}, u32[]{:S(2)}) %collective-permute-start.3) | collective-permute-done | bytes 217120 | tf_op jit(solution)/shard_map/ppermute | solution.py:447
  32.3 0.0 copy-done
  32.3 0.0 copy-done.7
  32.3 0.0 copy-start.8
  32.3 0.7 copy-done.8
  33.0 35.0 %shard_map.57 = (f32[3,32,128]{2,1,0:T(8,128)}, f32[32,8,128]{2,1,0:T(8,128)}, f32[3,42,48,128]{3,2,1,0:T(8,128)}, f32[3,42,48,128]{3,2,1,0:T(8,128)}, f32[3,42,48,128]{3,2,1,0:T(8,128)}) custom-call(f32[3,32,3072]{2,1,0:T(8,128)} %state.5, f32[16,3072]{1,0:T(8,128)} %copy-done.3, f32[16,3072]{1,0:T(8,128)} %copy-done.4, f32[424,128]{1,0:T(8,128)} %copy-done.7, ...), custom_call_target="tpu_custom_call" | custom-call | bytes 1048576 | tf_op jit(solution)/shard_map/pallas_call | solution.py:471
  68.0 12.1 %all_to_all.10.sums = f32[32,8,128]{2,1,0:T(8,128)} all-to-all(f32[32,8,128]{2,1,0:T(8,128)} %get-tuple-element.26), channel_id=1, replica_groups=mesh['gx'=4,'gy'=8] {'gx','gy'}, dimensions={0} | all-to-all | bytes 262144 | tf_op jit(solution)/shard_map/all_to_all | solution.py:476
  80.1 21.6 %shard_map.58 = (f32[9,32,32,128]{3,2,1,0:T(8,128)}, f32[18,24,128]{2,1,0:T(8,128)}, f32[18,24,128]{2,1,0:T(8,128)}) custom-call(f32[32,8,128]{2,1,0:T(8,128)} %copy-done, f32[3,32,128]{2,1,0:T(8,128)} %get-tuple-element.25.seen, f32[32,8,128]{2,1,0:T(8,128)} %all_to_all.10.sums), custom_call_target="tpu_custom_call" | custom-call | bytes 1048576 | tf_op jit(solution)/shard_map/pallas_call | solution.py:478
  101.7 1.6 %collective-permute-start.4 = (f32[18,24,128]{2,1,0:T(8,128)}, f32[18,24,128]{2,1,0:T(8,128)S(1)}, u32[]{:S(2)}, u32[]{:S(2)}) collective-permute-start(f32[18,24,128]{2,1,0:T(8,128)} %get-tuple-element.28), channel_id=1, source_target_pairs={{0,8},{8,16},{16,24},{1,9},{9,17},{17,25},{2,10},{10,18},{18,26},{... | collective-permute-start | bytes 663560 | tf_op jit(solution)/shard_map/ppermute | solution.py:447
  103.3 1.3 collective-permute-start.5
  104.6 2.6 %collective-permute-done.4.before = f32[18,24,128]{2,1,0:T(8,128)S(1)} collective-permute-done((f32[18,24,128]{2,1,0:T(8,128)}, f32[18,24,128]{2,1,0:T(8,128)S(1)}, u32[]{:S(2)}, u32[]{:S(2)}) %collective-permute-start.4) | collective-permute-done | bytes 221216 | tf_op jit(solution)/shard_map/ppermute | solution.py:447
  107.2 0.0 copy-start.1
  107.2 7.8 %collective-permute-done.5.after = f32[18,24,128]{2,1,0:T(8,128)S(1)} collective-permute-done((f32[18,24,128]{2,1,0:T(8,128)}, f32[18,24,128]{2,1,0:T(8,128)S(1)}, u32[]{:S(2)}, u32[]{:S(2)}) %collective-permute-start.5) | collective-permute-done | bytes 221216 | tf_op jit(solution)/shard_map/ppermute | solution.py:447
  115.0 0.0 copy-start.2
  115.0 0.0 copy-done.1
  115.0 0.7 copy-done.2
  115.7 3.4 %shard_map.59 = (f32[456,128]{1,0:T(8,128)}, f32[456,128]{1,0:T(8,128)}) custom-call(f32[9,32,32,128]{3,2,1,0:T(8,128)} %get-tuple-element.27.force, f32[18,24,128]{2,1,0:T(8,128)} %copy-done.1, f32[18,24,128]{2,1,0:T(8,128)} %copy-done.2), custom_call_target="tpu_custom_call" | custom-call | bytes 1048576 | tf_op jit(solution)/shard_map/pallas_call | solution.py:486
  119.1 3.4 %collective-permute-start.6 = (f32[456,128]{1,0:T(8,128)}, f32[456,128]{1,0:T(8,128)S(1)}, u32[]{:S(2)}, u32[]{:S(2)}) collective-permute-start(f32[456,128]{1,0:T(8,128)} %get-tuple-element.30), channel_id=1, source_target_pairs={{0,1},{1,2},{2,3},{3,4},{4,5},{5,6},{6,7},{8,9},{9,10},{10,11},{11... | collective-permute-start | bytes 700424 | tf_op jit(solution)/shard_map/ppermute | solution.py:447
  122.5 1.9 %collective-permute-start.7 = (f32[456,128]{1,0:T(8,128)}, f32[456,128]{1,0:T(8,128)S(1)}, u32[]{:S(2)}, u32[]{:S(2)}) collective-permute-start(f32[456,128]{1,0:T(8,128)} %get-tuple-element.31), channel_id=1, source_target_pairs={{1,0},{2,1},{3,2},{4,3},{5,4},{6,5},{7,6},{9,8},{10,9},{11,10},{12... | collective-permute-start | bytes 700424 | tf_op jit(solution)/shard_map/ppermute | solution.py:447
  124.4 1.4 collective-permute-done.6.below
  125.8 0.0 copy-start.5
  125.8 4.3 %collective-permute-done.7.above = f32[456,128]{1,0:T(8,128)S(1)} collective-permute-done((f32[456,128]{1,0:T(8,128)}, f32[456,128]{1,0:T(8,128)S(1)}, u32[]{:S(2)}, u32[]{:S(2)}) %collective-permute-start.7) | collective-permute-done | bytes 233504 | tf_op jit(solution)/shard_map/ppermute | solution.py:447
  130.1 0.0 copy-start.6
  130.1 0.0 copy-done.5
  130.1 0.7 copy-done.6
  130.8 22.8 %shard_map.60 = f32[3,32,3072]{2,1,0:T(8,128)} custom-call(f32[9,32,32,128]{3,2,1,0:T(8,128)} %get-tuple-element.27.force, f32[18,24,128]{2,1,0:T(8,128)} %copy-done.1, f32[18,24,128]{2,1,0:T(8,128)} %copy-done.2, f32[456,128]{1,0:T(8,128)} %copy-done.5, f32[456,128]{1,0:T(8,128)} %copy-done.6, f32[3,42,48,128]{3,2,1,0:T(8,128)} %get-tuple-element.32.s0, ...), custom_call_target="tpu_custom_call" | custom-call | bytes 1048576 | tf_op jit(solution)/shard_map/pallas_call | solution.py:490
Async XLA Ops:
  2.3 13.0 %collective-permute-start = (f32[16,3072]{1,0:T(8,128)}, f32[16,3072]{1,0:T(8,128)S(1)}, u32[]{:S(2)}, u32[]{:S(2)}) collective-permute-start(f32[16,3072]{1,0:T(8,128)} %get-tuple-element.21), channel_id=1, source_target_pairs={{0,8},{8,16},{16,24},{1,9},{9,17},{17,25},{2,10},{10,18},{18,26},{... | collective-permute-start | bytes 589832 | tf_op jit(solution)/shard_map/ppermute | solution.py:447
  6.3 9.9 %collective-permute-start.1 = (f32[16,3072]{1,0:T(8,128)}, f32[16,3072]{1,0:T(8,128)S(1)}, u32[]{:S(2)}, u32[]{:S(2)}) collective-permute-start(f32[16,3072]{1,0:T(8,128)} %get-tuple-element.22), channel_id=1, source_target_pairs={{8,0},{16,8},{24,16},{9,1},{17,9},{25,17},{10,2},{18,10},{26,18},{... | collective-permute-start | bytes 589832 | tf_op jit(solution)/shard_map/ppermute | solution.py:447
  7.6 19.2 %all-to-all-start = ((f32[32,8,128]{2,1,0:T(8,128)}), f32[32,8,128]{2,1,0:T(8,128)S(1)}, u32[]{:S(2)}, u32[]{:S(2)}) async-start(f32[32,8,128]{2,1,0:T(8,128)} %get-tuple-element.20), calls=%async_computation | async-start | bytes 262144 | tf_op jit(solution)/shard_map/all_to_all | solution.py:462
  15.3 0.9 copy-start.3
  16.2 0.7 copy-start.4
  20.2 7.8 %collective-permute-start.2 = (f32[424,128]{1,0:T(8,128)}, f32[424,128]{1,0:T(8,128)S(1)}, u32[]{:S(2)}, u32[]{:S(2)}) collective-permute-start(f32[424,128]{1,0:T(8,128)} %get-tuple-element.23), channel_id=1, source_target_pairs={{0,1},{1,2},{2,3},{3,4},{4,5},{5,6},{6,7},{8,9},{9,10},{10,11},{11... | collective-permute-start | bytes 651272 | tf_op jit(solution)/shard_map/ppermute | solution.py:447
  24.9 7.4 %collective-permute-start.3 = (f32[424,128]{1,0:T(8,128)}, f32[424,128]{1,0:T(8,128)S(1)}, u32[]{:S(2)}, u32[]{:S(2)}) collective-permute-start(f32[424,128]{1,0:T(8,128)} %get-tuple-element.24), channel_id=1, source_target_pairs={{1,0},{2,1},{3,2},{4,3},{5,4},{6,5},{7,6},{9,8},{10,9},{11,10},{12... | collective-permute-start | bytes 651272 | tf_op jit(solution)/shard_map/ppermute | solution.py:447
  26.8 5.5 %copy-start = (f32[32,8,128]{2,1,0:T(8,128)}, f32[32,8,128]{2,1,0:T(8,128)S(1)}, u32[]{:S(2)}) copy-start(f32[32,8,128]{2,1,0:T(8,128)S(1)} %all-to-all-done.slots) | copy-start | bytes 393220
  28.0 4.3 %copy-start.7 = (f32[424,128]{1,0:T(8,128)}, f32[424,128]{1,0:T(8,128)S(1)}, u32[]{:S(2)}) copy-start(f32[424,128]{1,0:T(8,128)S(1)} %collective-permute-done.2.below) | copy-start | bytes 651268
  32.3 0.7 copy-start.8
  101.7 5.5 %collective-permute-start.4 = (f32[18,24,128]{2,1,0:T(8,128)}, f32[18,24,128]{2,1,0:T(8,128)S(1)}, u32[]{:S(2)}, u32[]{:S(2)}) collective-permute-start(f32[18,24,128]{2,1,0:T(8,128)} %get-tuple-element.28), channel_id=1, source_target_pairs={{0,8},{8,16},{16,24},{1,9},{9,17},{17,25},{2,10},{10,18},{18,26},{... | collective-permute-start | bytes 663560 | tf_op jit(solution)/shard_map/ppermute | solution.py:447
  103.3 11.7 %collective-permute-start.5 = (f32[18,24,128]{2,1,0:T(8,128)}, f32[18,24,128]{2,1,0:T(8,128)S(1)}, u32[]{:S(2)}, u32[]{:S(2)}) collective-permute-start(f32[18,24,128]{2,1,0:T(8,128)} %get-tuple-element.29), channel_id=1, source_target_pairs={{8,0},{16,8},{24,16},{9,1},{17,9},{25,17},{10,2},{18,10},{26,18},{... | collective-permute-start | bytes 663560 | tf_op jit(solution)/shard_map/ppermute | solution.py:447
  107.2 7.8 %copy-start.1 = (f32[18,24,128]{2,1,0:T(8,128)}, f32[18,24,128]{2,1,0:T(8,128)S(1)}, u32[]{:S(2)}) copy-start(f32[18,24,128]{2,1,0:T(8,128)S(1)} %collective-permute-done.4.before) | copy-start | bytes 663556
  115.0 0.7 copy-start.2
  119.1 6.7 %collective-permute-start.6 = (f32[456,128]{1,0:T(8,128)}, f32[456,128]{1,0:T(8,128)S(1)}, u32[]{:S(2)}, u32[]{:S(2)}) collective-permute-start(f32[456,128]{1,0:T(8,128)} %get-tuple-element.30), channel_id=1, source_target_pairs={{0,1},{1,2},{2,3},{3,4},{4,5},{5,6},{6,7},{8,9},{9,10},{10,11},{11... | collective-permute-start | bytes 700424 | tf_op jit(solution)/shard_map/ppermute | solution.py:447
  122.5 7.6 %collective-permute-start.7 = (f32[456,128]{1,0:T(8,128)}, f32[456,128]{1,0:T(8,128)S(1)}, u32[]{:S(2)}, u32[]{:S(2)}) collective-permute-start(f32[456,128]{1,0:T(8,128)} %get-tuple-element.31), channel_id=1, source_target_pairs={{1,0},{2,1},{3,2},{4,3},{5,4},{6,5},{7,6},{9,8},{10,9},{11,10},{12... | collective-permute-start | bytes 700424 | tf_op jit(solution)/shard_map/ppermute | solution.py:447
  125.8 4.3 %copy-start.5 = (f32[456,128]{1,0:T(8,128)}, f32[456,128]{1,0:T(8,128)S(1)}, u32[]{:S(2)}) copy-start(f32[456,128]{1,0:T(8,128)S(1)} %collective-permute-done.6.below) | copy-start | bytes 700420
  130.1 0.7 copy-start.6
where the time goes:
time: 154 us
  Pallas kernels  88.5 us (57%)
  starting transfers between devices  27.7 us (18%)
  waiting for transfers between devices  22.4 us (15%)
  blocking collectives  12.1 us (8%)
  local copies, waits for them, and re-layouts  2.77 us (2%)
    pallas_call x1, Pallas kernels, local(): call(functools.partial(forward_kernel, beams, per_row), (shape(STEPS, row...  35 us
    pallas_call x1, Pallas kernels, local(): call(backward_kernel, shape(*initial_state.shape), [padded] * 4)  22.8 us
    ppermute x8, waiting for transfers between devices, shift(): lax.ppermute(values, axis, [(i, i + by) for i in range(count) if 0 <= i +...  22.4 us
    pallas_call x1, Pallas kernels, local(): call(functools.partial(force_kernel, beams, per_row), (shape(FIELDS, CY,...  21.6 us
    ppermute x8, starting transfers between devices, shift(): lax.ppermute(values, axis, [(i, i + by) for i in range(count) if 0 <= i +...  20 us
    all_to_all x1, blocking collectives, local(): sums = lax.all_to_all(sums, AXES, split_axis=0, concat_axis=0, tiled=True)  12.1 us
    all_to_all x1, starting transfers between devices, local(): slots = lax.all_to_all(slots, AXES, split_axis=0, concat_axis=0, tiled=True)  7.7 us
    pallas_call x1, Pallas kernels, local(): call(force_rim_kernel, (piece, piece))(force, before, after)  3.43 us
  transfers between devices with their start and end apart: 9, of which 7 were waited for; matrix products, arithmetic and copies ran while one was open for 0% of the time, Pallas kernels for 2%

commit v1 on v0

--- a/solution.py
+++ b/solution.py
@@ -26,16 +26,23 @@
 F32 = jnp.float32
 BF16 = jnp.bfloat16
 AXES = ("gx", "gy")
-VMEM_LIMIT = 60 * 1024 * 1024
-
-
-def call(kernel, outs, scratch=(), flops=0):
+MIB = 1024 * 1024
+
+
+def call(kernel, outs, scratch=(), limit=12, far_in=(), ins=0, far_out=()):
+    def specs(count, far):
+        spaces = [pl.ANY if i in far else pltpu.VMEM for i in range(count)]
+        return [pl.BlockSpec(memory_space=space) for space in spaces]
+
+    single = not isinstance(outs, tuple)
+    out_specs = specs(1 if single else len(outs), far_out)
     return pl.pallas_call(
         kernel,
         out_shape=outs,
+        in_specs=specs(ins, far_in),
+        out_specs=out_specs[0] if single else tuple(out_specs),
         scratch_shapes=list(scratch),
-        compiler_params=pltpu.CompilerParams(vmem_limit_bytes=VMEM_LIMIT),
-        cost_estimate=pl.CostEstimate(flops=flops, bytes_accessed=1 << 20, transcendentals=0),
+        compiler_params=pltpu.CompilerParams(vmem_limit_bytes=limit * MIB),
     )
 
 
@@ -156,14 +163,6 @@
     return jnp.where(outside, 0.0, 1.0).astype(F32)
 
 
-def next_row(v):
-    return pltpu.roll(v, v.shape[0] - 1, axis=0)
-
-
-def last_row(v):
-    return pltpu.roll(v, 1, axis=0)
-
-
 def next_level(v):
     return pltpu.roll(v, LANES - 1, axis=1)
 
@@ -172,23 +171,32 @@
     return pltpu.roll(v, 1, axis=1)
 
 
-def step_forward(src, dst, low, high, mask, places):
+def step_forward(src, dst, low, high, first_row, chunks, mask, places):
     def layer(i, carry):
         y = i + low
-        centre = [src[c, y + RIM] for c in range(3)]
-        plus = [0.1 - 0.1 * v for v in centre]
-        minus = [0.1 + 0.1 * v for v in centre]
-        keep = mask * layer_mask(y, places[2], places[3])
-        for c in range(3):
-            v = centre[c]
-            total = 0.4 * v
-            total = total + plus[0] * next_row(v) + minus[0] * last_row(v)
-            total = total + plus[1] * src[c, y + RIM + 1] + minus[1] * src[c, y + RIM - 1]
-            total = total + plus[2] * next_level(v) + minus[2] * last_level(v)
-            dst[c, y + RIM] = total * keep
+        keep = layer_mask(y, places[2], places[3])
+        done = []
+        for t in range(chunks):
+            r = first_row + 8 * t
+            here, ahead, behind = pl.ds(r, 8), pl.ds(r + 1, 8), pl.ds(r - 1, 8)
+            centre = [src[c, y + RIM, here, :] for c in range(3)]
+            scaled = [0.1 * v for v in centre]
+            plus = [0.1 - v for v in scaled]
+            minus = [0.1 + v for v in scaled]
+            inside = mask[here, :] * keep
+            for c in range(3):
+                v = centre[c]
+                total = 0.4 * v + (plus[2] * next_level(v) + minus[2] * last_level(v))
+                total = total + (plus[0] * src[c, y + RIM, ahead, :] + minus[0] * src[c, y + RIM, behind, :])
+                total = total + (
+                    plus[1] * src[c, y + RIM + 1, here, :] + minus[1] * src[c, y + RIM - 1, here, :]
+                )
+                done.append((c, here, total * inside))
+        for c, here, total in done:
+            dst[c, y + RIM, here, :] = total
         return carry
 
-    lax.fori_loop(0, high - low, layer, 0)
+    lax.fori_loop(0, high - low, layer, 0, unroll=True)
 
 
 def mesh_places():
@@ -227,10 +235,10 @@
 
 
 def forward_kernel(
-    beams, per_row, state, before, after, below, above, slots, seen, sums, s0, s1, s2, s3, table
+    beams, per_row, state, before, after, below, above, slots, seen, sums, kept0, kept1, kept2, s0, s1, s2, s3, table, mask, sem
 ):
     places = mesh_places()
-    mask = row_mask(places[0], places[1])
+    mask[...] = row_mask(places[0], places[1])
     s0[...] = jnp.zeros(s0.shape, F32)
     for c in range(3):
         for y in range(CY):
@@ -249,9 +257,16 @@
             s0[c, layer_of(dist), PAD + CX : PAD + CX + side, :] = piece[
                 base + row + side : base + row + 2 * side, :
             ]
-    step_forward(s0, s1, -4, CY + 4, mask, places)
-    step_forward(s1, s2, -3, CY + 3, mask, places)
-    step_forward(s2, s3, 0, CY, mask, places)
+    keeps = [
+        pltpu.make_async_copy(field, kept, sem.at[n])
+        for n, (field, kept) in enumerate(((s0, kept0), (s1, kept1), (s2, kept2)))
+    ]
+    keeps[0].start()
+    step_forward(s0, s1, -4, CY + 4, 4, 5, mask, places)
+    keeps[1].start()
+    step_forward(s1, s2, -3, CY + 3, 4, 5, mask, places)
+    keeps[2].start()
+    step_forward(s2, s3, 0, CY, PAD, 4, mask, places)
 
     half = FIELDS * NZ
     for n, field in enumerate((s1, s2, s3)):
@@ -298,6 +313,8 @@
             one = turned[line * per_line + k : line * per_line + k + 1]
             total = total + pltpu.roll(one, rows * k, axis=1)
         sums[:, line : line + 1, :] = jnp.broadcast_to(total[None], (sums.shape[0], 1, LANES))
+    for keep in keeps:
+        keep.wait()
 
 
 def row_beam(beams, per_row, slots):
@@ -385,9 +402,17 @@
             out[base + row : base + row + 1, :] = block[y : y + 1]
 
 
-def backward_kernel(force, before, after, below, above, s0, s1, s2, out, a3, a2, a1, a0):
+def backward_kernel(
+    force, before, after, below, above, kept0, kept1, kept2, out, s0, s1, s2, a3, a2, a1, a0, mask, sem
+):
+    loads = [
+        pltpu.make_async_copy(kept, field, sem.at[n])
+        for n, (field, kept) in enumerate(((s0, kept0), (s1, kept1), (s2, kept2)))
+    ]
+    for n in (2, 1, 0):
+        loads[n].start()
     places = mesh_places()
-    mask = row_mask(places[0], places[1])
+    mask[...] = row_mask(places[0], places[1])
     adjoints = (a1, a2, a3)
     for n in range(STEPS):
         adjoints[n][...] = jnp.zeros(adjoints[n].shape, F32)
@@ -404,39 +429,57 @@
             x = (PAD - k, PAD + CX - 1 + k)[side]
             adjoints[n][c, layer_of(dist), x : x + 1, :] = piece[base + row : base + row + 1, :]
 
-    def pull(field, source, target, low, high, add):
+    def pull(field, source, target, low, high, first_row, chunks, add):
         def layer(i, carry):
             y = i + low
-            v = [field[c, y + RIM] for c in range(3)]
-            v_next = [field[c, y + RIM + 1] for c in range(3)]
-            v_last = [field[c, y + RIM - 1] for c in range(3)]
-            a = [source[c, y + FRIM] for c in range(3)]
-            slopes = [
-                [next_row(f) - last_row(f) for f in v],
-                [n - p for n, p in zip(v_next, v_last)],
-                [next_level(f) - last_level(f) for f in v],
-            ]
-            keep = mask * layer_mask(y, places[2], places[3])
-            from_next = [0.1 + 0.1 * f for f in v]
-            from_last = [0.1 - 0.1 * f for f in v]
-            y_next = 0.1 + 0.1 * v_next[1]
-            y_last = 0.1 - 0.1 * v_last[1]
-            for c in range(3):
-                bend = slopes[c][0] * a[0] + slopes[c][1] * a[1] + slopes[c][2] * a[2]
-                total = 0.4 * a[c] - 0.1 * bend
-                total = total + next_row(from_next[0] * a[c]) + last_row(from_last[0] * a[c])
-                total = total + y_next * source[c, y + FRIM + 1] + y_last * source[c, y + FRIM - 1]
-                total = total + next_level(from_next[2] * a[c]) + last_level(from_last[2] * a[c])
-                if add:
-                    total = total + target[c, y + FRIM]
-                target[c, y + FRIM] = total * keep
+            keep = layer_mask(y, places[2], places[3])
+            done = []
+            for t in range(chunks):
+                r = first_row + 8 * t
+                here, ahead, behind = pl.ds(r, 8), pl.ds(r + 1, 8), pl.ds(r - 1, 8)
+                v = [field[c, y + RIM, here, :] for c in range(3)]
+                v_ahead = [field[c, y + RIM, ahead, :] for c in range(3)]
+                v_behind = [field[c, y + RIM, behind, :] for c in range(3)]
+                v_next = [field[c, y + RIM + 1, here, :] for c in range(3)]
+                v_last = [field[c, y + RIM - 1, here, :] for c in range(3)]
+                a = [source[c, y + FRIM, here, :] for c in range(3)]
+                scaled = [0.1 * f for f in a]
+                bends = [None] * 3
+                for d, (up, down) in enumerate(((v_ahead, v_behind), (v_next, v_last), (None, None))):
+                    for c in range(3):
+                        u, w = (up[c], down[c]) if d < 2 else (next_level(v[c]), last_level(v[c]))
+                        part = (u - w) * scaled[c]
+                        bends[d] = part if bends[d] is None else bends[d] + part
+                x_ahead = 0.1 + 0.1 * v_ahead[0]
+                x_behind = 0.1 - 0.1 * v_behind[0]
+                y_next = 0.1 + 0.1 * v_next[1]
+                y_last = 0.1 - 0.1 * v_last[1]
+                inside = mask[here, :] * keep
+                for c in range(3):
+                    total = 0.4 * a[c] - bends[c]
+                    total = total + (
+                        x_ahead * source[c, y + FRIM, ahead, :] + x_behind * source[c, y + FRIM, behind, :]
+                    )
+                    total = total + (
+                        y_next * source[c, y + FRIM + 1, here, :] + y_last * source[c, y + FRIM - 1, here, :]
+                    )
+                    product = v[2] * scaled[c]
+                    total = total + (next_level(scaled[c] + product) + last_level(scaled[c] - product))
+                    if add:
+                        total = total + target[c, y + FRIM, here, :]
+                    done.append((c, here, total * inside))
+            for c, here, total in done:
+                target[c, y + FRIM, here, :] = total
             return carry
 
-        lax.fori_loop(0, high - low, layer, 0)
-
-    pull(s2, a3, a2, -2, CY + 2, True)
-    pull(s1, a2, a1, -1, CY + 1, True)
-    pull(s0, a1, a0, 0, CY, False)
+        lax.fori_loop(0, high - low, layer, 0, unroll=True)
+
+    loads[2].wait()
+    pull(s2, a3, a2, -2, CY + 2, 4, 5, True)
+    loads[1].wait()
+    pull(s1, a2, a1, -1, CY + 1, 4, 5, True)
+    loads[0].wait()
+    pull(s0, a1, a0, 0, CY, PAD, 4, False)
     for c in range(3):
         for y in range(CY):
             out[c, :, NZ * y : NZ * y + NZ] = a0[c, FRIM + y, PAD : PAD + CX, 0:NZ]
@@ -455,7 +498,7 @@
     rows = peers // group
     rim_rows_shape = shape(16, CY * NZ)
     slots, first_rows, last_rows = call(
-        prepare_kernel, (shape(peers, 8, capacity), rim_rows_shape, rim_rows_shape)
+        prepare_kernel, (shape(peers, 8, capacity), rim_rows_shape, rim_rows_shape), limit=60, ins=5
     )(initial_state, beam_dir, gate_obs, slot_beam, slot_cell)
     after = shift(first_rows, "gx", -1)
     before = shift(last_rows, "gx", 1)
@@ -463,15 +506,20 @@
     if group > 1:
         slots = slots.reshape(rows, group, 8, capacity).transpose(0, 2, 1, 3).reshape(rows, 8, LANES)
     piece = shape(STATE_PIECE, LANES)
-    first_layers, last_layers = call(state_rim_kernel, (piece, piece))(initial_state, before, after)
+    first_layers, last_layers = call(state_rim_kernel, (piece, piece), ins=3)(initial_state, before, after)
     above = shift(first_layers, "gy", -1)
     below = shift(last_layers, "gy", 1)
     lines = -(-STEPS * per_row * rows // LANES // 8) * 8
     field = shape(3, YH, XH, LANES)
+    mask = pltpu.VMEM((XH, LANES), F32)
     seen, sums, s0, s1, s2 = call(
         functools.partial(forward_kernel, beams, per_row),
         (shape(STEPS, rows, LANES), shape(peers, lines, LANES), field, field, field),
-        [pltpu.VMEM(field.shape, F32), pltpu.VMEM((2 * FIELDS * NZ, COLUMNS), BF16)],
+        [pltpu.VMEM(field.shape, F32)] * 4
+        + [pltpu.VMEM((2 * FIELDS * NZ, COLUMNS), BF16), mask, pltpu.SemaphoreType.DMA((3,))],
+        limit=40,
+        ins=6,
+        far_out=(2, 3, 4),
     )(initial_state, before, after, below, above, slots)
     sums = lax.all_to_all(sums, AXES, split_axis=0, concat_axis=0, tiled=True)
     rim = shape(len(FORCE_BLOCKS), PACKED, LANES)
@@ -479,15 +527,24 @@
         functools.partial(force_kernel, beams, per_row),
         (shape(FIELDS, CY, CX, LANES), rim, rim),
         [pltpu.VMEM((FIELDS, LANES, COLUMNS), F32), pltpu.VMEM((FIELDS, rows, LANES), F32)],
+        limit=40,
+        ins=3,
     )(slots, seen, sums)
     after = shift(first_rows, "gx", -1)
     before = shift(last_rows, "gx", 1)
     piece = shape(FORCE_PIECE, LANES)
-    first_layers, last_layers = call(force_rim_kernel, (piece, piece))(force, before, after)
+    first_layers, last_layers = call(force_rim_kernel, (piece, piece), ins=3)(force, before, after)
     above = shift(first_layers, "gy", -1)
     below = shift(last_layers, "gy", 1)
     padded = pltpu.VMEM((3, FH, XH, LANES), F32)
-    return call(backward_kernel, shape(*initial_state.shape), [padded] * 4)(
+    return call(
+        backward_kernel,
+        shape(*initial_state.shape),
+        [pltpu.VMEM(field.shape, F32)] * 3 + [padded] * 4 + [mask, pltpu.SemaphoreType.DMA((3,))],
+        limit=40,
+        ins=8,
+        far_in=(5, 6, 7),
+    )(
         force, before, after, below, above, s0, s1, s2
     )
 

time: 154 us -> 123 us (0.80)
  Pallas kernels: 88.5 us -> 59.6 us
    pallas_call x3, Pallas kernels: 29.6 us -> 13.9 us  [the longest x1 12.4 us: local(): call(backward_kernel, shape(*initial_state.shape), [pltpu.VMEM(field.shap...]
    pallas_call x1, Pallas kernels: 35 us -> 24.7 us  [local(): call(functools.partial(forward_kernel, beams, per_row), (shape(STEPS, row...]
    pallas_call x1, Pallas kernels: 21.6 us -> 18.6 us  [local(): call(functools.partial(force_kernel, beams, per_row), (shape(FIELDS, CY,...]
  transfers between devices with their start and end apart: 9 -> 9, of which waited for: 7 -> 7; matrix products, arithmetic and copies ran while one was open for 0% -> 0% of each run, Pallas kernels for 2% -> 1%
where the time goes in v1:
time: 123 us; the launch traced here: 122 us
  Pallas kernels  59.6 us (48%)
  starting transfers between devices  27.7 us (23%)
  waiting for transfers between devices  21.8 us (18%)
  blocking collectives  11.8 us (10%)
  local copies, waits for them, and re-layouts  1.28 us (1%)
    pallas_call x1, Pallas kernels, local(): call(functools.partial(forward_kernel, beams, per_row), (shape(STEPS, row...  24.7 us
    ppermute x8, waiting for transfers between devices, shift(): lax.ppermute(values, axis, [(i, i + by) for i in range(count) if 0 <= i +...  21.8 us
    ppermute x8, starting transfers between devices, shift(): lax.ppermute(values, axis, [(i, i + by) for i in range(count) if 0 <= i +...  20 us
    pallas_call x1, Pallas kernels, local(): call(functools.partial(force_kernel, beams, per_row), (shape(FIELDS, CY,...  18.6 us
    pallas_call x1, Pallas kernels, local(): call(backward_kernel, shape(*initial_state.shape), [pltpu.VMEM(field.shap...  12.4 us
    all_to_all x1, blocking collectives, local(): sums = lax.all_to_all(sums, AXES, split_axis=0, concat_axis=0, tiled=True)  11.8 us
    all_to_all x1, starting transfers between devices, local(): slots = lax.all_to_all(slots, AXES, split_axis=0, concat_axis=0, tiled=True)  7.7 us
  transfers between devices with their start and end apart: 9, of which 7 were waited for; matrix products, arithmetic and copies ran while one was open for 0% of the time, Pallas kernels for 1%

profile of v1, /device:TPU:1, one launch (start us, length us, event | category | flops | bytes accessed | tf_op | source)
XLA Modules:
  0.0 122.5 jit_solution(6944194071320336304)
XLA Ops:
  0.0 0.0 copy-start.2
  0.0 2.4 %shard_map.55 = (f32[32,8,128]{2,1,0:T(8,128)}, f32[16,3072]{1,0:T(8,128)}, f32[16,3072]{1,0:T(8,128)}) custom-call(f32[3,32,3072]{2,1,0:T(8,128)} %state.5, f32[3,4]{1,0:T(4,128)} %beam_dir.1, f32[3,1,32,128]{3,2,1,0:T(8,128)} %obs.1, s32[1,32,128]{2,1,0:T(8,128)} %beam.1, s32[1,32,128]{2,1,0:T(8,128)} %cell.1), custom_call_target="tpu_custom_call" | custom-call | tf_op jit(solution)/shard_map/pallas_call | solution.py:500
  2.4 3.9 %collective-permute-start = (f32[16,3072]{1,0:T(8,128)}, f32[16,3072]{1,0:T(8,128)S(1)}, u32[]{:S(2)}, u32[]{:S(2)}) collective-permute-start(f32[16,3072]{1,0:T(8,128)} %get-tuple-element.21), channel_id=1, source_target_pairs={{0,8},{8,16},{16,24},{1,9},{9,17},{17,25},{2,10},{10,18},{18,26},{... | collective-permute-start | bytes 589832 | tf_op jit(solution)/shard_map/ppermute | solution.py:490
  6.4 1.3 %collective-permute-start.1 = (f32[16,3072]{1,0:T(8,128)}, f32[16,3072]{1,0:T(8,128)S(1)}, u32[]{:S(2)}, u32[]{:S(2)}) collective-permute-start(f32[16,3072]{1,0:T(8,128)} %get-tuple-element.22), channel_id=1, source_target_pairs={{8,0},{16,8},{24,16},{9,1},{17,9},{25,17},{10,2},{18,10},{26,18},{... | collective-permute-start | bytes 589832 | tf_op jit(solution)/shard_map/ppermute | solution.py:490
  7.7 7.7 %all-to-all-start = ((f32[32,8,128]{2,1,0:T(8,128)}), f32[32,8,128]{2,1,0:T(8,128)S(1)}, u32[]{:S(2)}, u32[]{:S(2)}) async-start(f32[32,8,128]{2,1,0:T(8,128)} %get-tuple-element.20), calls=%async_computation | async-start | bytes 262144 | tf_op jit(solution)/shard_map/all_to_all | solution.py:505
  15.4 0.0 collective-permute-done.before
  15.4 0.9 collective-permute-done.1.after
  16.3 0.0 copy-start.1
  16.3 1.3 %copy-done.1 = f32[3,32,3072]{2,1,0:T(8,128)S(1)} copy-done((f32[3,32,3072]{2,1,0:T(8,128)S(1)}, f32[3,32,3072]{2,1,0:T(8,128)}, u32[]{:S(2)}) %copy-start.1) | copy-done | bytes 1179672
  17.6 1.3 %shard_map.56 = (f32[424,128]{1,0:T(8,128)S(1)}, f32[424,128]{1,0:T(8,128)S(1)}) custom-call(f32[3,32,3072]{2,1,0:T(8,128)S(1)} %copy-done.1, f32[16,3072]{1,0:T(8,128)S(1)} %collective-permute-done.before, f32[16,3072]{1,0:T(8,128)S(1)} %collective-permute-done.1.after), custom_call_target="tpu_custom_call" | custom-call | tf_op jit(solution)/shard_map/pallas_call | solution.py:509
  18.8 4.6 %collective-permute-start.2 = (f32[424,128]{1,0:T(8,128)S(1)}, f32[424,128]{1,0:T(8,128)S(1)}, u32[]{:S(2)}, u32[]{:S(2)}) collective-permute-start(f32[424,128]{1,0:T(8,128)S(1)} %get-tuple-element.23), channel_id=1, source_target_pairs={{0,1},{1,2},{2,3},{3,4},{4,5},{5,6},{6,7},{8,9},{9,10},{10,11},{11... | collective-permute-start | bytes 651272 | tf_op jit(solution)/shard_map/ppermute | solution.py:490
  23.5 1.9 %collective-permute-start.3 = (f32[424,128]{1,0:T(8,128)S(1)}, f32[424,128]{1,0:T(8,128)S(1)}, u32[]{:S(2)}, u32[]{:S(2)}) collective-permute-start(f32[424,128]{1,0:T(8,128)S(1)} %get-tuple-element.24), channel_id=1, source_target_pairs={{1,0},{2,1},{3,2},{4,3},{5,4},{6,5},{7,6},{9,8},{10,9},{11,10},{12... | collective-permute-start | bytes 651272 | tf_op jit(solution)/shard_map/ppermute | solution.py:490
  25.4 0.0 all-to-all-done.slots
  25.4 0.9 collective-permute-done.2.below
  26.3 4.4 %collective-permute-done.3.above = f32[424,128]{1,0:T(8,128)S(1)} collective-permute-done((f32[424,128]{1,0:T(8,128)S(1)}, f32[424,128]{1,0:T(8,128)S(1)}, u32[]{:S(2)}, u32[]{:S(2)}) %collective-permute-start.3) | collective-permute-done | bytes 217120 | tf_op jit(solution)/shard_map/ppermute | solution.py:490
  30.7 0.0 copy-done.2
  30.7 24.7 %shard_map.57 = (f32[3,32,128]{2,1,0:T(8,128)S(1)}, f32[32,8,128]{2,1,0:T(8,128)S(1)}, f32[3,42,48,128]{3,2,1,0:T(8,128)S(1)}, f32[3,42,48,128]{3,2,1,0:T(8,128)S(1)}, f32[3,42,48,128]{3,2,1,0:T(8,128)S(1)}) custom-call(f32[3,32,3072]{2,1,0:T(8,128)S(1)} %copy-done.2, f32[16,3072]{1,0:T(8,128)S(1)} %collective-permute-done.before, ...), custom_call_target="tpu_custom_call" | custom-call | tf_op jit(solution)/shard_map/pallas_call | solution.py:515
  55.4 11.8 %all_to_all.10.sums = f32[32,8,128]{2,1,0:T(8,128)S(1)} all-to-all(f32[32,8,128]{2,1,0:T(8,128)S(1)} %get-tuple-element.26), channel_id=1, replica_groups=mesh['gx'=4,'gy'=8] {'gx','gy'}, dimensions={0} | all-to-all | bytes 262144 | tf_op jit(solution)/shard_map/all_to_all | solution.py:524
  67.2 18.6 %shard_map.58 = (f32[9,32,32,128]{3,2,1,0:T(8,128)S(1)}, f32[18,24,128]{2,1,0:T(8,128)S(1)}, f32[18,24,128]{2,1,0:T(8,128)S(1)}) custom-call(f32[32,8,128]{2,1,0:T(8,128)S(1)} %all-to-all-done.slots, f32[3,32,128]{2,1,0:T(8,128)S(1)} %get-tuple-element.25.seen, f32[32,8,128]{2,1,0:T(8,128)S(1)} %all_to_all.10.sums), custom_call_target="tpu_custom_call" | custom-call | tf_op jit(solution)/shard_map/pallas_call | solution.py:526
  85.8 0.0 copy-start
  85.8 1.6 %collective-permute-start.4 = (f32[18,24,128]{2,1,0:T(8,128)S(1)}, f32[18,24,128]{2,1,0:T(8,128)S(1)}, u32[]{:S(2)}, u32[]{:S(2)}) collective-permute-start(f32[18,24,128]{2,1,0:T(8,128)S(1)} %get-tuple-element.28), channel_id=1, source_target_pairs={{0,8},{8,16},{16,24},{1,9},{9,17},{17,25},{2,10},{10,18},{18,26},{... | collective-permute-start | bytes 663560 | tf_op jit(solution)/shard_map/ppermute | solution.py:490
  87.3 1.3 %collective-permute-start.5 = (f32[18,24,128]{2,1,0:T(8,128)S(1)}, f32[18,24,128]{2,1,0:T(8,128)S(1)}, u32[]{:S(2)}, u32[]{:S(2)}) collective-permute-start(f32[18,24,128]{2,1,0:T(8,128)S(1)} %get-tuple-element.29), channel_id=1, source_target_pairs={{8,0},{16,8},{24,16},{9,1},{17,9},{25,17},{10,2},{18,10},{26,18},{... | collective-permute-start | bytes 663560 | tf_op jit(solution)/shard_map/ppermute | solution.py:490
  88.6 2.3 %collective-permute-done.4.before = f32[18,24,128]{2,1,0:T(8,128)S(1)} collective-permute-done((f32[18,24,128]{2,1,0:T(8,128)S(1)}, f32[18,24,128]{2,1,0:T(8,128)S(1)}, u32[]{:S(2)}, u32[]{:S(2)}) %collective-permute-start.4) | collective-permute-done | bytes 221216 | tf_op jit(solution)/shard_map/ppermute | solution.py:490
  90.9 7.9 %collective-permute-done.5.after = f32[18,24,128]{2,1,0:T(8,128)S(1)} collective-permute-done((f32[18,24,128]{2,1,0:T(8,128)S(1)}, f32[18,24,128]{2,1,0:T(8,128)S(1)}, u32[]{:S(2)}, u32[]{:S(2)}) %collective-permute-start.5) | collective-permute-done | bytes 221216 | tf_op jit(solution)/shard_map/ppermute | solution.py:490
  98.9 0.3 shard_map.59
  99.1 3.4 %collective-permute-start.6 = (f32[456,128]{1,0:T(8,128)S(1)}, f32[456,128]{1,0:T(8,128)S(1)}, u32[]{:S(2)}, u32[]{:S(2)}) collective-permute-start(f32[456,128]{1,0:T(8,128)S(1)} %get-tuple-element.30), channel_id=1, source_target_pairs={{0,1},{1,2},{2,3},{3,4},{4,5},{5,6},{6,7},{8,9},{9,10},{10,11},{11... | collective-permute-start | bytes 700424 | tf_op jit(solution)/shard_map/ppermute | solution.py:490
  102.5 1.9 %collective-permute-start.7 = (f32[456,128]{1,0:T(8,128)S(1)}, f32[456,128]{1,0:T(8,128)S(1)}, u32[]{:S(2)}, u32[]{:S(2)}) collective-permute-start(f32[456,128]{1,0:T(8,128)S(1)} %get-tuple-element.31), channel_id=1, source_target_pairs={{1,0},{2,1},{3,2},{4,3},{5,4},{6,5},{7,6},{9,8},{10,9},{11,10},{12... | collective-permute-start | bytes 700424 | tf_op jit(solution)/shard_map/ppermute | solution.py:490
  104.5 1.1 collective-permute-done.6.below
  105.5 4.4 %collective-permute-done.7.above = f32[456,128]{1,0:T(8,128)S(1)} collective-permute-done((f32[456,128]{1,0:T(8,128)S(1)}, f32[456,128]{1,0:T(8,128)S(1)}, u32[]{:S(2)}, u32[]{:S(2)}) %collective-permute-start.7) | collective-permute-done | bytes 233504 | tf_op jit(solution)/shard_map/ppermute | solution.py:490
  109.9 0.0 copy-done
  109.9 12.4 %shard_map.60 = f32[3,32,3072]{2,1,0:T(8,128)} custom-call(f32[9,32,32,128]{3,2,1,0:T(8,128)} %copy-done, f32[18,24,128]{2,1,0:T(8,128)S(1)} %collective-permute-done.4.before, f32[18,24,128]{2,1,0:T(8,128)S(1)} %collective-permute-done.5.after, f32[456,128]{1,0:T(8,128)S(1)} %collective-permute-done.6.below, f32[456,128]{1,0:T(8,128)S(1)} %collective-permute-done.7.above, ...), custom_call_target="tpu_custom_call" | custom-call | tf_op jit(solution)/shard_map/pallas_call | solution.py:540
Async XLA Ops:
  0.0 30.7 %copy-start.2 = (f32[3,32,3072]{2,1,0:T(8,128)S(1)}, f32[3,32,3072]{2,1,0:T(8,128)}, u32[]{:S(2)}) copy-start(f32[3,32,3072]{2,1,0:T(8,128)} %state.5) | copy-start | bytes 3538948
  2.4 13.0 %collective-permute-start = (f32[16,3072]{1,0:T(8,128)}, f32[16,3072]{1,0:T(8,128)S(1)}, u32[]{:S(2)}, u32[]{:S(2)}) collective-permute-start(f32[16,3072]{1,0:T(8,128)} %get-tuple-element.21), channel_id=1, source_target_pairs={{0,8},{8,16},{16,24},{1,9},{9,17},{17,25},{2,10},{10,18},{18,26},{... | collective-permute-start | bytes 589832 | tf_op jit(solution)/shard_map/ppermute | solution.py:490
  6.4 9.9 %collective-permute-start.1 = (f32[16,3072]{1,0:T(8,128)}, f32[16,3072]{1,0:T(8,128)S(1)}, u32[]{:S(2)}, u32[]{:S(2)}) collective-permute-start(f32[16,3072]{1,0:T(8,128)} %get-tuple-element.22), channel_id=1, source_target_pairs={{8,0},{16,8},{24,16},{9,1},{17,9},{25,17},{10,2},{18,10},{26,18},{... | collective-permute-start | bytes 589832 | tf_op jit(solution)/shard_map/ppermute | solution.py:490
  7.7 17.8 %all-to-all-start = ((f32[32,8,128]{2,1,0:T(8,128)}), f32[32,8,128]{2,1,0:T(8,128)S(1)}, u32[]{:S(2)}, u32[]{:S(2)}) async-start(f32[32,8,128]{2,1,0:T(8,128)} %get-tuple-element.20), calls=%async_computation | async-start | bytes 262144 | tf_op jit(solution)/shard_map/all_to_all | solution.py:505
  16.3 1.3 %copy-start.1 = (f32[3,32,3072]{2,1,0:T(8,128)S(1)}, f32[3,32,3072]{2,1,0:T(8,128)}, u32[]{:S(2)}) copy-start(f32[3,32,3072]{2,1,0:T(8,128)} %state.5) | copy-start | bytes 3538948
  18.8 7.5 %collective-permute-start.2 = (f32[424,128]{1,0:T(8,128)S(1)}, f32[424,128]{1,0:T(8,128)S(1)}, u32[]{:S(2)}, u32[]{:S(2)}) collective-permute-start(f32[424,128]{1,0:T(8,128)S(1)} %get-tuple-element.23), channel_id=1, source_target_pairs={{0,1},{1,2},{2,3},{3,4},{4,5},{5,6},{6,7},{8,9},{9,10},{10,11},{11... | collective-permute-start | bytes 651272 | tf_op jit(solution)/shard_map/ppermute | solution.py:490
  23.5 7.2 %collective-permute-start.3 = (f32[424,128]{1,0:T(8,128)S(1)}, f32[424,128]{1,0:T(8,128)S(1)}, u32[]{:S(2)}, u32[]{:S(2)}) collective-permute-start(f32[424,128]{1,0:T(8,128)S(1)} %get-tuple-element.24), channel_id=1, source_target_pairs={{1,0},{2,1},{3,2},{4,3},{5,4},{6,5},{7,6},{9,8},{10,9},{11,10},{12... | collective-permute-start | bytes 651272 | tf_op jit(solution)/shard_map/ppermute | solution.py:490
  85.8 24.2 %copy-start = (f32[9,32,32,128]{3,2,1,0:T(8,128)}, f32[9,32,32,128]{3,2,1,0:T(8,128)S(1)}, u32[]{:S(2)}) copy-start(f32[9,32,32,128]{3,2,1,0:T(8,128)S(1)} %get-tuple-element.27.force) | copy-start | bytes 14155780
  85.8 5.2 %collective-permute-start.4 = (f32[18,24,128]{2,1,0:T(8,128)S(1)}, f32[18,24,128]{2,1,0:T(8,128)S(1)}, u32[]{:S(2)}, u32[]{:S(2)}) collective-permute-start(f32[18,24,128]{2,1,0:T(8,128)S(1)} %get-tuple-element.28), channel_id=1, source_target_pairs={{0,8},{8,16},{16,24},{1,9},{9,17},{17,25},{2,10},{10,18},{18,26},{... | collective-permute-start | bytes 663560 | tf_op jit(solution)/shard_map/ppermute | solution.py:490
  87.3 11.5 %collective-permute-start.5 = (f32[18,24,128]{2,1,0:T(8,128)S(1)}, f32[18,24,128]{2,1,0:T(8,128)S(1)}, u32[]{:S(2)}, u32[]{:S(2)}) collective-permute-start(f32[18,24,128]{2,1,0:T(8,128)S(1)} %get-tuple-element.29), channel_id=1, source_target_pairs={{8,0},{16,8},{24,16},{9,1},{17,9},{25,17},{10,2},{18,10},{26,18},{... | collective-permute-start | bytes 663560 | tf_op jit(solution)/shard_map/ppermute | solution.py:490
  99.1 6.4 %collective-permute-start.6 = (f32[456,128]{1,0:T(8,128)S(1)}, f32[456,128]{1,0:T(8,128)S(1)}, u32[]{:S(2)}, u32[]{:S(2)}) collective-permute-start(f32[456,128]{1,0:T(8,128)S(1)} %get-tuple-element.30), channel_id=1, source_target_pairs={{0,1},{1,2},{2,3},{3,4},{4,5},{5,6},{6,7},{8,9},{9,10},{10,11},{11... | collective-permute-start | bytes 700424 | tf_op jit(solution)/shard_map/ppermute | solution.py:490
  102.5 7.4 %collective-permute-start.7 = (f32[456,128]{1,0:T(8,128)S(1)}, f32[456,128]{1,0:T(8,128)S(1)}, u32[]{:S(2)}, u32[]{:S(2)}) collective-permute-start(f32[456,128]{1,0:T(8,128)S(1)} %get-tuple-element.31), channel_id=1, source_target_pairs={{1,0},{2,1},{3,2},{4,3},{5,4},{6,5},{7,6},{9,8},{10,9},{11,10},{12... | collective-permute-start | bytes 700424 | tf_op jit(solution)/shard_map/ppermute | solution.py:490

commit v2 on v1

--- a/solution.py
+++ b/solution.py
@@ -22,6 +22,10 @@
 FRIM = 3
 FH = CY + 2 * FRIM
 FIELDS = 3 * STEPS
+UNROLL = 4
+ROWS = 8
+GROUPS = CX // ROWS
+GROUP = ROWS * CY
 BLOCK = 512
 F32 = jnp.float32
 BF16 = jnp.bfloat16
@@ -29,7 +33,7 @@
 MIB = 1024 * 1024
 
 
-def call(kernel, outs, scratch=(), limit=12, far_in=(), ins=0, far_out=()):
+def call(kernel, outs, scratch=(), limit=12, far_in=(), ins=0, far_out=(), micros=1):
     def specs(count, far):
         spaces = [pl.ANY if i in far else pltpu.VMEM for i in range(count)]
         return [pl.BlockSpec(memory_space=space) for space in spaces]
@@ -43,6 +47,7 @@
         out_specs=out_specs[0] if single else tuple(out_specs),
         scratch_shapes=list(scratch),
         compiler_params=pltpu.CompilerParams(vmem_limit_bytes=limit * MIB),
+        cost_estimate=pl.CostEstimate(flops=0, bytes_accessed=micros * 3_000_000, transcendentals=0),
     )
 
 
@@ -196,7 +201,7 @@
             dst[c, y + RIM, here, :] = total
         return carry
 
-    lax.fori_loop(0, high - low, layer, 0, unroll=True)
+    lax.fori_loop(0, high - low, layer, 0, unroll=UNROLL)
 
 
 def mesh_places():
@@ -213,11 +218,12 @@
     x = ((cell + 0.5) * (1.0 / (CY * NZ))).astype(jnp.int32)
     rest = cell.astype(jnp.int32) - x * (CY * NZ)
     y = ((rest.astype(F32) + 0.5) * (1.0 / NZ)).astype(jnp.int32)
-    return y * CX + x, rest - y * NZ
-
-
-def column_hits(columns):
-    place = lax.broadcasted_iota(jnp.int32, (COLUMNS, columns.shape[1]), 0)
+    high = x // ROWS
+    return high * (GROUP - ROWS) + y * ROWS + x, rest - y * NZ
+
+
+def column_hits(columns, count=COLUMNS):
+    place = lax.broadcasted_iota(jnp.int32, (count, columns.shape[1]), 0)
     return jnp.where(place == columns, 1.0, 0.0).astype(BF16)
 
 
@@ -226,7 +232,7 @@
     columns = jnp.concatenate([r[0] for r in rows], axis=1)
     level = jnp.concatenate([r[1] for r in rows], axis=1)
     here = lax.broadcasted_iota(jnp.int32, (NZ, BLOCK), 0) == level
-    return column_hits(columns), here
+    return columns, here
 
 
 def block_values(slots, block, which):
@@ -271,16 +277,18 @@
     half = FIELDS * NZ
     for n, field in enumerate((s1, s2, s3)):
         for c in range(3):
-            tile = field[c, RIM : RIM + CY, PAD : PAD + CX, :].reshape(COLUMNS, LANES)
-            turned = tile.T[0:NZ]
-            high = turned.astype(BF16)
             base = (3 * n + c) * NZ
-            table[base : base + NZ, :] = high
-            table[half + base : half + base + NZ, :] = (turned - high.astype(F32)).astype(BF16)
+            for g in range(GROUPS):
+                rows = field[c, RIM : RIM + CY, PAD + ROWS * g : PAD + ROWS * g + ROWS, :]
+                turned = rows.reshape(GROUP, LANES).T[0:NZ]
+                high = turned.astype(BF16)
+                span = slice(GROUP * g, GROUP * g + GROUP)
+                table[base : base + NZ, span] = high
+                table[half + base : half + base + NZ, span] = (turned - high.astype(F32)).astype(BF16)
 
     def gather(block, carry):
-        hits, here = block_places(slots, block)
-        found = jnp.dot(table[...], hits, preferred_element_type=F32)
+        columns, here = block_places(slots, block)
+        found = jnp.dot(table[...], column_hits(columns), preferred_element_type=F32)
         weights = [block_values(slots, block, 5 + c) for c in range(3)]
         for n in range(STEPS):
             total = jnp.zeros((1, BLOCK), F32)
@@ -326,7 +334,35 @@
     return beam
 
 
-def force_kernel(beams, per_row, slots, seen, sums, force, first_rows, last_rows, total, weight):
+def scatter_slots(groups, slots, weight, total, force):
+    total[...] = jnp.zeros(total.shape, F32)
+
+    def scatter(block, carry):
+        columns, here = block_places(slots, block)
+        hits = jnp.concatenate([column_hits(columns - GROUP * g, GROUP) for g in groups], axis=0)
+        high_rows, low_rows = [], []
+        for f in range(FIELDS):
+            value = jnp.concatenate(
+                [weight[f, pl.ds(block * (BLOCK // LANES) + r, 1), :] for r in range(BLOCK // LANES)],
+                axis=1,
+            )
+            high = value.astype(BF16).astype(F32)
+            high_rows.append(jnp.where(here, high, 0.0).astype(BF16))
+            low_rows.append(jnp.where(here, value - high, 0.0).astype(BF16))
+        table = jnp.concatenate(high_rows + low_rows, axis=0)
+        added = lax.dot_general(table, hits, (((1,), (1,)), ((), ())), preferred_element_type=F32)
+        half = FIELDS * NZ
+        for f in range(FIELDS):
+            total[f, 0:NZ, :] += added[NZ * f : NZ * f + NZ] + added[half + NZ * f : half + NZ * f + NZ]
+        return carry
+
+    lax.fori_loop(0, slots.shape[0] * LANES // BLOCK, scatter, 0)
+    for f in range(FIELDS):
+        for k in range(len(groups)):
+            force[f, k] = total[f, :, GROUP * k : GROUP * k + GROUP].T.reshape(CY, ROWS, LANES)
+
+
+def outer_force_kernel(beams, per_row, slots, seen, sums, force, weight, first_rows, last_rows, total):
     rows = slots.shape[0]
     per_line = LANES // rows
     lines = jnp.sum(sums[...], axis=0) / GATES
@@ -338,54 +374,29 @@
     spread.append(jnp.zeros((LANES - count, LANES), F32))
     means = jnp.concatenate(spread, axis=0).T[0:rows]
     beam = row_beam(beams, per_row, slots)
-    misfit = []
     for n in range(STEPS):
         mean = jnp.zeros((rows, LANES), F32)
         for k in range(per_row):
             one = means[:, n * per_row + k : n * per_row + k + 1]
             mean = jnp.where(beam == k, one, mean)
-        misfit.append(seen[n] - mean - slots[:, 2 + n, :])
-    for n in range(STEPS):
+        misfit = seen[n] - mean - slots[:, 2 + n, :]
         for c in range(3):
-            weight[3 * n + c] = slots[:, 5 + c, :] * misfit[n]
-
-    total[...] = jnp.zeros(total.shape, F32)
-
-    def scatter(block, carry):
-        hits, here = block_places(slots, block)
-        high_rows, low_rows = [], []
-        for f in range(FIELDS):
-            value = jnp.concatenate(
-                [weight[f, pl.ds(block * (BLOCK // LANES) + r, 1), :] for r in range(BLOCK // LANES)],
-                axis=1,
-            )
-            high = value.astype(BF16).astype(F32)
-            high_rows.append(jnp.where(here, high, 0.0).astype(BF16))
-            low_rows.append(jnp.where(here, value - high, 0.0).astype(BF16))
-        table = jnp.concatenate(high_rows + low_rows, axis=0)
-        added = lax.dot_general(table, hits, (((1,), (1,)), ((), ())), preferred_element_type=F32)
-        for f in range(FIELDS):
-            half = FIELDS * NZ
-            total[f, 0:NZ, :] += added[NZ * f : NZ * f + NZ] + added[half + NZ * f : half + NZ * f + NZ]
-        return carry
-
-    lax.fori_loop(0, rows * LANES // BLOCK, scatter, 0)
-    for f in range(FIELDS):
-        force[f] = total[f].T.reshape(CY, CX, LANES)
-    for out, row_of in ((first_rows, lambda i: i), (last_rows, lambda i: CX - 1 - i)):
+            weight[3 * n + c] = slots[:, 5 + c, :] * misfit
+    scatter_slots((0, GROUPS - 1), slots, weight, total, force)
+    for out, k, row_of in ((first_rows, 0, lambda i: i), (last_rows, 1, lambda i: ROWS - 1 - i)):
         for b, (n, c, i) in enumerate(FORCE_BLOCKS):
 
             def put(row, rows, b=b, out=out):
                 out[b, row : row + 8, :] = rows
 
-            pack(put, force[3 * n + c, :, row_of(i), :])
-
-
-def rim_rows(piece, which):
-    return unpack(piece[which])
-
-
-def force_rim_kernel(force, before, after, first_layers, last_layers):
+            pack(put, force[3 * n + c, k, :, row_of(i), :])
+
+
+def inner_force_kernel(slots, weight, force, total):
+    scatter_slots((1, 2), slots, weight, total, force)
+
+
+def force_rim_kernel(outer, inner, before, after, first_layers, last_layers):
     index = {key: b for b, key in enumerate(FORCE_BLOCKS)}
     for out, layer_of in ((first_layers, lambda d: d - 1), (last_layers, lambda d: CY - d)):
         for b, (n, c, i) in enumerate(FORCE_BLOCKS):
@@ -393,7 +404,8 @@
             def put(row, rows, b=b, out=out):
                 out[b * PACKED + row : b * PACKED + row + 8, :] = rows
 
-            pack(put, force[3 * n + c, layer_of(i + 1)])
+            f, y = 3 * n + c, layer_of(i + 1)
+            pack(put, jnp.concatenate([outer[f, 0, y], inner[f, 0, y], inner[f, 1, y], outer[f, 1, y]], axis=0))
         base = len(FORCE_BLOCKS) * PACKED
         for row, (n, c, dist, side, k) in enumerate(FORCE_CORNERS):
             piece = (before, after)[side]
@@ -403,7 +415,7 @@
 
 
 def backward_kernel(
-    force, before, after, below, above, kept0, kept1, kept2, out, s0, s1, s2, a3, a2, a1, a0, mask, sem
+    outer, inner, before, after, below, above, kept0, kept1, kept2, out, s0, s1, s2, a3, a2, a1, a0, mask, sem
 ):
     loads = [
         pltpu.make_async_copy(kept, field, sem.at[n])
@@ -417,7 +429,9 @@
     for n in range(STEPS):
         adjoints[n][...] = jnp.zeros(adjoints[n].shape, F32)
         for c in range(3):
-            adjoints[n][c, FRIM : FRIM + CY, PAD : PAD + CX, :] = force[3 * n + c]
+            for g, (part, k) in enumerate(((outer, 0), (inner, 0), (inner, 1), (outer, 1))):
+                row = PAD + ROWS * g
+                adjoints[n][c, FRIM : FRIM + CY, row : row + ROWS, :] = part[3 * n + c, k]
     for b, (n, c, i) in enumerate(FORCE_BLOCKS):
         adjoints[n][c, FRIM : FRIM + CY, PAD - 1 - i, :] = unpack(before[b])
         adjoints[n][c, FRIM : FRIM + CY, PAD + CX + i, :] = unpack(after[b])
@@ -472,7 +486,7 @@
                 target[c, y + FRIM, here, :] = total
             return carry
 
-        lax.fori_loop(0, high - low, layer, 0, unroll=True)
+        lax.fori_loop(0, high - low, layer, 0, unroll=UNROLL)
 
     loads[2].wait()
     pull(s2, a3, a2, -2, CY + 2, 4, 5, True)
@@ -523,17 +537,20 @@
     )(initial_state, before, after, below, above, slots)
     sums = lax.all_to_all(sums, AXES, split_axis=0, concat_axis=0, tiled=True)
     rim = shape(len(FORCE_BLOCKS), PACKED, LANES)
-    force, first_rows, last_rows = call(
-        functools.partial(force_kernel, beams, per_row),
-        (shape(FIELDS, CY, CX, LANES), rim, rim),
-        [pltpu.VMEM((FIELDS, LANES, COLUMNS), F32), pltpu.VMEM((FIELDS, rows, LANES), F32)],
+    part = shape(FIELDS, 2, CY, ROWS, LANES)
+    total = pltpu.VMEM((FIELDS, LANES, 2 * GROUP), F32)
+    outer, weight, first_rows, last_rows = call(
+        functools.partial(outer_force_kernel, beams, per_row),
+        (part, shape(FIELDS, rows, LANES), rim, rim),
+        [total],
         limit=40,
         ins=3,
     )(slots, seen, sums)
     after = shift(first_rows, "gx", -1)
     before = shift(last_rows, "gx", 1)
+    inner = call(inner_force_kernel, part, [total], limit=40, ins=2, micros=9)(slots, weight)
     piece = shape(FORCE_PIECE, LANES)
-    first_layers, last_layers = call(force_rim_kernel, (piece, piece), ins=3)(force, before, after)
+    first_layers, last_layers = call(force_rim_kernel, (piece, piece), ins=4)(outer, inner, before, after)
     above = shift(first_layers, "gy", -1)
     below = shift(last_layers, "gy", 1)
     padded = pltpu.VMEM((3, FH, XH, LANES), F32)
@@ -542,10 +559,10 @@
         shape(*initial_state.shape),
         [pltpu.VMEM(field.shape, F32)] * 3 + [padded] * 4 + [mask, pltpu.SemaphoreType.DMA((3,))],
         limit=40,
-        ins=8,
-        far_in=(5, 6, 7),
+        ins=9,
+        far_in=(6, 7, 8),
     )(
-        force, before, after, below, above, s0, s1, s2
+        outer, inner, before, after, below, above, s0, s1, s2
     )
 
 

time: 123 us -> 117 us (0.951)
  the two profiles are of different devices: /device:TPU:1 before, /device:TPU:5 now
where the time goes in v2:
time: 117 us
  Pallas kernels  61.6 us (53%)
  starting transfers between devices  28.7 us (25%)
  blocking collectives  12.6 us (11%)
  waiting for transfers between devices  10.7 us (9%)
  local copies, waits for them, and re-layouts  2.88 us (2%)
    pallas_call x1, Pallas kernels, local(): call(functools.partial(forward_kernel, beams, per_row), (shape(STEPS, row...  25.9 us
    ppermute x8, starting transfers between devices, shift(): lax.ppermute(values, axis, [(i, i + by) for i in range(count) if 0 <= i +...  22.6 us
    all_to_all x1, blocking collectives, local(): sums = lax.all_to_all(sums, AXES, split_axis=0, concat_axis=0, tiled=True)  12.6 us
    pallas_call x1, Pallas kernels, local(): call(backward_kernel, shape(*initial_state.shape), [pltpu.VMEM(field.shap...  11.3 us
    ppermute x8, waiting for transfers between devices, shift(): lax.ppermute(values, axis, [(i, i + by) for i in range(count) if 0 <= i +...  10.7 us
    pallas_call x1, Pallas kernels, local(): call(functools.partial(outer_force_kernel, beams, per_row), (part, shape(...  10.5 us
    pallas_call x1, Pallas kernels, local(): call(inner_force_kernel, part, [total], limit=40, ins=2, micros=9)  9.91 us
    all_to_all x1, starting transfers between devices, local(): slots = lax.all_to_all(slots, AXES, split_axis=0, concat_axis=0, tiled=True)  6.09 us
  transfers between devices with their start and end apart: 9, of which 4 were waited for; matrix products, arithmetic and copies ran while one was open for 0% of the time, Pallas kernels for 10%

profile of v2, /device:TPU:5, one launch (start us, length us, event | category | flops | bytes accessed | tf_op | source)
XLA Modules:
  0.0 116.6 jit_solution(16397047395150408396)
XLA Ops:
  0.0 0.0 copy-start.1
  0.0 2.4 %shard_map.55 = (f32[32,8,128]{2,1,0:T(8,128)}, f32[16,3072]{1,0:T(8,128)}, f32[16,3072]{1,0:T(8,128)}) custom-call(f32[3,32,3072]{2,1,0:T(8,128)} %state.5, f32[3,4]{1,0:T(4,128)} %beam_dir.1, f32[3,1,32,128]{3,2,1,0:T(8,128)} %obs.1, s32[1,32,128]{2,1,0:T(8,128)} %beam.1, s32[1,32,128]{2,1,0:T(8,128)} %cell.1), custom_call_target="tpu_custom_call" | custom-call | bytes 3000000 | tf_op jit(solution)/shard_map/pallas_call | solution.py:514
  2.4 3.1 %collective-permute-start = (f32[16,3072]{1,0:T(8,128)}, f32[16,3072]{1,0:T(8,128)S(1)}, u32[]{:S(2)}, u32[]{:S(2)}) collective-permute-start(f32[16,3072]{1,0:T(8,128)} %get-tuple-element.22), channel_id=1, source_target_pairs={{0,8},{8,16},{16,24},{1,9},{9,17},{17,25},{2,10},{10,18},{18,26},{... | collective-permute-start | bytes 589832 | tf_op jit(solution)/shard_map/ppermute | solution.py:504
  5.5 3.1 %collective-permute-start.1 = (f32[16,3072]{1,0:T(8,128)}, f32[16,3072]{1,0:T(8,128)S(1)}, u32[]{:S(2)}, u32[]{:S(2)}) collective-permute-start(f32[16,3072]{1,0:T(8,128)} %get-tuple-element.23), channel_id=1, source_target_pairs={{8,0},{16,8},{24,16},{9,1},{17,9},{25,17},{10,2},{18,10},{26,18},{... | collective-permute-start | bytes 589832 | tf_op jit(solution)/shard_map/ppermute | solution.py:504
  8.6 6.1 %all-to-all-start = ((f32[32,8,128]{2,1,0:T(8,128)}), f32[32,8,128]{2,1,0:T(8,128)S(1)}, u32[]{:S(2)}, u32[]{:S(2)}) async-start(f32[32,8,128]{2,1,0:T(8,128)} %get-tuple-element.21), calls=%async_computation | async-start | bytes 262144 | tf_op jit(solution)/shard_map/all_to_all | solution.py:519
  14.7 0.0 collective-permute-done.before
  14.7 0.0 collective-permute-done.1.after
  14.7 0.0 copy-start
  14.7 1.3 %copy-done = f32[3,32,3072]{2,1,0:T(8,128)S(1)} copy-done((f32[3,32,3072]{2,1,0:T(8,128)S(1)}, f32[3,32,3072]{2,1,0:T(8,128)}, u32[]{:S(2)}) %copy-start) | copy-done | bytes 1179672
  16.0 1.3 %shard_map.56 = (f32[424,128]{1,0:T(8,128)S(1)}, f32[424,128]{1,0:T(8,128)S(1)}) custom-call(f32[3,32,3072]{2,1,0:T(8,128)S(1)} %copy-done, f32[16,3072]{1,0:T(8,128)S(1)} %collective-permute-done.before, f32[16,3072]{1,0:T(8,128)S(1)} %collective-permute-done.1.after), custom_call_target="tpu_custom_call" | custom-call | bytes 3000000 | tf_op jit(solution)/shard_map/pallas_call | solution.py:523
  17.3 3.5 %collective-permute-start.2 = (f32[424,128]{1,0:T(8,128)S(1)}, f32[424,128]{1,0:T(8,128)S(1)}, u32[]{:S(2)}, u32[]{:S(2)}) collective-permute-start(f32[424,128]{1,0:T(8,128)S(1)} %get-tuple-element.24), channel_id=1, source_target_pairs={{0,1},{1,2},{2,3},{3,4},{4,5},{5,6},{6,7},{8,9},{9,10},{10,11},{11... | collective-permute-start | bytes 651272 | tf_op jit(solution)/shard_map/ppermute | solution.py:504
  20.8 1.9 %collective-permute-start.3 = (f32[424,128]{1,0:T(8,128)S(1)}, f32[424,128]{1,0:T(8,128)S(1)}, u32[]{:S(2)}, u32[]{:S(2)}) collective-permute-start(f32[424,128]{1,0:T(8,128)S(1)} %get-tuple-element.25), channel_id=1, source_target_pairs={{1,0},{2,1},{3,2},{4,3},{5,4},{6,5},{7,6},{9,8},{10,9},{11,10},{12... | collective-permute-start | bytes 651272 | tf_op jit(solution)/shard_map/ppermute | solution.py:504
  22.7 0.0 all-to-all-done.slots
  22.8 0.9 collective-permute-done.2.below
  23.6 4.4 %collective-permute-done.3.above = f32[424,128]{1,0:T(8,128)S(1)} collective-permute-done((f32[424,128]{1,0:T(8,128)S(1)}, f32[424,128]{1,0:T(8,128)S(1)}, u32[]{:S(2)}, u32[]{:S(2)}) %collective-permute-start.3) | collective-permute-done | bytes 217120 | tf_op jit(solution)/shard_map/ppermute | solution.py:504
  28.0 0.0 copy-done.1
  28.0 25.9 %shard_map.57 = (f32[3,32,128]{2,1,0:T(8,128)S(1)}, f32[32,8,128]{2,1,0:T(8,128)S(1)}, f32[3,42,48,128]{3,2,1,0:T(8,128)S(1)}, f32[3,42,48,128]{3,2,1,0:T(8,128)S(1)}, f32[3,42,48,128]{3,2,1,0:T(8,128)S(1)}) custom-call(f32[3,32,3072]{2,1,0:T(8,128)S(1)} %copy-done.1, f32[16,3072]{1,0:T(8,128)S(1)} %collective-permute-done.before, ...), custom_call_target="tpu_custom_call" | custom-call | bytes 3000000 | tf_op jit(solution)/shard_map/pallas_call | solution.py:529
  53.9 0.0 copy-start.2
  54.0 1.6 %copy-done.2 = f32[3,42,48,128]{3,2,1,0:T(8,128)} copy-done((f32[3,42,48,128]{3,2,1,0:T(8,128)}, f32[3,42,48,128]{3,2,1,0:T(8,128)S(1)}, u32[]{:S(2)}) %copy-start.2) | copy-done | bytes 3096600
  55.6 12.6 %all_to_all.10.sums = f32[32,8,128]{2,1,0:T(8,128)S(1)} all-to-all(f32[32,8,128]{2,1,0:T(8,128)S(1)} %get-tuple-element.27), channel_id=1, replica_groups=mesh['gx'=4,'gy'=8] {'gx','gy'}, dimensions={0} | all-to-all | bytes 262144 | tf_op jit(solution)/shard_map/all_to_all | solution.py:538
  68.2 10.5 %shard_map.58 = (f32[9,2,32,8,128]{4,3,2,1,0:T(8,128)S(1)}, f32[9,32,128]{2,1,0:T(8,128)S(1)}, f32[18,24,128]{2,1,0:T(8,128)S(1)}, f32[18,24,128]{2,1,0:T(8,128)S(1)}) custom-call(f32[32,8,128]{2,1,0:T(8,128)S(1)} %all-to-all-done.slots, f32[3,32,128]{2,1,0:T(8,128)S(1)} %get-tuple-element.26.seen, f32[32,8,128]{2,1,0:T(8,128)S(1)} %all_to_all.10.sums), custom_call_target="tpu_custom_call" | custom-call | bytes 3000000 | tf_op jit(solution)/shard_map/pallas_call | solution.py:542
  78.7 2.2 %collective-permute-start.4 = (f32[18,24,128]{2,1,0:T(8,128)S(1)}, f32[18,24,128]{2,1,0:T(8,128)S(1)}, u32[]{:S(2)}, u32[]{:S(2)}) collective-permute-start(f32[18,24,128]{2,1,0:T(8,128)S(1)} %get-tuple-element.30), channel_id=1, source_target_pairs={{0,8},{8,16},{16,24},{1,9},{9,17},{17,25},{2,10},{10,18},{18,26},{... | collective-permute-start | bytes 663560 | tf_op jit(solution)/shard_map/ppermute | solution.py:504
  81.0 3.9 %collective-permute-start.5 = (f32[18,24,128]{2,1,0:T(8,128)S(1)}, f32[18,24,128]{2,1,0:T(8,128)S(1)}, u32[]{:S(2)}, u32[]{:S(2)}) collective-permute-start(f32[18,24,128]{2,1,0:T(8,128)S(1)} %get-tuple-element.31), channel_id=1, source_target_pairs={{8,0},{16,8},{24,16},{9,1},{17,9},{25,17},{10,2},{18,10},{26,18},{... | collective-permute-start | bytes 663560 | tf_op jit(solution)/shard_map/ppermute | solution.py:504
  84.9 9.9 %shard_map.59.inner = f32[9,2,32,8,128]{4,3,2,1,0:T(8,128)S(1)} custom-call(f32[32,8,128]{2,1,0:T(8,128)S(1)} %all-to-all-done.slots, f32[9,32,128]{2,1,0:T(8,128)S(1)} %get-tuple-element.29.weight), custom_call_target="tpu_custom_call" | custom-call | bytes 27000000 | tf_op jit(solution)/shard_map/pallas_call | solution.py:551
  94.8 0.0 collective-permute-done.4.before
  94.9 0.0 collective-permute-done.5.after
  94.9 0.3 shard_map.60
  95.1 2.9 %collective-permute-start.6 = (f32[456,128]{1,0:T(8,128)S(1)}, f32[456,128]{1,0:T(8,128)S(1)}, u32[]{:S(2)}, u32[]{:S(2)}) collective-permute-start(f32[456,128]{1,0:T(8,128)S(1)} %get-tuple-element.32), channel_id=1, source_target_pairs={{0,1},{1,2},{2,3},{3,4},{4,5},{5,6},{6,7},{8,9},{9,10},{10,11},{11... | collective-permute-start | bytes 700424 | tf_op jit(solution)/shard_map/ppermute | solution.py:504
  98.0 1.9 %collective-permute-start.7 = (f32[456,128]{1,0:T(8,128)S(1)}, f32[456,128]{1,0:T(8,128)S(1)}, u32[]{:S(2)}, u32[]{:S(2)}) collective-permute-start(f32[456,128]{1,0:T(8,128)S(1)} %get-tuple-element.33), channel_id=1, source_target_pairs={{1,0},{2,1},{3,2},{4,3},{5,4},{6,5},{7,6},{9,8},{10,9},{11,10},{12... | collective-permute-start | bytes 700424 | tf_op jit(solution)/shard_map/ppermute | solution.py:504
  99.9 1.1 collective-permute-done.6.below
  101.0 4.4 %collective-permute-done.7.above = f32[456,128]{1,0:T(8,128)S(1)} collective-permute-done((f32[456,128]{1,0:T(8,128)S(1)}, f32[456,128]{1,0:T(8,128)S(1)}, u32[]{:S(2)}, u32[]{:S(2)}) %collective-permute-start.7) | collective-permute-done | bytes 233504 | tf_op jit(solution)/shard_map/ppermute | solution.py:504
  105.4 11.3 %shard_map.61 = f32[3,32,3072]{2,1,0:T(8,128)} custom-call(f32[9,2,32,8,128]{4,3,2,1,0:T(8,128)S(1)} %get-tuple-element.28.outer, f32[9,2,32,8,128]{4,3,2,1,0:T(8,128)S(1)} %shard_map.59.inner, f32[18,24,128]{2,1,0:T(8,128)S(1)} %collective-permute-done.4.before, f32[18,24,128]{2,1,0:T(8,128)S(1)} %collective-permute-done.5.after, ...), custom_call_target="tpu_custom_call" | custom-call | bytes 3000000 | tf_op jit(solution)/shard_map/pallas_call | solution.py:557
Async XLA Ops:
  0.0 28.0 %copy-start.1 = (f32[3,32,3072]{2,1,0:T(8,128)S(1)}, f32[3,32,3072]{2,1,0:T(8,128)}, u32[]{:S(2)}) copy-start(f32[3,32,3072]{2,1,0:T(8,128)} %state.5) | copy-start | bytes 3538948
  2.4 12.3 %collective-permute-start = (f32[16,3072]{1,0:T(8,128)}, f32[16,3072]{1,0:T(8,128)S(1)}, u32[]{:S(2)}, u32[]{:S(2)}) collective-permute-start(f32[16,3072]{1,0:T(8,128)} %get-tuple-element.22), channel_id=1, source_target_pairs={{0,8},{8,16},{16,24},{1,9},{9,17},{17,25},{2,10},{10,18},{18,26},{... | collective-permute-start | bytes 589832 | tf_op jit(solution)/shard_map/ppermute | solution.py:504
  5.5 9.2 %collective-permute-start.1 = (f32[16,3072]{1,0:T(8,128)}, f32[16,3072]{1,0:T(8,128)S(1)}, u32[]{:S(2)}, u32[]{:S(2)}) collective-permute-start(f32[16,3072]{1,0:T(8,128)} %get-tuple-element.23), channel_id=1, source_target_pairs={{8,0},{16,8},{24,16},{9,1},{17,9},{25,17},{10,2},{18,10},{26,18},{... | collective-permute-start | bytes 589832 | tf_op jit(solution)/shard_map/ppermute | solution.py:504
  8.6 14.1 %all-to-all-start = ((f32[32,8,128]{2,1,0:T(8,128)}), f32[32,8,128]{2,1,0:T(8,128)S(1)}, u32[]{:S(2)}, u32[]{:S(2)}) async-start(f32[32,8,128]{2,1,0:T(8,128)} %get-tuple-element.21), calls=%async_computation | async-start | bytes 262144 | tf_op jit(solution)/shard_map/all_to_all | solution.py:519
  14.7 1.3 %copy-start = (f32[3,32,3072]{2,1,0:T(8,128)S(1)}, f32[3,32,3072]{2,1,0:T(8,128)}, u32[]{:S(2)}) copy-start(f32[3,32,3072]{2,1,0:T(8,128)} %state.5) | copy-start | bytes 3538948
  17.3 6.3 %collective-permute-start.2 = (f32[424,128]{1,0:T(8,128)S(1)}, f32[424,128]{1,0:T(8,128)S(1)}, u32[]{:S(2)}, u32[]{:S(2)}) collective-permute-start(f32[424,128]{1,0:T(8,128)S(1)} %get-tuple-element.24), channel_id=1, source_target_pairs={{0,1},{1,2},{2,3},{3,4},{4,5},{5,6},{6,7},{8,9},{9,10},{10,11},{11... | collective-permute-start | bytes 651272 | tf_op jit(solution)/shard_map/ppermute | solution.py:504
  20.8 7.2 %collective-permute-start.3 = (f32[424,128]{1,0:T(8,128)S(1)}, f32[424,128]{1,0:T(8,128)S(1)}, u32[]{:S(2)}, u32[]{:S(2)}) collective-permute-start(f32[424,128]{1,0:T(8,128)S(1)} %get-tuple-element.25), channel_id=1, source_target_pairs={{1,0},{2,1},{3,2},{4,3},{5,4},{6,5},{7,6},{9,8},{10,9},{11,10},{12... | collective-permute-start | bytes 651272 | tf_op jit(solution)/shard_map/ppermute | solution.py:504
  53.9 1.6 %copy-start.2 = (f32[3,42,48,128]{3,2,1,0:T(8,128)}, f32[3,42,48,128]{3,2,1,0:T(8,128)S(1)}, u32[]{:S(2)}) copy-start(f32[3,42,48,128]{3,2,1,0:T(8,128)S(1)} %get-tuple-element.36.kept2) | copy-start | bytes 9289732
  78.7 16.1 %collective-permute-start.4 = (f32[18,24,128]{2,1,0:T(8,128)S(1)}, f32[18,24,128]{2,1,0:T(8,128)S(1)}, u32[]{:S(2)}, u32[]{:S(2)}) collective-permute-start(f32[18,24,128]{2,1,0:T(8,128)S(1)} %get-tuple-element.30), channel_id=1, source_target_pairs={{0,8},{8,16},{16,24},{1,9},{9,17},{17,25},{2,10},{10,18},{18,26},{... | collective-permute-start | bytes 663560 | tf_op jit(solution)/shard_map/ppermute | solution.py:504
  81.0 13.9 %collective-permute-start.5 = (f32[18,24,128]{2,1,0:T(8,128)S(1)}, f32[18,24,128]{2,1,0:T(8,128)S(1)}, u32[]{:S(2)}, u32[]{:S(2)}) collective-permute-start(f32[18,24,128]{2,1,0:T(8,128)S(1)} %get-tuple-element.31), channel_id=1, source_target_pairs={{8,0},{16,8},{24,16},{9,1},{17,9},{25,17},{10,2},{18,10},{26,18},{... | collective-permute-start | bytes 663560 | tf_op jit(solution)/shard_map/ppermute | solution.py:504
  95.1 5.9 %collective-permute-start.6 = (f32[456,128]{1,0:T(8,128)S(1)}, f32[456,128]{1,0:T(8,128)S(1)}, u32[]{:S(2)}, u32[]{:S(2)}) collective-permute-start(f32[456,128]{1,0:T(8,128)S(1)} %get-tuple-element.32), channel_id=1, source_target_pairs={{0,1},{1,2},{2,3},{3,4},{4,5},{5,6},{6,7},{8,9},{9,10},{10,11},{11... | collective-permute-start | bytes 700424 | tf_op jit(solution)/shard_map/ppermute | solution.py:504
  98.0 7.4 %collective-permute-start.7 = (f32[456,128]{1,0:T(8,128)S(1)}, f32[456,128]{1,0:T(8,128)S(1)}, u32[]{:S(2)}, u32[]{:S(2)}) collective-permute-start(f32[456,128]{1,0:T(8,128)S(1)} %get-tuple-element.33), channel_id=1, source_target_pairs={{1,0},{2,1},{3,2},{4,3},{5,4},{6,5},{7,6},{9,8},{10,9},{11,10},{12... | collective-permute-start | bytes 700424 | tf_op jit(solution)/shard_map/ppermute | solution.py:504

commit v3 on v2

--- a/solution.py
+++ b/solution.py
@@ -79,12 +79,20 @@
     return jnp.concatenate(parts + [last], axis=0)
 
 
-def column_block(ref, comp, y):
-    return ref[comp, :, NZ * y : NZ * y + NZ]
-
-
-def widen(block):
-    return jnp.concatenate([block, jnp.zeros((block.shape[0], LANES - NZ), F32)], axis=1)
+def is_odd(axis):
+    return lax.axis_index(axis) % 2 == 1
+
+
+def to_partners(axis, first, last, near, far):
+    odd = is_odd(axis)
+    near[...] = jnp.where(odd, first[...], last[...])
+    far[...] = jnp.where(odd, last[...], first[...])
+
+
+def from_partners(axis, near, far, behind, ahead):
+    odd = is_odd(axis)
+    behind[...] = jnp.where(odd, near[...], far[...])
+    ahead[...] = jnp.where(odd, far[...], near[...])
 
 
 def corner_rows(rim):
@@ -110,7 +118,13 @@
 FORCE_PIECE = len(FORCE_BLOCKS) * PACKED + 24
 
 
-def prepare_kernel(state, beam_dir, obs, beam, cell, slots, first_rows, last_rows):
+def prepare_kernel(state, beam_dir, obs, beam, cell, slots, near, far, first_rows, last_rows):
+    for c in range(3):
+        first_rows[RIM * c : RIM * c + RIM, :] = state[c, 0:RIM, :]
+        last_rows[RIM * c : RIM * c + RIM, :] = state[c, CX - RIM : CX, :]
+    first_rows[3 * RIM : 16, :] = jnp.zeros((1, CY * NZ), F32)
+    last_rows[3 * RIM : 16, :] = jnp.zeros((1, CY * NZ), F32)
+    to_partners("gx", first_rows, last_rows, near, far)
     beams = beam_dir.shape[1]
     owned = beam[0]
     used = owned >= 0
@@ -130,14 +144,13 @@
         slots[:, 2 + n, :] = jnp.where(used, seen - spread(means), 0.0)
     for c in range(3):
         slots[:, 5 + c, :] = spread([beam_dir[c : c + 1, k : k + 1] for k in range(beams)])
+
+
+def layout_kernel(state, wide, first_layers, last_layers):
+    wide[...] = jnp.zeros(wide.shape, F32)
     for c in range(3):
-        first_rows[RIM * c : RIM * c + RIM, :] = state[c, 0:RIM, :]
-        last_rows[RIM * c : RIM * c + RIM, :] = state[c, CX - RIM : CX, :]
-    first_rows[3 * RIM : 16, :] = jnp.zeros((1, CY * NZ), F32)
-    last_rows[3 * RIM : 16, :] = jnp.zeros((1, CY * NZ), F32)
-
-
-def state_rim_kernel(state, before, after, first_layers, last_layers):
+        for y in range(CY):
+            wide[c, RIM + y, PAD : PAD + CX, 0:NZ] = state[c, :, NZ * y : NZ * y + NZ]
     for out, layer_of in ((first_layers, lambda d: d - 1), (last_layers, lambda d: CY - d)):
         for c in range(3):
             for dist in range(1, RIM + 1):
@@ -146,13 +159,23 @@
                 def put(row, rows, base=base, out=out):
                     out[base + row : base + row + 8, :] = rows
 
-                pack(put, widen(column_block(state, c, layer_of(dist))))
-        base = 3 * RIM * PACKED
+                pack(put, wide[c, RIM + layer_of(dist), PAD : PAD + CX, :])
+
+
+def state_corner_kernel(bulk_first, bulk_last, x_near, x_far, near, far, first, last, before, after):
+    from_partners("gx", x_near, x_far, before, after)
+    base = 3 * RIM * PACKED
+    for bulk, out, layer_of in (
+        (bulk_first, first, lambda d: d - 1),
+        (bulk_last, last, lambda d: CY - d),
+    ):
+        out[0:base, :] = bulk[...]
         out[base : base + 64, :] = jnp.zeros((64, LANES), F32)
         for c, dist, row, side in STATE_CORNERS:
             lanes = slice(NZ * layer_of(dist), NZ * layer_of(dist) + NZ)
             out[base + row : base + row + side, 0:NZ] = before[RIM * c + dist : RIM * c + RIM, lanes]
             out[base + row + side : base + row + 2 * side, 0:NZ] = after[RIM * c : RIM * c + side, lanes]
+    to_partners("gy", first, last, near, far)
 
 
 def row_mask(x_place, x_count):
@@ -241,15 +264,35 @@
 
 
 def forward_kernel(
-    beams, per_row, state, before, after, below, above, slots, seen, sums, kept0, kept1, kept2, s0, s1, s2, s3, table, mask, sem
+    beams,
+    per_row,
+    wide,
+    x_near,
+    x_far,
+    y_near,
+    y_far,
+    slots,
+    seen,
+    sums,
+    s0,
+    s1,
+    s2,
+    s3,
+    table,
+    mask,
+    below,
+    above,
+    before,
+    after,
 ):
     places = mesh_places()
+    from_partners("gx", x_near, x_far, before, after)
     mask[...] = row_mask(places[0], places[1])
-    s0[...] = jnp.zeros(s0.shape, F32)
+    from_partners("gy", y_near, y_far, below, above)
+    s0[...] = wide[...]
     for c in range(3):
         for y in range(CY):
             lanes = slice(NZ * y, NZ * y + NZ)
-            s0[c, RIM + y, PAD : PAD + CX, 0:NZ] = state[c, :, lanes]
             s0[c, RIM + y, PAD - RIM : PAD, 0:NZ] = before[RIM * c : RIM * c + RIM, lanes]
             s0[c, RIM + y, PAD + CX : PAD + CX + RIM, 0:NZ] = after[RIM * c : RIM * c + RIM, lanes]
     for piece, layer_of in ((above, lambda d: RIM + CY - 1 + d), (below, lambda d: RIM - d)):
@@ -263,15 +306,8 @@
             s0[c, layer_of(dist), PAD + CX : PAD + CX + side, :] = piece[
                 base + row + side : base + row + 2 * side, :
             ]
-    keeps = [
-        pltpu.make_async_copy(field, kept, sem.at[n])
-        for n, (field, kept) in enumerate(((s0, kept0), (s1, kept1), (s2, kept2)))
-    ]
-    keeps[0].start()
     step_forward(s0, s1, -4, CY + 4, 4, 5, mask, places)
-    keeps[1].start()
     step_forward(s1, s2, -3, CY + 3, 4, 5, mask, places)
-    keeps[2].start()
     step_forward(s2, s3, 0, CY, PAD, 4, mask, places)
 
     half = FIELDS * NZ
@@ -321,8 +357,6 @@
             one = turned[line * per_line + k : line * per_line + k + 1]
             total = total + pltpu.roll(one, rows * k, axis=1)
         sums[:, line : line + 1, :] = jnp.broadcast_to(total[None], (sums.shape[0], 1, LANES))
-    for keep in keeps:
-        keep.wait()
 
 
 def row_beam(beams, per_row, slots):
@@ -362,7 +396,9 @@
             force[f, k] = total[f, :, GROUP * k : GROUP * k + GROUP].T.reshape(CY, ROWS, LANES)
 
 
-def outer_force_kernel(beams, per_row, slots, seen, sums, force, weight, first_rows, last_rows, total):
+def outer_force_kernel(
+    beams, per_row, slots, seen, sums, force, weight, near, far, first_rows, last_rows, total
+):
     rows = slots.shape[0]
     per_line = LANES // rows
     lines = jnp.sum(sums[...], axis=0) / GATES
@@ -390,13 +426,15 @@
                 out[b, row : row + 8, :] = rows
 
             pack(put, force[3 * n + c, k, :, row_of(i), :])
+    to_partners("gx", first_rows, last_rows, near, far)
 
 
 def inner_force_kernel(slots, weight, force, total):
     scatter_slots((1, 2), slots, weight, total, force)
 
 
-def force_rim_kernel(outer, inner, before, after, first_layers, last_layers):
+def force_rim_kernel(outer, inner, x_near, x_far, near, far, first_layers, last_layers, before, after):
+    from_partners("gx", x_near, x_far, before, after)
     index = {key: b for b, key in enumerate(FORCE_BLOCKS)}
     for out, layer_of in ((first_layers, lambda d: d - 1), (last_layers, lambda d: CY - d)):
         for b, (n, c, i) in enumerate(FORCE_BLOCKS):
@@ -412,17 +450,32 @@
             block = unpack(piece[index[(n, c, k - 1)]])
             y = layer_of(dist)
             out[base + row : base + row + 1, :] = block[y : y + 1]
+    to_partners("gy", first_layers, last_layers, near, far)
 
 
 def backward_kernel(
-    outer, inner, before, after, below, above, kept0, kept1, kept2, out, s0, s1, s2, a3, a2, a1, a0, mask, sem
+    outer,
+    inner,
+    x_near,
+    x_far,
+    y_near,
+    y_far,
+    s0,
+    s1,
+    s2,
+    out,
+    a3,
+    a2,
+    a1,
+    a0,
+    mask,
+    below,
+    above,
+    before,
+    after,
 ):
-    loads = [
-        pltpu.make_async_copy(kept, field, sem.at[n])
-        for n, (field, kept) in enumerate(((s0, kept0), (s1, kept1), (s2, kept2)))
-    ]
-    for n in (2, 1, 0):
-        loads[n].start()
+    from_partners("gx", x_near, x_far, before, after)
+    from_partners("gy", y_near, y_far, below, above)
     places = mesh_places()
     mask[...] = row_mask(places[0], places[1])
     adjoints = (a1, a2, a3)
@@ -488,20 +541,20 @@
 
         lax.fori_loop(0, high - low, layer, 0, unroll=UNROLL)
 
-    loads[2].wait()
     pull(s2, a3, a2, -2, CY + 2, 4, 5, True)
-    loads[1].wait()
     pull(s1, a2, a1, -1, CY + 1, 4, 5, True)
-    loads[0].wait()
     pull(s0, a1, a0, 0, CY, PAD, 4, False)
     for c in range(3):
         for y in range(CY):
             out[c, :, NZ * y : NZ * y + NZ] = a0[c, FRIM + y, PAD : PAD + CX, 0:NZ]
 
 
-def shift(values, axis, by):
-    count = lax.axis_size(axis)
-    return lax.ppermute(values, axis, [(i, i + by) for i in range(count) if 0 <= i + by < count])
+def swap(near, far, axis):
+    def pairs(start):
+        lows = range(start, lax.axis_size(axis) - 1, 2)
+        return [(i, i + 1) for i in lows] + [(i + 1, i) for i in lows]
+
+    return lax.ppermute(near, axis, pairs(0)), lax.ppermute(far, axis, pairs(1))
 
 
 def local(initial_state, beam_dir, gate_obs, slot_beam, slot_cell):
@@ -510,60 +563,71 @@
     beams = beam_dir.shape[1]
     per_row = group * beams
     rows = peers // group
-    rim_rows_shape = shape(16, CY * NZ)
-    slots, first_rows, last_rows = call(
-        prepare_kernel, (shape(peers, 8, capacity), rim_rows_shape, rim_rows_shape), limit=60, ins=5
+    x_rim = (16, CY * NZ)
+    slots, near, far = call(
+        prepare_kernel,
+        (shape(peers, 8, capacity), shape(*x_rim), shape(*x_rim)),
+        [pltpu.VMEM(x_rim, F32)] * 2,
+        limit=60,
+        ins=5,
     )(initial_state, beam_dir, gate_obs, slot_beam, slot_cell)
-    after = shift(first_rows, "gx", -1)
-    before = shift(last_rows, "gx", 1)
+    x_near, x_far = swap(near, far, "gx")
     slots = lax.all_to_all(slots, AXES, split_axis=0, concat_axis=0, tiled=True)
     if group > 1:
         slots = slots.reshape(rows, group, 8, capacity).transpose(0, 2, 1, 3).reshape(rows, 8, LANES)
-    piece = shape(STATE_PIECE, LANES)
-    first_layers, last_layers = call(state_rim_kernel, (piece, piece), ins=3)(initial_state, before, after)
-    above = shift(first_layers, "gy", -1)
-    below = shift(last_layers, "gy", 1)
+    field = shape(3, YH, XH, LANES)
+    bulk = shape(3 * RIM * PACKED, LANES)
+    wide, bulk_first, bulk_last = call(layout_kernel, (field, bulk, bulk), ins=1, micros=2)(initial_state)
+    y_rim = (STATE_PIECE, LANES)
+    near, far = call(
+        state_corner_kernel,
+        (shape(*y_rim), shape(*y_rim)),
+        [pltpu.VMEM(y_rim, F32)] * 2 + [pltpu.VMEM(x_rim, F32)] * 2,
+        ins=4,
+    )(bulk_first, bulk_last, x_near, x_far)
+    y_near, y_far = swap(near, far, "gy")
     lines = -(-STEPS * per_row * rows // LANES // 8) * 8
-    field = shape(3, YH, XH, LANES)
     mask = pltpu.VMEM((XH, LANES), F32)
     seen, sums, s0, s1, s2 = call(
         functools.partial(forward_kernel, beams, per_row),
         (shape(STEPS, rows, LANES), shape(peers, lines, LANES), field, field, field),
-        [pltpu.VMEM(field.shape, F32)] * 4
-        + [pltpu.VMEM((2 * FIELDS * NZ, COLUMNS), BF16), mask, pltpu.SemaphoreType.DMA((3,))],
-        limit=40,
+        [pltpu.VMEM(field.shape, F32), pltpu.VMEM((2 * FIELDS * NZ, COLUMNS), BF16), mask]
+        + [pltpu.VMEM(y_rim, F32)] * 2
+        + [pltpu.VMEM(x_rim, F32)] * 2,
+        limit=32,
         ins=6,
-        far_out=(2, 3, 4),
-    )(initial_state, before, after, below, above, slots)
+    )(wide, x_near, x_far, y_near, y_far, slots)
     sums = lax.all_to_all(sums, AXES, split_axis=0, concat_axis=0, tiled=True)
-    rim = shape(len(FORCE_BLOCKS), PACKED, LANES)
+    x_rim = (len(FORCE_BLOCKS), PACKED, LANES)
     part = shape(FIELDS, 2, CY, ROWS, LANES)
     total = pltpu.VMEM((FIELDS, LANES, 2 * GROUP), F32)
-    outer, weight, first_rows, last_rows = call(
+    outer, weight, near, far = call(
         functools.partial(outer_force_kernel, beams, per_row),
-        (part, shape(FIELDS, rows, LANES), rim, rim),
-        [total],
-        limit=40,
+        (part, shape(FIELDS, rows, LANES), shape(*x_rim), shape(*x_rim)),
+        [pltpu.VMEM(x_rim, F32)] * 2 + [total],
+        limit=24,
         ins=3,
     )(slots, seen, sums)
-    after = shift(first_rows, "gx", -1)
-    before = shift(last_rows, "gx", 1)
-    inner = call(inner_force_kernel, part, [total], limit=40, ins=2, micros=9)(slots, weight)
-    piece = shape(FORCE_PIECE, LANES)
-    first_layers, last_layers = call(force_rim_kernel, (piece, piece), ins=4)(outer, inner, before, after)
-    above = shift(first_layers, "gy", -1)
-    below = shift(last_layers, "gy", 1)
-    padded = pltpu.VMEM((3, FH, XH, LANES), F32)
+    x_near, x_far = swap(near, far, "gx")
+    inner = call(inner_force_kernel, part, [total], limit=24, ins=2, micros=9)(slots, weight)
+    y_rim = (FORCE_PIECE, LANES)
+    near, far = call(
+        force_rim_kernel,
+        (shape(*y_rim), shape(*y_rim)),
+        [pltpu.VMEM(y_rim, F32)] * 2 + [pltpu.VMEM(x_rim, F32)] * 2,
+        ins=4,
+    )(outer, inner, x_near, x_far)
+    y_near, y_far = swap(near, far, "gy")
     return call(
         backward_kernel,
         shape(*initial_state.shape),
-        [pltpu.VMEM(field.shape, F32)] * 3 + [padded] * 4 + [mask, pltpu.SemaphoreType.DMA((3,))],
-        limit=40,
+        [pltpu.VMEM((3, FH, XH, LANES), F32)] * 4
+        + [mask]
+        + [pltpu.VMEM(y_rim, F32)] * 2
+        + [pltpu.VMEM(x_rim, F32)] * 2,
+        limit=32,
         ins=9,
-        far_in=(6, 7, 8),
-    )(
-        outer, inner, before, after, below, above, s0, s1, s2
-    )
+    )(outer, inner, x_near, x_far, y_near, y_far, s0, s1, s2)
 
 
 def solution(mesh):

time: 117 us -> 106 us (0.906)
  starting transfers between devices: 28.7 us -> 21.1 us
  local copies, waits for them, and re-layouts: 2.88 us -> 1.27 us
    ppermute x8, starting transfers between devices: 22.6 us -> 13.9 us  [the longest x4 11.1 us: swap(): lax.ppermute(far, axis, pairs(1))]
    unnamed x6 -> x2, local copies, waits for them, and re-layouts: 2.88 us -> 1.27 us
    pallas_call x5 -> x6, Pallas kernels: 25.1 us -> 25.5 us  [the longest x1 10.3 us: local(): call(backward_kernel, shape(*initial_state.shape), [pltpu.VMEM((3, FH, XH...]
  transfers between devices with their start and end apart: 9 -> 9, of which waited for: 4 -> 2; matrix products, arithmetic and copies ran while one was open for 0% -> 0% of each run, Pallas kernels for 10% -> 12%
where the time goes in v3:
time: 106 us
  Pallas kernels  61.2 us (58%)
  starting transfers between devices  21.1 us (20%)
  blocking collectives  12.5 us (12%)
  waiting for transfers between devices  9.64 us (9%)
  local copies, waits for them, and re-layouts  1.27 us (1%)
    pallas_call x1, Pallas kernels, local(): call(functools.partial(forward_kernel, beams, per_row), (shape(STEPS, row...  25.1 us
    all_to_all x1, blocking collectives, local(): sums = lax.all_to_all(sums, AXES, split_axis=0, concat_axis=0, tiled=True)  12.5 us
    ppermute x4, starting transfers between devices, swap(): lax.ppermute(far, axis, pairs(1))  11.1 us
    pallas_call x1, Pallas kernels, local(): call(functools.partial(outer_force_kernel, beams, per_row), (part, shape(...  10.6 us
    pallas_call x1, Pallas kernels, local(): call(backward_kernel, shape(*initial_state.shape), [pltpu.VMEM((3, FH, XH...  10.3 us
    pallas_call x1, Pallas kernels, local(): call(inner_force_kernel, part, [total], limit=24, ins=2, micros=9)  9.91 us
    ppermute x4, waiting for transfers between devices, swap(): lax.ppermute(far, axis, pairs(1))  9.62 us
    all_to_all x1, starting transfers between devices, local(): slots = lax.all_to_all(slots, AXES, split_axis=0, concat_axis=0, tiled=True)  7.22 us
  transfers between devices with their start and end apart: 9, of which 2 were waited for; matrix products, arithmetic and copies ran while one was open for 0% of the time, Pallas kernels for 12%

profile of v3, /device:TPU:5, one launch (start us, length us, event | category | flops | bytes accessed | tf_op | source)
XLA Modules:
  0.0 105.8 jit_solution(3206575339709430228)
XLA Ops:
  0.0 2.4 %shard_map.55 = (f32[32,8,128]{2,1,0:T(8,128)}, f32[16,3072]{1,0:T(8,128)}, f32[16,3072]{1,0:T(8,128)}) custom-call(f32[3,32,3072]{2,1,0:T(8,128)} %state.3, f32[3,4]{1,0:T(4,128)} %beam_dir.1, f32[3,1,32,128]{3,2,1,0:T(8,128)} %obs.1, s32[1,32,128]{2,1,0:T(8,128)} %beam.1, s32[1,32,128]{2,1,0:T(8,128)} %cell.1), custom_call_target="tpu_custom_call" | custom-call | bytes 3000000 | tf_op jit(solution)/shard_map/pallas_call | solution.py:567
  2.4 1.2 %collective-permute-start = (f32[16,3072]{1,0:T(8,128)}, f32[16,3072]{1,0:T(8,128)S(1)}, u32[]{:S(2)}, u32[]{:S(2)}) collective-permute-start(f32[16,3072]{1,0:T(8,128)} %get-tuple-element.26), channel_id=1, source_target_pairs={{0,8},{16,24},{8,0},{24,16},{1,9},{17,25},{9,1},{25,17},{2,10},{18... | collective-permute-start | bytes 589832 | tf_op jit(solution)/shard_map/ppermute | solution.py:557
  3.6 1.9 %collective-permute-start.1 = (f32[16,3072]{1,0:T(8,128)}, f32[16,3072]{1,0:T(8,128)}, u32[]{:S(2)}, u32[]{:S(2)}) collective-permute-start(f32[16,3072]{1,0:T(8,128)} %get-tuple-element.27), channel_id=1, source_target_pairs={{8,16},{16,8},{9,17},{17,9},{10,18},{18,10},{11,19},{19,11},{12,20... | collective-permute-start | bytes 589832 | tf_op jit(solution)/shard_map/ppermute | solution.py:557
  5.5 7.2 %all-to-all-start = ((f32[32,8,128]{2,1,0:T(8,128)}), f32[32,8,128]{2,1,0:T(8,128)S(1)}, u32[]{:S(2)}, u32[]{:S(2)}) async-start(f32[32,8,128]{2,1,0:T(8,128)} %get-tuple-element.24), calls=%async_computation | async-start | bytes 262144 | tf_op jit(solution)/shard_map/all_to_all | solution.py:575
  12.7 0.0 copy-start
  12.8 1.3 %copy-done = f32[3,32,3072]{2,1,0:T(8,128)S(1)} copy-done((f32[3,32,3072]{2,1,0:T(8,128)S(1)}, f32[3,32,3072]{2,1,0:T(8,128)}, u32[]{:S(2)}) %copy-start) | copy-done | bytes 1179672
  14.0 0.8 shard_map.56
  14.8 0.0 collective-permute-done.x_near
  14.8 0.0 collective-permute-done.1.x_far
  14.8 1.9 %shard_map.57 = (f32[424,128]{1,0:T(8,128)}, f32[424,128]{1,0:T(8,128)}) custom-call(f32[360,128]{1,0:T(8,128)S(1)} %get-tuple-element.28.bulk_first, f32[360,128]{1,0:T(8,128)S(1)} %get-tuple-element.29.bulk_last, f32[16,3072]{1,0:T(8,128)S(1)} %collective-permute-done.x_near, f32[16,3072]{1,0:T(8,128)} %collective-permute-done.1.x_far), custom_call_target="tpu_custom_call" | custom-call | bytes 3000000 | tf_op jit(solution)/shard_map/pallas_call | solution.py:582
  16.7 0.4 collective-permute-start.2
  17.1 3.1 %collective-permute-start.3 = (f32[424,128]{1,0:T(8,128)}, f32[424,128]{1,0:T(8,128)}, u32[]{:S(2)}, u32[]{:S(2)}) collective-permute-start(f32[424,128]{1,0:T(8,128)} %get-tuple-element.31), channel_id=1, source_target_pairs={{1,2},{3,4},{5,6},{2,1},{4,3},{6,5},{9,10},{11,12},{13,14},{10,9},... | collective-permute-start | bytes 651272 | tf_op jit(solution)/shard_map/ppermute | solution.py:557
  20.2 0.0 all-to-all-done.slots
  20.2 0.0 collective-permute-done.2.y_near
  20.2 4.4 %collective-permute-done.3.y_far = f32[424,128]{1,0:T(8,128)} collective-permute-done((f32[424,128]{1,0:T(8,128)}, f32[424,128]{1,0:T(8,128)}, u32[]{:S(2)}, u32[]{:S(2)}) %collective-permute-start.3) | collective-permute-done | bytes 217120 | tf_op jit(solution)/shard_map/ppermute | solution.py:557
  24.6 25.1 %shard_map.58 = (f32[3,32,128]{2,1,0:T(8,128)S(1)}, f32[32,8,128]{2,1,0:T(8,128)S(1)}, f32[3,42,48,128]{3,2,1,0:T(8,128)S(1)}, f32[3,42,48,128]{3,2,1,0:T(8,128)S(1)}, f32[3,42,48,128]{3,2,1,0:T(8,128)S(1)}) custom-call(f32[3,42,48,128]{3,2,1,0:T(8,128)S(1)} %get-tuple-element.25.wide, f32[16,3072]{1,0:T(8,128)S(1)} %collective-permute-done.x_near, ...), custom_call_target="tpu_custom_call" | custom-call | bytes 3000000 | tf_op jit(solution)/shard_map/pallas_call | solution.py:591
  49.7 12.5 %all_to_all.10.sums = f32[32,8,128]{2,1,0:T(8,128)S(1)} all-to-all(f32[32,8,128]{2,1,0:T(8,128)S(1)} %get-tuple-element.33), channel_id=1, replica_groups=mesh['gx'=4,'gy'=8] {'gx','gy'}, dimensions={0} | all-to-all | bytes 262144 | tf_op jit(solution)/shard_map/all_to_all | solution.py:600
  62.2 10.6 %shard_map.59 = (f32[9,2,32,8,128]{4,3,2,1,0:T(8,128)S(1)}, f32[9,32,128]{2,1,0:T(8,128)S(1)}, f32[18,24,128]{2,1,0:T(8,128)S(1)}, f32[18,24,128]{2,1,0:T(8,128)S(1)}) custom-call(f32[32,8,128]{2,1,0:T(8,128)S(1)} %all-to-all-done.slots, f32[3,32,128]{2,1,0:T(8,128)S(1)} %get-tuple-element.32.seen, f32[32,8,128]{2,1,0:T(8,128)S(1)} %all_to_all.10.sums), custom_call_target="tpu_custom_call" | custom-call | bytes 3000000 | tf_op jit(solution)/shard_map/pallas_call | solution.py:604
  72.8 0.4 collective-permute-start.4
  73.2 4.0 %collective-permute-start.5 = (f32[18,24,128]{2,1,0:T(8,128)S(1)}, f32[18,24,128]{2,1,0:T(8,128)S(1)}, u32[]{:S(2)}, u32[]{:S(2)}) collective-permute-start(f32[18,24,128]{2,1,0:T(8,128)S(1)} %get-tuple-element.37), channel_id=1, source_target_pairs={{8,16},{16,8},{9,17},{17,9},{10,18},{18,10},{11,19},{19,11},{12,20... | collective-permute-start | bytes 663560 | tf_op jit(solution)/shard_map/ppermute | solution.py:557
  77.1 9.9 %shard_map.60.inner = f32[9,2,32,8,128]{4,3,2,1,0:T(8,128)S(1)} custom-call(f32[32,8,128]{2,1,0:T(8,128)S(1)} %all-to-all-done.slots, f32[9,32,128]{2,1,0:T(8,128)S(1)} %get-tuple-element.35.weight), custom_call_target="tpu_custom_call" | custom-call | bytes 27000000 | tf_op jit(solution)/shard_map/pallas_call | solution.py:612
  87.1 0.0 collective-permute-done.4.x_near
  87.1 0.0 collective-permute-done.5.x_far
  87.1 0.3 shard_map.61
  87.3 0.8 collective-permute-start.6
  88.2 2.1 %collective-permute-start.7 = (f32[456,128]{1,0:T(8,128)S(1)}, f32[456,128]{1,0:T(8,128)S(1)}, u32[]{:S(2)}, u32[]{:S(2)}) collective-permute-start(f32[456,128]{1,0:T(8,128)S(1)} %get-tuple-element.39), channel_id=1, source_target_pairs={{1,2},{3,4},{5,6},{2,1},{4,3},{6,5},{9,10},{11,12},{13,14},{10,9},... | collective-permute-start | bytes 700424 | tf_op jit(solution)/shard_map/ppermute | solution.py:557
  90.3 0.0 collective-permute-done.6.y_near
  90.3 5.3 %collective-permute-done.7.y_far = f32[456,128]{1,0:T(8,128)S(1)} collective-permute-done((f32[456,128]{1,0:T(8,128)S(1)}, f32[456,128]{1,0:T(8,128)S(1)}, u32[]{:S(2)}, u32[]{:S(2)}) %collective-permute-start.7) | collective-permute-done | bytes 233504 | tf_op jit(solution)/shard_map/ppermute | solution.py:557
  95.5 10.3 %shard_map.62 = f32[3,32,3072]{2,1,0:T(8,128)} custom-call(f32[9,2,32,8,128]{4,3,2,1,0:T(8,128)S(1)} %get-tuple-element.34.outer, f32[9,2,32,8,128]{4,3,2,1,0:T(8,128)S(1)} %shard_map.60.inner, f32[18,24,128]{2,1,0:T(8,128)S(1)} %collective-permute-done.4.x_near, f32[18,24,128]{2,1,0:T(8,128)S(1)} %collective-permute-done.5.x_far, ...), custom_call_target="tpu_custom_call" | custom-call | bytes 3000000 | tf_op jit(solution)/shard_map/pallas_call | solution.py:621
Async XLA Ops:
  2.4 12.4 %collective-permute-start = (f32[16,3072]{1,0:T(8,128)}, f32[16,3072]{1,0:T(8,128)S(1)}, u32[]{:S(2)}, u32[]{:S(2)}) collective-permute-start(f32[16,3072]{1,0:T(8,128)} %get-tuple-element.26), channel_id=1, source_target_pairs={{0,8},{16,24},{8,0},{24,16},{1,9},{17,25},{9,1},{25,17},{2,10},{18... | collective-permute-start | bytes 589832 | tf_op jit(solution)/shard_map/ppermute | solution.py:557
  3.6 11.2 %collective-permute-start.1 = (f32[16,3072]{1,0:T(8,128)}, f32[16,3072]{1,0:T(8,128)}, u32[]{:S(2)}, u32[]{:S(2)}) collective-permute-start(f32[16,3072]{1,0:T(8,128)} %get-tuple-element.27), channel_id=1, source_target_pairs={{8,16},{16,8},{9,17},{17,9},{10,18},{18,10},{11,19},{19,11},{12,20... | collective-permute-start | bytes 589832 | tf_op jit(solution)/shard_map/ppermute | solution.py:557
  5.5 14.7 %all-to-all-start = ((f32[32,8,128]{2,1,0:T(8,128)}), f32[32,8,128]{2,1,0:T(8,128)S(1)}, u32[]{:S(2)}, u32[]{:S(2)}) async-start(f32[32,8,128]{2,1,0:T(8,128)} %get-tuple-element.24), calls=%async_computation | async-start | bytes 262144 | tf_op jit(solution)/shard_map/all_to_all | solution.py:575
  12.7 1.3 %copy-start = (f32[3,32,3072]{2,1,0:T(8,128)S(1)}, f32[3,32,3072]{2,1,0:T(8,128)}, u32[]{:S(2)}) copy-start(f32[3,32,3072]{2,1,0:T(8,128)} %state.3) | copy-start | bytes 3538948
  16.7 3.5 %collective-permute-start.2 = (f32[424,128]{1,0:T(8,128)}, f32[424,128]{1,0:T(8,128)}, u32[]{:S(2)}, u32[]{:S(2)}) collective-permute-start(f32[424,128]{1,0:T(8,128)} %get-tuple-element.30), channel_id=1, source_target_pairs={{0,1},{2,3},{4,5},{6,7},{1,0},{3,2},{5,4},{7,6},{8,9},{10,11},{12,... | collective-permute-start | bytes 651272 | tf_op jit(solution)/shard_map/ppermute | solution.py:557
  17.1 7.5 %collective-permute-start.3 = (f32[424,128]{1,0:T(8,128)}, f32[424,128]{1,0:T(8,128)}, u32[]{:S(2)}, u32[]{:S(2)}) collective-permute-start(f32[424,128]{1,0:T(8,128)} %get-tuple-element.31), channel_id=1, source_target_pairs={{1,2},{3,4},{5,6},{2,1},{4,3},{6,5},{9,10},{11,12},{13,14},{10,9},... | collective-permute-start | bytes 651272 | tf_op jit(solution)/shard_map/ppermute | solution.py:557
  72.8 14.3 %collective-permute-start.4 = (f32[18,24,128]{2,1,0:T(8,128)S(1)}, f32[18,24,128]{2,1,0:T(8,128)S(1)}, u32[]{:S(2)}, u32[]{:S(2)}) collective-permute-start(f32[18,24,128]{2,1,0:T(8,128)S(1)} %get-tuple-element.36), channel_id=1, source_target_pairs={{0,8},{16,24},{8,0},{24,16},{1,9},{17,25},{9,1},{25,17},{2,10},{18... | collective-permute-start | bytes 663560 | tf_op jit(solution)/shard_map/ppermute | solution.py:557
  73.2 13.9 %collective-permute-start.5 = (f32[18,24,128]{2,1,0:T(8,128)S(1)}, f32[18,24,128]{2,1,0:T(8,128)S(1)}, u32[]{:S(2)}, u32[]{:S(2)}) collective-permute-start(f32[18,24,128]{2,1,0:T(8,128)S(1)} %get-tuple-element.37), channel_id=1, source_target_pairs={{8,16},{16,8},{9,17},{17,9},{10,18},{18,10},{11,19},{19,11},{12,20... | collective-permute-start | bytes 663560 | tf_op jit(solution)/shard_map/ppermute | solution.py:557
  87.3 2.9 %collective-permute-start.6 = (f32[456,128]{1,0:T(8,128)S(1)}, f32[456,128]{1,0:T(8,128)S(1)}, u32[]{:S(2)}, u32[]{:S(2)}) collective-permute-start(f32[456,128]{1,0:T(8,128)S(1)} %get-tuple-element.38), channel_id=1, source_target_pairs={{0,1},{2,3},{4,5},{6,7},{1,0},{3,2},{5,4},{7,6},{8,9},{10,11},{12,... | collective-permute-start | bytes 700424 | tf_op jit(solution)/shard_map/ppermute | solution.py:557
  88.2 7.4 %collective-permute-start.7 = (f32[456,128]{1,0:T(8,128)S(1)}, f32[456,128]{1,0:T(8,128)S(1)}, u32[]{:S(2)}, u32[]{:S(2)}) collective-permute-start(f32[456,128]{1,0:T(8,128)S(1)} %get-tuple-element.39), channel_id=1, source_target_pairs={{1,2},{3,4},{5,6},{2,1},{4,3},{6,5},{9,10},{11,12},{13,14},{10,9},... | collective-permute-start | bytes 700424 | tf_op jit(solution)/shard_map/ppermute | solution.py:557

commit v4 on v3

--- a/solution.py
+++ b/solution.py
@@ -26,24 +26,27 @@
 ROWS = 8
 GROUPS = CX // ROWS
 GROUP = ROWS * CY
-BLOCK = 512
+BLOCK = 256
+BLOCK_ROWS = BLOCK // LANES
+TOGETHER = 4
+WORK = 128
 F32 = jnp.float32
 BF16 = jnp.bfloat16
 AXES = ("gx", "gy")
 MIB = 1024 * 1024
 
 
-def call(kernel, outs, scratch=(), limit=12, far_in=(), ins=0, far_out=(), micros=1):
-    def specs(count, far):
-        spaces = [pl.ANY if i in far else pltpu.VMEM for i in range(count)]
+def call(kernel, outs, scratch=(), limit=12, ins=0, scalar_in=(), scalar_out=(), micros=1):
+    def specs(count, scalar):
+        spaces = [pltpu.SMEM if i in scalar else pltpu.VMEM for i in range(count)]
         return [pl.BlockSpec(memory_space=space) for space in spaces]
 
     single = not isinstance(outs, tuple)
-    out_specs = specs(1 if single else len(outs), far_out)
+    out_specs = specs(1 if single else len(outs), scalar_out)
     return pl.pallas_call(
         kernel,
         out_shape=outs,
-        in_specs=specs(ins, far_in),
+        in_specs=specs(ins, scalar_in),
         out_specs=out_specs[0] if single else tuple(out_specs),
         scratch_shapes=list(scratch),
         compiler_params=pltpu.CompilerParams(vmem_limit_bytes=limit * MIB),
@@ -118,32 +121,103 @@
 FORCE_PIECE = len(FORCE_BLOCKS) * PACKED + 24
 
 
-def prepare_kernel(state, beam_dir, obs, beam, cell, slots, near, far, first_rows, last_rows):
+def state_rows_kernel(state, near, far, first_rows, last_rows):
     for c in range(3):
         first_rows[RIM * c : RIM * c + RIM, :] = state[c, 0:RIM, :]
         last_rows[RIM * c : RIM * c + RIM, :] = state[c, CX - RIM : CX, :]
     first_rows[3 * RIM : 16, :] = jnp.zeros((1, CY * NZ), F32)
     last_rows[3 * RIM : 16, :] = jnp.zeros((1, CY * NZ), F32)
     to_partners("gx", first_rows, last_rows, near, far)
+
+
+def arrange_kernel(beam_dir, obs, beam, cell, slots, values, places):
     beams = beam_dir.shape[1]
     owned = beam[0]
+    lists, capacity = owned.shape
     used = owned >= 0
     masks = [owned == k for k in range(beams)]
 
-    def spread(values):
+    def spread(parts):
         total = jnp.zeros(owned.shape, F32)
         for k in range(beams):
-            total = jnp.where(masks[k], values[k], total)
+            total = jnp.where(masks[k], parts[k], total)
         return total
 
-    slots[:, 0, :] = cell[0].astype(F32)
-    slots[:, 1, :] = owned.astype(F32)
+    cells = cell[0].astype(F32)
+    values[:, 0, :] = cells + 1.0
+    values[:, 1, :] = owned.astype(F32)
     for n in range(STEPS):
         seen = obs[n, 0]
         means = [jnp.sum(jnp.where(m, seen, 0.0), keepdims=True) / GATES for m in masks]
-        slots[:, 2 + n, :] = jnp.where(used, seen - spread(means), 0.0)
+        values[:, 2 + n, :] = jnp.where(used, seen - spread(means), 0.0)
     for c in range(3):
-        slots[:, 5 + c, :] = spread([beam_dir[c : c + 1, k : k + 1] for k in range(beams)])
+        values[:, 5 + c, :] = spread([beam_dir[c : c + 1, k : k + 1] for k in range(beams)])
+
+    group = ((cells + 0.5) * (1.0 / (GROUP * NZ))).astype(jnp.int32)
+    row = lax.broadcasted_iota(jnp.int32, (capacity, capacity), 0)
+    column = lax.broadcasted_iota(jnp.int32, (capacity, capacity), 1)
+    ahead = jnp.where(row <= column, 1.0, 0.0).astype(BF16)
+    ones = [jnp.where(used & (group == g), 1.0, 0.0) for g in range(GROUPS)]
+    counts = [jnp.sum(o, axis=1, keepdims=True) for o in ones]
+    place = jnp.full(owned.shape, -1.0, F32)
+    end = jnp.zeros((lists, 1), F32)
+    left = counts[0] + counts[1] + counts[2] + counts[3]
+    for g in range(GROUPS):
+        start = jnp.minimum(jnp.maximum(float(capacity // GROUPS * g), end), capacity - left)
+        upto = jnp.dot(ones[g].astype(BF16), ahead, preferred_element_type=F32)
+        place = jnp.where(ones[g] > 0.5, start + upto - 1.0, place)
+        end = start + counts[g]
+        left = left - counts[g]
+    places[...] = place.astype(jnp.int32)
+
+    def move(i, carry):
+        full = values[i]
+        high = full.astype(BF16).astype(F32)
+        mid = (full - high).astype(BF16).astype(F32)
+        low = full - high - mid
+        three = jnp.concatenate([high, mid, low], axis=0).astype(BF16)
+        hits = jnp.where(row == places[pl.ds(i, 1), :], 1.0, 0.0).astype(BF16)
+        moved = lax.dot_general(three, hits, (((1,), (1,)), ((), ())), preferred_element_type=F32)
+        slots[i] = moved[0:8] + moved[8:16] + moved[16:24]
+        return carry
+
+    lax.fori_loop(0, lists, move, 0, unroll=8)
+
+
+def regroup_kernel(received, slots, every_work, outer_work, inner_work, turned):
+    owners, _, capacity = received.shape
+    apart = LANES // owners
+    rows = capacity // apart
+    for j in range(8):
+        lists = received[:, j, :]
+        if capacity < LANES:
+            lists = jnp.concatenate([lists, jnp.zeros((owners, LANES - capacity), F32)], axis=1)
+        if owners < LANES:
+            lists = jnp.concatenate([lists, jnp.zeros((LANES - owners, LANES), F32)], axis=0)
+        turned[...] = lists.T
+        line = turned[pl.ds(0, rows, stride=apart), :]
+        for k in range(1, apart):
+            line = line + pltpu.roll(turned[pl.ds(k, rows, stride=apart), :], k * owners, axis=1)
+        slots[:, j, :] = line
+    cell = slots[:, 0, :]
+    group = ((cell - 0.5) * (1.0 / (GROUP * NZ))).astype(jnp.int32).astype(F32)
+    low = jnp.where(cell > 0.5, group, float(GROUPS))
+    high = jnp.where(cell > 0.5, group, -1.0)
+    counts = [jnp.int32(0)] * 3
+    works = (every_work, outer_work, inner_work)
+    for block in range(rows // BLOCK_ROWS):
+        span = slice(block * BLOCK_ROWS, block * BLOCK_ROWS + BLOCK_ROWS)
+        first = jnp.min(low[span]).astype(jnp.int32)
+        last = jnp.max(high[span]).astype(jnp.int32)
+        for g in range(GROUPS):
+            hit = ((first <= g) & (last >= g)).astype(jnp.int32)
+            for w in (0, 1 if g in (0, GROUPS - 1) else 2):
+                works[w][counts[w]] = block * GROUPS + g
+                counts[w] = counts[w] + hit
+    for w in range(3):
+        for k in range(TOGETHER):
+            works[w][counts[w] + k] = 0
+        works[w][WORK - 1] = counts[w]
 
 
 def layout_kernel(state, wide, first_layers, last_layers):
@@ -237,7 +311,7 @@
 
 
 def slot_columns(slots, row):
-    cell = slots[row, 0:1, :]
+    cell = slots[row, 0:1, :] - 1.0
     x = ((cell + 0.5) * (1.0 / (CY * NZ))).astype(jnp.int32)
     rest = cell.astype(jnp.int32) - x * (CY * NZ)
     y = ((rest.astype(F32) + 0.5) * (1.0 / NZ)).astype(jnp.int32)
@@ -245,13 +319,13 @@
     return high * (GROUP - ROWS) + y * ROWS + x, rest - y * NZ
 
 
-def column_hits(columns, count=COLUMNS):
-    place = lax.broadcasted_iota(jnp.int32, (count, columns.shape[1]), 0)
+def column_hits(columns):
+    place = lax.broadcasted_iota(jnp.int32, (GROUP, columns.shape[1]), 0)
     return jnp.where(place == columns, 1.0, 0.0).astype(BF16)
 
 
 def block_places(slots, block):
-    rows = [slot_columns(slots, block * (BLOCK // LANES) + r) for r in range(BLOCK // LANES)]
+    rows = [slot_columns(slots, block * BLOCK_ROWS + r) for r in range(BLOCK_ROWS)]
     columns = jnp.concatenate([r[0] for r in rows], axis=1)
     level = jnp.concatenate([r[1] for r in rows], axis=1)
     here = lax.broadcasted_iota(jnp.int32, (NZ, BLOCK), 0) == level
@@ -259,13 +333,36 @@
 
 
 def block_values(slots, block, which):
-    rows = [slots[block * (BLOCK // LANES) + r, which : which + 1, :] for r in range(BLOCK // LANES)]
+    rows = [slots[block * BLOCK_ROWS + r, which : which + 1, :] for r in range(BLOCK_ROWS)]
     return jnp.concatenate(rows, axis=1)
+
+
+def each_product(work, together, body):
+    count = work[WORK - 1]
+
+    def some(i, carry):
+        for k in range(together):
+            item = i * together + k
+            code = work[item]
+            group = code & (GROUPS - 1)
+            offset = jnp.where(item < count, group * GROUP, -(1 << 20))
+            body(lax.shift_right_logical(code, GROUPS // 2), group, offset)
+        return carry
+
+    lax.fori_loop(0, lax.shift_right_logical(count + together - 1, together // 2), some, 0)
+
+
+def fold(owners, line):
+    reach = LANES // 2
+    while reach >= owners:
+        line = line + pltpu.roll(line, reach, axis=1)
+        reach //= 2
+    return line
 
 
 def forward_kernel(
     beams,
-    per_row,
+    work,
     wide,
     x_near,
     x_far,
@@ -318,13 +415,14 @@
                 rows = field[c, RIM : RIM + CY, PAD + ROWS * g : PAD + ROWS * g + ROWS, :]
                 turned = rows.reshape(GROUP, LANES).T[0:NZ]
                 high = turned.astype(BF16)
-                span = slice(GROUP * g, GROUP * g + GROUP)
-                table[base : base + NZ, span] = high
-                table[half + base : half + base + NZ, span] = (turned - high.astype(F32)).astype(BF16)
-
-    def gather(block, carry):
+                table[g, base : base + NZ, :] = high
+                table[g, half + base : half + base + NZ, :] = (turned - high.astype(F32)).astype(BF16)
+
+    seen[...] = jnp.zeros(seen.shape, F32)
+
+    def gather(block, group, offset):
         columns, here = block_places(slots, block)
-        found = jnp.dot(table[...], column_hits(columns), preferred_element_type=F32)
+        found = jnp.dot(table[group], column_hits(columns - offset), preferred_element_type=F32)
         weights = [block_values(slots, block, 5 + c) for c in range(3)]
         for n in range(STEPS):
             total = jnp.zeros((1, BLOCK), F32)
@@ -333,92 +431,73 @@
                 both = found[base : base + NZ] + found[half + base : half + base + NZ]
                 value = jnp.sum(jnp.where(here, both, 0.0), axis=0, keepdims=True)
                 total = total + weights[c] * value
-            for r in range(BLOCK // LANES):
-                seen[n, pl.ds(block * (BLOCK // LANES) + r, 1), :] = total[:, LANES * r : LANES * r + LANES]
-        return carry
-
-    rows = slots.shape[0]
-    lax.fori_loop(0, rows * LANES // BLOCK, gather, 0)
-
-    beam = row_beam(beams, per_row, slots)
-    lane = lax.broadcasted_iota(jnp.int32, (rows, LANES), 1)
-    partial = jnp.zeros((rows, LANES), F32)
+            for r in range(BLOCK_ROWS):
+                seen[n, pl.ds(block * BLOCK_ROWS + r, 1), :] += total[:, LANES * r : LANES * r + LANES]
+
+    each_product(work, TOGETHER, gather)
+
+    owners = sums.shape[0]
+    apart = LANES // owners
+    beam = slots[:, 1, :].astype(jnp.int32)
+    lane = lax.broadcasted_iota(jnp.int32, (1, LANES), 1)
+    lines = [jnp.zeros((1, LANES), F32)] * (STEPS * beams // apart)
     for n in range(STEPS):
-        values = seen[n]
-        for k in range(per_row):
-            one = jnp.sum(jnp.where(beam == k, values, 0.0), axis=1, keepdims=True)
-            partial = jnp.where(lane == n * per_row + k, one, partial)
-    turned = jnp.concatenate([partial, jnp.zeros((LANES - rows, LANES), F32)], axis=0).T
-    per_line = LANES // rows
+        for k in range(beams):
+            one = fold(owners, jnp.sum(jnp.where(beam == k, seen[n], 0.0), axis=0, keepdims=True))
+            line, place = divmod(n * beams + k, apart)
+            here = (lane >= place * owners) & (lane < place * owners + owners)
+            lines[line] = jnp.where(here, one, lines[line])
     sums[...] = jnp.zeros(sums.shape, F32)
-    for line in range(STEPS * per_row // per_line):
-        total = turned[line * per_line : line * per_line + 1]
-        for k in range(1, per_line):
-            one = turned[line * per_line + k : line * per_line + k + 1]
-            total = total + pltpu.roll(one, rows * k, axis=1)
-        sums[:, line : line + 1, :] = jnp.broadcast_to(total[None], (sums.shape[0], 1, LANES))
-
-
-def row_beam(beams, per_row, slots):
-    group = per_row // beams
-    lane = lax.broadcasted_iota(jnp.int32, (slots.shape[0], LANES), 1)
-    beam = slots[:, 1, :].astype(jnp.int32)
-    for g in range(1, group):
-        beam = beam + jnp.where(lane >= g * (LANES // group), beams, 0)
-    return beam
-
-
-def scatter_slots(groups, slots, weight, total, force):
+    for line, total in enumerate(lines):
+        sums[:, line : line + 1, :] = jnp.broadcast_to(total[None], (owners, 1, LANES))
+
+
+def scatter_slots(part_of, together, work, slots, weight, total, force):
     total[...] = jnp.zeros(total.shape, F32)
-
-    def scatter(block, carry):
+    half = FIELDS * NZ
+
+    def scatter(block, group, offset):
         columns, here = block_places(slots, block)
-        hits = jnp.concatenate([column_hits(columns - GROUP * g, GROUP) for g in groups], axis=0)
         high_rows, low_rows = [], []
         for f in range(FIELDS):
             value = jnp.concatenate(
-                [weight[f, pl.ds(block * (BLOCK // LANES) + r, 1), :] for r in range(BLOCK // LANES)],
-                axis=1,
+                [weight[f, pl.ds(block * BLOCK_ROWS + r, 1), :] for r in range(BLOCK_ROWS)], axis=1
             )
             high = value.astype(BF16).astype(F32)
             high_rows.append(jnp.where(here, high, 0.0).astype(BF16))
             low_rows.append(jnp.where(here, value - high, 0.0).astype(BF16))
         table = jnp.concatenate(high_rows + low_rows, axis=0)
+        hits = column_hits(columns - offset)
         added = lax.dot_general(table, hits, (((1,), (1,)), ((), ())), preferred_element_type=F32)
-        half = FIELDS * NZ
+        part = part_of(group)
         for f in range(FIELDS):
-            total[f, 0:NZ, :] += added[NZ * f : NZ * f + NZ] + added[half + NZ * f : half + NZ * f + NZ]
-        return carry
-
-    lax.fori_loop(0, slots.shape[0] * LANES // BLOCK, scatter, 0)
+            total[part, f, 0:NZ, :] += added[NZ * f : NZ * f + NZ] + added[half + NZ * f : half + NZ * f + NZ]
+
+    each_product(work, together, scatter)
     for f in range(FIELDS):
-        for k in range(len(groups)):
-            force[f, k] = total[f, :, GROUP * k : GROUP * k + GROUP].T.reshape(CY, ROWS, LANES)
+        for k in range(2):
+            force[f, k] = total[k, f].T.reshape(CY, ROWS, LANES)
 
 
 def outer_force_kernel(
-    beams, per_row, slots, seen, sums, force, weight, near, far, first_rows, last_rows, total
+    beams, work, slots, seen, sums, force, weight, near, far, first_rows, last_rows, total
 ):
-    rows = slots.shape[0]
-    per_line = LANES // rows
+    owners = sums.shape[0]
+    apart = LANES // owners
     lines = jnp.sum(sums[...], axis=0) / GATES
-    count = STEPS * per_row
-    spread = []
-    for k in range(count):
-        line = lines[k // per_line : k // per_line + 1]
-        spread.append(pltpu.roll(line, (-rows * (k % per_line)) % LANES, axis=1))
-    spread.append(jnp.zeros((LANES - count, LANES), F32))
-    means = jnp.concatenate(spread, axis=0).T[0:rows]
-    beam = row_beam(beams, per_row, slots)
+    beam = slots[:, 1, :].astype(jnp.int32)
+    lane = lax.broadcasted_iota(jnp.int32, (1, LANES), 1)
     for n in range(STEPS):
-        mean = jnp.zeros((rows, LANES), F32)
-        for k in range(per_row):
-            one = means[:, n * per_row + k : n * per_row + k + 1]
+        mean = jnp.zeros(beam.shape, F32)
+        for k in range(beams):
+            line, place = divmod(n * beams + k, apart)
+            here = (lane >= place * owners) & (lane < place * owners + owners)
+            one = fold(owners, jnp.where(here, lines[line : line + 1], 0.0))
             mean = jnp.where(beam == k, one, mean)
         misfit = seen[n] - mean - slots[:, 2 + n, :]
         for c in range(3):
             weight[3 * n + c] = slots[:, 5 + c, :] * misfit
-    scatter_slots((0, GROUPS - 1), slots, weight, total, force)
+    scatter_slots(lambda g: (g == GROUPS - 1).astype(jnp.int32), 2, work, slots, weight, total, force)
     for out, k, row_of in ((first_rows, 0, lambda i: i), (last_rows, 1, lambda i: ROWS - 1 - i)):
         for b, (n, c, i) in enumerate(FORCE_BLOCKS):
 
@@ -429,8 +508,8 @@
     to_partners("gx", first_rows, last_rows, near, far)
 
 
-def inner_force_kernel(slots, weight, force, total):
-    scatter_slots((1, 2), slots, weight, total, force)
+def inner_force_kernel(work, slots, weight, force, total):
+    scatter_slots(lambda g: (g == 2).astype(jnp.int32), TOGETHER, work, slots, weight, total, force)
 
 
 def force_rim_kernel(outer, inner, x_near, x_far, near, far, first_layers, last_layers, before, after):
@@ -559,22 +638,31 @@
 
 def local(initial_state, beam_dir, gate_obs, slot_beam, slot_cell):
     peers, capacity = slot_beam.shape[1:]
-    group = LANES // capacity
     beams = beam_dir.shape[1]
-    per_row = group * beams
-    rows = peers // group
+    rows = peers * capacity // LANES
     x_rim = (16, CY * NZ)
-    slots, near, far = call(
-        prepare_kernel,
-        (shape(peers, 8, capacity), shape(*x_rim), shape(*x_rim)),
-        [pltpu.VMEM(x_rim, F32)] * 2,
+    near, far = call(
+        state_rows_kernel, (shape(*x_rim), shape(*x_rim)), [pltpu.VMEM(x_rim, F32)] * 2, limit=60, ins=1
+    )(initial_state)
+    x_near, x_far = swap(near, far, "gx")
+    lists = (peers, 8, capacity)
+    slots = call(
+        arrange_kernel,
+        shape(*lists),
+        [pltpu.VMEM(lists, F32), pltpu.VMEM((peers, capacity), jnp.int32)],
         limit=60,
-        ins=5,
-    )(initial_state, beam_dir, gate_obs, slot_beam, slot_cell)
-    x_near, x_far = swap(near, far, "gx")
+        ins=4,
+    )(beam_dir, gate_obs, slot_beam, slot_cell)
     slots = lax.all_to_all(slots, AXES, split_axis=0, concat_axis=0, tiled=True)
-    if group > 1:
-        slots = slots.reshape(rows, group, 8, capacity).transpose(0, 2, 1, 3).reshape(rows, 8, LANES)
+    work = jax.ShapeDtypeStruct((WORK,), jnp.int32)
+    slots, every_work, outer_work, inner_work = call(
+        regroup_kernel,
+        (shape(rows, 8, LANES), work, work, work),
+        [pltpu.VMEM((LANES, LANES), F32)],
+        ins=1,
+        scalar_out=(1, 2, 3),
+        micros=2,
+    )(slots)
     field = shape(3, YH, XH, LANES)
     bulk = shape(3 * RIM * PACKED, LANES)
     wide, bulk_first, bulk_last = call(layout_kernel, (field, bulk, bulk), ins=1, micros=2)(initial_state)
@@ -586,30 +674,34 @@
         ins=4,
     )(bulk_first, bulk_last, x_near, x_far)
     y_near, y_far = swap(near, far, "gy")
-    lines = -(-STEPS * per_row * rows // LANES // 8) * 8
+    lines = -(-STEPS * beams * peers // LANES // 8) * 8
     mask = pltpu.VMEM((XH, LANES), F32)
     seen, sums, s0, s1, s2 = call(
-        functools.partial(forward_kernel, beams, per_row),
+        functools.partial(forward_kernel, beams),
         (shape(STEPS, rows, LANES), shape(peers, lines, LANES), field, field, field),
-        [pltpu.VMEM(field.shape, F32), pltpu.VMEM((2 * FIELDS * NZ, COLUMNS), BF16), mask]
+        [pltpu.VMEM(field.shape, F32), pltpu.VMEM((GROUPS, 2 * FIELDS * NZ, GROUP), BF16), mask]
         + [pltpu.VMEM(y_rim, F32)] * 2
         + [pltpu.VMEM(x_rim, F32)] * 2,
         limit=32,
-        ins=6,
-    )(wide, x_near, x_far, y_near, y_far, slots)
+        ins=7,
+        scalar_in=(0,),
+    )(every_work, wide, x_near, x_far, y_near, y_far, slots)
     sums = lax.all_to_all(sums, AXES, split_axis=0, concat_axis=0, tiled=True)
     x_rim = (len(FORCE_BLOCKS), PACKED, LANES)
     part = shape(FIELDS, 2, CY, ROWS, LANES)
-    total = pltpu.VMEM((FIELDS, LANES, 2 * GROUP), F32)
+    total = pltpu.VMEM((2, FIELDS, LANES, GROUP), F32)
     outer, weight, near, far = call(
-        functools.partial(outer_force_kernel, beams, per_row),
+        functools.partial(outer_force_kernel, beams),
         (part, shape(FIELDS, rows, LANES), shape(*x_rim), shape(*x_rim)),
         [pltpu.VMEM(x_rim, F32)] * 2 + [total],
         limit=24,
-        ins=3,
-    )(slots, seen, sums)
+        ins=4,
+        scalar_in=(0,),
+    )(outer_work, slots, seen, sums)
     x_near, x_far = swap(near, far, "gx")
-    inner = call(inner_force_kernel, part, [total], limit=24, ins=2, micros=9)(slots, weight)
+    inner = call(inner_force_kernel, part, [total], limit=24, ins=3, scalar_in=(0,), micros=6)(
+        inner_work, slots, weight
+    )
     y_rim = (FORCE_PIECE, LANES)
     near, far = call(
         force_rim_kernel,

time: 106 us -> 93.7 us (0.88)
  Pallas kernels: 61.2 us -> 49.1 us
  waiting for transfers between devices: 9.64 us -> 7.65 us
  starting transfers between devices: 21.1 us -> 22.3 us
    pallas_call x4 -> x6, Pallas kernels: 47.9 us -> 36.8 us  [the longest x1 15.5 us: local(): call(functools.partial(forward_kernel, beams), (shape(STEPS, rows, LANES)...]
    ppermute x4, waiting for transfers between devices: 9.62 us -> 7.02 us  [swap(): lax.ppermute(far, axis, pairs(1))]
    ppermute x4, starting transfers between devices: 2.8 us -> 4.16 us  [swap(): lax.ppermute(near, axis, pairs(0))]
  transfers between devices with their start and end apart: 9 -> 9, of which waited for: 2 -> 3; matrix products, arithmetic and copies ran while one was open for 0% -> 0% of each run, Pallas kernels for 12% -> 15%
where the time goes in v4:
time: 93.7 us; the launch traced here: 93 us
  Pallas kernels  49.1 us (52%)
  starting transfers between devices  22.3 us (24%)
  blocking collectives  12.5 us (13%)
  waiting for transfers between devices  7.65 us (8%)
  local copies, waits for them, and re-layouts  1.27 us (1%)
    pallas_call x1, Pallas kernels, local(): call(functools.partial(forward_kernel, beams), (shape(STEPS, rows, LANES)...  15.5 us
    all_to_all x1, blocking collectives, local(): sums = lax.all_to_all(sums, AXES, split_axis=0, concat_axis=0, tiled=True)  12.5 us
    ppermute x4, starting transfers between devices, swap(): lax.ppermute(far, axis, pairs(1))  10.9 us
    pallas_call x1, Pallas kernels, local(): call(backward_kernel, shape(*initial_state.shape), [pltpu.VMEM((3, FH, XH...  10.3 us
    all_to_all x1, starting transfers between devices, local(): slots = lax.all_to_all(slots, AXES, split_axis=0, concat_axis=0, tiled=True)  7.27 us
    pallas_call x1, Pallas kernels, local(): call(functools.partial(outer_force_kernel, beams), (part, shape(FIELDS, r...  7.21 us
    pallas_call x1, Pallas kernels, local(): call(inner_force_kernel, part, [total], limit=24, ins=3, scalar_in=(0,),...  7.07 us
    ppermute x4, waiting for transfers between devices, swap(): lax.ppermute(far, axis, pairs(1))  7.02 us
  transfers between devices with their start and end apart: 9, of which 3 were waited for; matrix products, arithmetic and copies ran while one was open for 0% of the time, Pallas kernels for 15%

profile of v4, /device:TPU:5, one launch (start us, length us, event | category | flops | bytes accessed | tf_op | source)
XLA Modules:
  0.0 93.0 jit_solution(4105357720082842028)
XLA Ops:
  0.0 2.1 %shard_map.58 = (f32[16,3072]{1,0:T(8,128)}, f32[16,3072]{1,0:T(8,128)}) custom-call(f32[3,32,3072]{2,1,0:T(8,128)} %state.3), custom_call_target="tpu_custom_call" | custom-call | bytes 3000000 | tf_op jit(solution)/shard_map/pallas_call | solution.py:644
  2.1 1.2 %collective-permute-start = (f32[16,3072]{1,0:T(8,128)}, f32[16,3072]{1,0:T(8,128)S(1)}, u32[]{:S(2)}, u32[]{:S(2)}) collective-permute-start(f32[16,3072]{1,0:T(8,128)} %get-tuple-element.31), channel_id=1, source_target_pairs={{0,8},{16,24},{8,0},{24,16},{1,9},{17,25},{9,1},{25,17},{2,10},{18... | collective-permute-start | bytes 589832 | tf_op jit(solution)/shard_map/ppermute | solution.py:636
  3.3 1.9 %collective-permute-start.1 = (f32[16,3072]{1,0:T(8,128)}, f32[16,3072]{1,0:T(8,128)S(1)}, u32[]{:S(2)}, u32[]{:S(2)}) collective-permute-start(f32[16,3072]{1,0:T(8,128)} %get-tuple-element.32), channel_id=1, source_target_pairs={{8,16},{16,8},{9,17},{17,9},{10,18},{18,10},{11,19},{19,11},{12,20... | collective-permute-start | bytes 589832 | tf_op jit(solution)/shard_map/ppermute | solution.py:636
  5.2 2.7 %shard_map.55 = f32[32,8,128]{2,1,0:T(8,128)} custom-call(f32[3,4]{1,0:T(4,128)} %beam_dir.1, f32[3,1,32,128]{3,2,1,0:T(8,128)} %obs.1, s32[1,32,128]{2,1,0:T(8,128)} %beam.1, s32[1,32,128]{2,1,0:T(8,128)} %cell.1), custom_call_target="tpu_custom_call" | custom-call | bytes 3000000 | tf_op jit(solution)/shard_map/pallas_call | solution.py:649
  7.9 7.3 %all-to-all-start = ((f32[32,8,128]{2,1,0:T(8,128)}), f32[32,8,128]{2,1,0:T(8,128)}, u32[]{:S(2)}, u32[]{:S(2)}) async-start(f32[32,8,128]{2,1,0:T(8,128)} %shard_map.55), calls=%async_computation | async-start | bytes 262144 | tf_op jit(solution)/shard_map/all_to_all | solution.py:656
  15.2 0.0 copy-start
  15.2 1.3 %copy-done = f32[3,32,3072]{2,1,0:T(8,128)S(1)} copy-done((f32[3,32,3072]{2,1,0:T(8,128)S(1)}, f32[3,32,3072]{2,1,0:T(8,128)}, u32[]{:S(2)}) %copy-start) | copy-done | bytes 1179672
  16.5 0.8 shard_map.57
  17.3 0.0 collective-permute-done.x_near
  17.3 0.0 collective-permute-done.1.x_far
  17.3 0.9 %shard_map.59 = (f32[424,128]{1,0:T(8,128)}, f32[424,128]{1,0:T(8,128)}) custom-call(f32[360,128]{1,0:T(8,128)S(1)} %get-tuple-element.33.bulk_first, f32[360,128]{1,0:T(8,128)S(1)} %get-tuple-element.34.bulk_last, f32[16,3072]{1,0:T(8,128)S(1)} %collective-permute-done.x_near, f32[16,3072]{1,0:T(8,128)S(1)} %collective-permute-done.1.x_far), custom_call_target="tpu_custom_call" | custom-call | bytes 3000000 | tf_op jit(solution)/shard_map/pallas_call | solution.py:670
  18.3 0.4 collective-permute-start.2
  18.6 3.1 %collective-permute-start.3 = (f32[424,128]{1,0:T(8,128)}, f32[424,128]{1,0:T(8,128)}, u32[]{:S(2)}, u32[]{:S(2)}) collective-permute-start(f32[424,128]{1,0:T(8,128)} %get-tuple-element.36), channel_id=1, source_target_pairs={{1,2},{3,4},{5,6},{2,1},{4,3},{6,5},{9,10},{11,12},{13,14},{10,9},... | collective-permute-start | bytes 651272 | tf_op jit(solution)/shard_map/ppermute | solution.py:636
  21.7 0.6 all-to-all-done.received
  22.4 2.2 %shard_map.56 = (f32[32,8,128]{2,1,0:T(8,128)S(1)}, s32[128]{0:T(128)S(1)}, s32[128]{0:T(128)S(1)}, s32[128]{0:T(128)S(1)}) custom-call(f32[32,8,128]{2,1,0:T(8,128)} %all-to-all-done.received), custom_call_target="tpu_custom_call" | custom-call | bytes 6000000 | tf_op jit(solution)/shard_map/pallas_call | solution.py:658
  24.6 0.0 collective-permute-done.2.y_near
  24.6 1.6 %collective-permute-done.3.y_far = f32[424,128]{1,0:T(8,128)} collective-permute-done((f32[424,128]{1,0:T(8,128)}, f32[424,128]{1,0:T(8,128)}, u32[]{:S(2)}, u32[]{:S(2)}) %collective-permute-start.3) | collective-permute-done | bytes 217120 | tf_op jit(solution)/shard_map/ppermute | solution.py:636
  26.1 15.5 %shard_map.60 = (f32[3,32,128]{2,1,0:T(8,128)S(1)}, f32[32,8,128]{2,1,0:T(8,128)S(1)}, f32[3,42,48,128]{3,2,1,0:T(8,128)S(1)}, f32[3,42,48,128]{3,2,1,0:T(8,128)S(1)}, f32[3,42,48,128]{3,2,1,0:T(8,128)S(1)}) custom-call(s32[128]{0:T(128)S(1)} %get-tuple-element.29.work, f32[3,42,48,128]{3,2,1,0:T(8,128)S(1)} %get-tuple-element.30.wide, ...), custom_call_target="tpu_custom_call" | custom-call | bytes 3000000 | tf_op jit(solution)/shard_map/pallas_call | solution.py:679
  41.7 12.5 %all_to_all.10.sums = f32[32,8,128]{2,1,0:T(8,128)S(1)} all-to-all(f32[32,8,128]{2,1,0:T(8,128)S(1)} %get-tuple-element.38), channel_id=1, replica_groups=mesh['gx'=4,'gy'=8] {'gx','gy'}, dimensions={0} | all-to-all | bytes 262144 | tf_op jit(solution)/shard_map/all_to_all | solution.py:689
  54.2 7.2 %shard_map.61 = (f32[9,2,32,8,128]{4,3,2,1,0:T(8,128)S(1)}, f32[9,32,128]{2,1,0:T(8,128)S(1)}, f32[18,24,128]{2,1,0:T(8,128)S(1)}, f32[18,24,128]{2,1,0:T(8,128)S(1)}) custom-call(s32[128]{0:T(128)S(1)} %get-tuple-element.27.work, f32[32,8,128]{2,1,0:T(8,128)S(1)} %get-tuple-element.28.slots, f32[3,32,128]{2,1,0:T(8,128)S(1)} %get-tuple-element.37.seen, ...), custom_call_target="tpu_custom_call" | custom-call | bytes 3000000 | tf_op jit(solution)/shard_map/pallas_call | solution.py:693
  61.4 0.4 collective-permute-start.4
  61.8 3.9 %collective-permute-start.5 = (f32[18,24,128]{2,1,0:T(8,128)S(1)}, f32[18,24,128]{2,1,0:T(8,128)S(1)}, u32[]{:S(2)}, u32[]{:S(2)}) collective-permute-start(f32[18,24,128]{2,1,0:T(8,128)S(1)} %get-tuple-element.43), channel_id=1, source_target_pairs={{8,16},{16,8},{9,17},{17,9},{10,18},{18,10},{11,19},{19,11},{12,20... | collective-permute-start | bytes 663560 | tf_op jit(solution)/shard_map/ppermute | solution.py:636
  65.8 7.1 %shard_map.62.inner = f32[9,2,32,8,128]{4,3,2,1,0:T(8,128)S(1)} custom-call(s32[128]{0:T(128)S(1)} %get-tuple-element.40.work, f32[32,8,128]{2,1,0:T(8,128)S(1)} %get-tuple-element.28.slots, f32[9,32,128]{2,1,0:T(8,128)S(1)} %get-tuple-element.41.weight), custom_call_target="tpu_custom_call" | custom-call | bytes 18000000 | tf_op jit(solution)/shard_map/pallas_call | solution.py:702
  72.9 0.0 collective-permute-done.4.x_near
  72.9 0.0 collective-permute-done.5.x_far
  72.9 0.3 shard_map.63
  73.1 2.2 %collective-permute-start.6 = (f32[456,128]{1,0:T(8,128)S(1)}, f32[456,128]{1,0:T(8,128)S(1)}, u32[]{:S(2)}, u32[]{:S(2)}) collective-permute-start(f32[456,128]{1,0:T(8,128)S(1)} %get-tuple-element.44), channel_id=1, source_target_pairs={{0,1},{2,3},{4,5},{6,7},{1,0},{3,2},{5,4},{7,6},{8,9},{10,11},{12,... | collective-permute-start | bytes 700424 | tf_op jit(solution)/shard_map/ppermute | solution.py:636
  75.3 1.9 %collective-permute-start.7 = (f32[456,128]{1,0:T(8,128)S(1)}, f32[456,128]{1,0:T(8,128)S(1)}, u32[]{:S(2)}, u32[]{:S(2)}) collective-permute-start(f32[456,128]{1,0:T(8,128)S(1)} %get-tuple-element.45), channel_id=1, source_target_pairs={{1,2},{3,4},{5,6},{2,1},{4,3},{6,5},{9,10},{11,12},{13,14},{10,9},... | collective-permute-start | bytes 700424 | tf_op jit(solution)/shard_map/ppermute | solution.py:636
  77.2 0.0 collective-permute-done.6.y_near
  77.3 5.4 %collective-permute-done.7.y_far = f32[456,128]{1,0:T(8,128)S(1)} collective-permute-done((f32[456,128]{1,0:T(8,128)S(1)}, f32[456,128]{1,0:T(8,128)S(1)}, u32[]{:S(2)}, u32[]{:S(2)}) %collective-permute-start.7) | collective-permute-done | bytes 233504 | tf_op jit(solution)/shard_map/ppermute | solution.py:636
  82.7 10.3 %shard_map.64 = f32[3,32,3072]{2,1,0:T(8,128)} custom-call(f32[9,2,32,8,128]{4,3,2,1,0:T(8,128)S(1)} %get-tuple-element.39.outer, f32[9,2,32,8,128]{4,3,2,1,0:T(8,128)S(1)} %shard_map.62.inner, f32[18,24,128]{2,1,0:T(8,128)S(1)} %collective-permute-done.4.x_near, f32[18,24,128]{2,1,0:T(8,128)S(1)} %collective-permute-done.5.x_far, ...), custom_call_target="tpu_custom_call" | custom-call | bytes 3000000 | tf_op jit(solution)/shard_map/pallas_call | solution.py:713
Async XLA Ops:
  2.1 15.2 %collective-permute-start = (f32[16,3072]{1,0:T(8,128)}, f32[16,3072]{1,0:T(8,128)S(1)}, u32[]{:S(2)}, u32[]{:S(2)}) collective-permute-start(f32[16,3072]{1,0:T(8,128)} %get-tuple-element.31), channel_id=1, source_target_pairs={{0,8},{16,24},{8,0},{24,16},{1,9},{17,25},{9,1},{25,17},{2,10},{18... | collective-permute-start | bytes 589832 | tf_op jit(solution)/shard_map/ppermute | solution.py:636
  3.3 14.0 %collective-permute-start.1 = (f32[16,3072]{1,0:T(8,128)}, f32[16,3072]{1,0:T(8,128)S(1)}, u32[]{:S(2)}, u32[]{:S(2)}) collective-permute-start(f32[16,3072]{1,0:T(8,128)} %get-tuple-element.32), channel_id=1, source_target_pairs={{8,16},{16,8},{9,17},{17,9},{10,18},{18,10},{11,19},{19,11},{12,20... | collective-permute-start | bytes 589832 | tf_op jit(solution)/shard_map/ppermute | solution.py:636
  7.9 14.4 %all-to-all-start = ((f32[32,8,128]{2,1,0:T(8,128)}), f32[32,8,128]{2,1,0:T(8,128)}, u32[]{:S(2)}, u32[]{:S(2)}) async-start(f32[32,8,128]{2,1,0:T(8,128)} %shard_map.55), calls=%async_computation | async-start | bytes 262144 | tf_op jit(solution)/shard_map/all_to_all | solution.py:656
  15.2 1.3 %copy-start = (f32[3,32,3072]{2,1,0:T(8,128)S(1)}, f32[3,32,3072]{2,1,0:T(8,128)}, u32[]{:S(2)}) copy-start(f32[3,32,3072]{2,1,0:T(8,128)} %state.3) | copy-start | bytes 3538948
  18.3 6.3 %collective-permute-start.2 = (f32[424,128]{1,0:T(8,128)}, f32[424,128]{1,0:T(8,128)}, u32[]{:S(2)}, u32[]{:S(2)}) collective-permute-start(f32[424,128]{1,0:T(8,128)} %get-tuple-element.35), channel_id=1, source_target_pairs={{0,1},{2,3},{4,5},{6,7},{1,0},{3,2},{5,4},{7,6},{8,9},{10,11},{12,... | collective-permute-start | bytes 651272 | tf_op jit(solution)/shard_map/ppermute | solution.py:636
  18.6 7.5 %collective-permute-start.3 = (f32[424,128]{1,0:T(8,128)}, f32[424,128]{1,0:T(8,128)}, u32[]{:S(2)}, u32[]{:S(2)}) collective-permute-start(f32[424,128]{1,0:T(8,128)} %get-tuple-element.36), channel_id=1, source_target_pairs={{1,2},{3,4},{5,6},{2,1},{4,3},{6,5},{9,10},{11,12},{13,14},{10,9},... | collective-permute-start | bytes 651272 | tf_op jit(solution)/shard_map/ppermute | solution.py:636
  61.4 11.5 %collective-permute-start.4 = (f32[18,24,128]{2,1,0:T(8,128)S(1)}, f32[18,24,128]{2,1,0:T(8,128)S(1)}, u32[]{:S(2)}, u32[]{:S(2)}) collective-permute-start(f32[18,24,128]{2,1,0:T(8,128)S(1)} %get-tuple-element.42), channel_id=1, source_target_pairs={{0,8},{16,24},{8,0},{24,16},{1,9},{17,25},{9,1},{25,17},{2,10},{18... | collective-permute-start | bytes 663560 | tf_op jit(solution)/shard_map/ppermute | solution.py:636
  61.8 11.1 %collective-permute-start.5 = (f32[18,24,128]{2,1,0:T(8,128)S(1)}, f32[18,24,128]{2,1,0:T(8,128)S(1)}, u32[]{:S(2)}, u32[]{:S(2)}) collective-permute-start(f32[18,24,128]{2,1,0:T(8,128)S(1)} %get-tuple-element.43), channel_id=1, source_target_pairs={{8,16},{16,8},{9,17},{17,9},{10,18},{18,10},{11,19},{19,11},{12,20... | collective-permute-start | bytes 663560 | tf_op jit(solution)/shard_map/ppermute | solution.py:636
  73.1 4.1 %collective-permute-start.6 = (f32[456,128]{1,0:T(8,128)S(1)}, f32[456,128]{1,0:T(8,128)S(1)}, u32[]{:S(2)}, u32[]{:S(2)}) collective-permute-start(f32[456,128]{1,0:T(8,128)S(1)} %get-tuple-element.44), channel_id=1, source_target_pairs={{0,1},{2,3},{4,5},{6,7},{1,0},{3,2},{5,4},{7,6},{8,9},{10,11},{12,... | collective-permute-start | bytes 700424 | tf_op jit(solution)/shard_map/ppermute | solution.py:636
  75.3 7.4 %collective-permute-start.7 = (f32[456,128]{1,0:T(8,128)S(1)}, f32[456,128]{1,0:T(8,128)S(1)}, u32[]{:S(2)}, u32[]{:S(2)}) collective-permute-start(f32[456,128]{1,0:T(8,128)S(1)} %get-tuple-element.45), channel_id=1, source_target_pairs={{1,2},{3,4},{5,6},{2,1},{4,3},{6,5},{9,10},{11,12},{13,14},{10,9},... | collective-permute-start | bytes 700424 | tf_op jit(solution)/shard_map/ppermute | solution.py:636

commit v5 on v4

--- a/solution.py
+++ b/solution.py
@@ -21,8 +21,9 @@
 PACKED = CX * NZ // LANES
 FRIM = 3
 FH = CY + 2 * FRIM
+EDGE = 4
 FIELDS = 3 * STEPS
-UNROLL = 4
+UNROLL = 8
 ROWS = 8
 GROUPS = CX // ROWS
 GROUP = ROWS * CY
@@ -121,10 +122,10 @@
 FORCE_PIECE = len(FORCE_BLOCKS) * PACKED + 24
 
 
-def state_rows_kernel(state, near, far, first_rows, last_rows):
+def state_rows_kernel(top, bottom, near, far, first_rows, last_rows):
     for c in range(3):
-        first_rows[RIM * c : RIM * c + RIM, :] = state[c, 0:RIM, :]
-        last_rows[RIM * c : RIM * c + RIM, :] = state[c, CX - RIM : CX, :]
+        first_rows[RIM * c : RIM * c + RIM, :] = top[c, 0:RIM, :]
+        last_rows[RIM * c : RIM * c + RIM, :] = bottom[c, ROWS - RIM : ROWS, :]
     first_rows[3 * RIM : 16, :] = jnp.zeros((1, CY * NZ), F32)
     last_rows[3 * RIM : 16, :] = jnp.zeros((1, CY * NZ), F32)
     to_partners("gx", first_rows, last_rows, near, far)
@@ -220,20 +221,18 @@
         works[w][WORK - 1] = counts[w]
 
 
-def layout_kernel(state, wide, first_layers, last_layers):
-    wide[...] = jnp.zeros(wide.shape, F32)
-    for c in range(3):
-        for y in range(CY):
-            wide[c, RIM + y, PAD : PAD + CX, 0:NZ] = state[c, :, NZ * y : NZ * y + NZ]
+def state_layers_kernel(state, first_layers, last_layers):
+    blank = jnp.zeros((CX, LANES - NZ), F32)
     for out, layer_of in ((first_layers, lambda d: d - 1), (last_layers, lambda d: CY - d)):
         for c in range(3):
             for dist in range(1, RIM + 1):
                 base = (c * RIM + dist - 1) * PACKED
+                y = layer_of(dist)
 
                 def put(row, rows, base=base, out=out):
                     out[base + row : base + row + 8, :] = rows
 
-                pack(put, wide[c, RIM + layer_of(dist), PAD : PAD + CX, :])
+                pack(put, jnp.concatenate([state[c, :, NZ * y : NZ * y + NZ], blank], axis=1))
 
 
 def state_corner_kernel(bulk_first, bulk_last, x_near, x_far, near, far, first, last, before, after):
@@ -363,7 +362,7 @@
 def forward_kernel(
     beams,
     work,
-    wide,
+    state,
     x_near,
     x_far,
     y_near,
@@ -386,10 +385,11 @@
     from_partners("gx", x_near, x_far, before, after)
     mask[...] = row_mask(places[0], places[1])
     from_partners("gy", y_near, y_far, below, above)
-    s0[...] = wide[...]
+    s0[...] = jnp.zeros(s0.shape, F32)
     for c in range(3):
         for y in range(CY):
             lanes = slice(NZ * y, NZ * y + NZ)
+            s0[c, RIM + y, PAD : PAD + CX, 0:NZ] = state[c, :, lanes]
             s0[c, RIM + y, PAD - RIM : PAD, 0:NZ] = before[RIM * c : RIM * c + RIM, lanes]
             s0[c, RIM + y, PAD + CX : PAD + CX + RIM, 0:NZ] = after[RIM * c : RIM * c + RIM, lanes]
     for piece, layer_of in ((above, lambda d: RIM + CY - 1 + d), (below, lambda d: RIM - d)):
@@ -447,9 +447,9 @@
             line, place = divmod(n * beams + k, apart)
             here = (lane >= place * owners) & (lane < place * owners + owners)
             lines[line] = jnp.where(here, one, lines[line])
-    sums[...] = jnp.zeros(sums.shape, F32)
     for line, total in enumerate(lines):
-        sums[:, line : line + 1, :] = jnp.broadcast_to(total[None], (owners, 1, LANES))
+        span = slice(LANES * line, LANES * line + LANES)
+        sums[:, :, span] = jnp.broadcast_to(total[None], (owners, 1, LANES))
 
 
 def scatter_slots(part_of, together, work, slots, weight, total, force):
@@ -492,7 +492,7 @@
         for k in range(beams):
             line, place = divmod(n * beams + k, apart)
             here = (lane >= place * owners) & (lane < place * owners + owners)
-            one = fold(owners, jnp.where(here, lines[line : line + 1], 0.0))
+            one = fold(owners, jnp.where(here, lines[:, LANES * line : LANES * line + LANES], 0.0))
             mean = jnp.where(beam == k, one, mean)
         misfit = seen[n] - mean - slots[:, 2 + n, :]
         for c in range(3):
@@ -532,41 +532,97 @@
     to_partners("gy", first_layers, last_layers, near, far)
 
 
-def backward_kernel(
-    outer,
-    inner,
-    x_near,
-    x_far,
-    y_near,
-    y_far,
-    s0,
-    s1,
-    s2,
-    out,
-    a3,
-    a2,
-    a1,
-    a0,
-    mask,
-    below,
-    above,
-    before,
-    after,
+def pull(field, source, target, low, high, first_row, chunks, add, mask, places):
+    def layer(i, carry):
+        y = i + low
+        keep = layer_mask(y, places[2], places[3])
+        done = []
+        for t in range(chunks):
+            r = first_row + 8 * t
+            here, ahead, behind = pl.ds(r, 8), pl.ds(r + 1, 8), pl.ds(r - 1, 8)
+            v = [field[c, y + RIM, here, :] for c in range(3)]
+            v_ahead = [field[c, y + RIM, ahead, :] for c in range(3)]
+            v_behind = [field[c, y + RIM, behind, :] for c in range(3)]
+            v_next = [field[c, y + RIM + 1, here, :] for c in range(3)]
+            v_last = [field[c, y + RIM - 1, here, :] for c in range(3)]
+            a = [source[c, y + FRIM, here, :] for c in range(3)]
+            scaled = [0.1 * f for f in a]
+            bends = [None] * 3
+            for d, (up, down) in enumerate(((v_ahead, v_behind), (v_next, v_last), (None, None))):
+                for c in range(3):
+                    u, w = (up[c], down[c]) if d < 2 else (next_level(v[c]), last_level(v[c]))
+                    part = (u - w) * scaled[c]
+                    bends[d] = part if bends[d] is None else bends[d] + part
+            x_ahead = 0.1 + 0.1 * v_ahead[0]
+            x_behind = 0.1 - 0.1 * v_behind[0]
+            y_next = 0.1 + 0.1 * v_next[1]
+            y_last = 0.1 - 0.1 * v_last[1]
+            inside = mask[here, :] * keep
+            for c in range(3):
+                total = 0.4 * a[c] - bends[c]
+                total = total + (
+                    x_ahead * source[c, y + FRIM, ahead, :] + x_behind * source[c, y + FRIM, behind, :]
+                )
+                total = total + (
+                    y_next * source[c, y + FRIM + 1, here, :] + y_last * source[c, y + FRIM - 1, here, :]
+                )
+                product = v[2] * scaled[c]
+                total = total + (next_level(scaled[c] + product) + last_level(scaled[c] - product))
+                if add:
+                    total = total + target[c, y + FRIM, here, :]
+                done.append((c, here, total * inside))
+        for c, here, total in done:
+            target[c, y + FRIM, here, :] = total
+        return carry
+
+    lax.fori_loop(0, high - low, layer, 0, unroll=min(UNROLL, high - low))
+
+
+def edge_layers(side):
+    start = (FRIM, FRIM + CY - EDGE)[side]
+    return slice(start, start + EDGE)
+
+
+def inner_backward_kernel(
+    outer, inner, x_near, x_far, s0, s1, s2, part, e1, e2, e3, a1, a2, a3, a0, mask, before, after
 ):
     from_partners("gx", x_near, x_far, before, after)
-    from_partners("gy", y_near, y_far, below, above)
     places = mesh_places()
     mask[...] = row_mask(places[0], places[1])
     adjoints = (a1, a2, a3)
     for n in range(STEPS):
         adjoints[n][...] = jnp.zeros(adjoints[n].shape, F32)
         for c in range(3):
-            for g, (part, k) in enumerate(((outer, 0), (inner, 0), (inner, 1), (outer, 1))):
+            for g, (force, k) in enumerate(((outer, 0), (inner, 0), (inner, 1), (outer, 1))):
                 row = PAD + ROWS * g
-                adjoints[n][c, FRIM : FRIM + CY, row : row + ROWS, :] = part[3 * n + c, k]
+                adjoints[n][c, FRIM : FRIM + CY, row : row + ROWS, :] = force[3 * n + c, k]
     for b, (n, c, i) in enumerate(FORCE_BLOCKS):
         adjoints[n][c, FRIM : FRIM + CY, PAD - 1 - i, :] = unpack(before[b])
         adjoints[n][c, FRIM : FRIM + CY, PAD + CX + i, :] = unpack(after[b])
+    pull(s2, a3, a2, 1, CY - 1, 4, 5, True, mask, places)
+    pull(s1, a2, a1, 2, CY - 2, 4, 5, True, mask, places)
+    pull(s0, a1, a0, 3, CY - 3, PAD, 4, False, mask, places)
+    for n, edges in enumerate((e1, e2, e3)):
+        for side in range(2):
+            edges[:, side] = adjoints[n][:, edge_layers(side)]
+    for c in range(3):
+        for y in range(3, CY - 3):
+            part[c, :, NZ * y : NZ * y + NZ] = a0[c, FRIM + y, PAD : PAD + CX, 0:NZ]
+
+
+def backward_kernel(
+    part, e1, e2, e3, y_near, y_far, s0, s1, s2, out, a1, a2, a3, a0, mask, below, above
+):
+    from_partners("gy", y_near, y_far, below, above)
+    places = mesh_places()
+    mask[...] = row_mask(places[0], places[1])
+    adjoints = (a1, a2, a3)
+    out[...] = part[...]
+    for n, edges in enumerate((e1, e2, e3)):
+        for side in range(2):
+            adjoints[n][:, edge_layers(side)] = edges[:, side]
+        for start in (0, FRIM + CY):
+            adjoints[n][:, start : start + FRIM] = jnp.zeros((3, FRIM, XH, LANES), F32)
     for piece, layer_of in ((above, lambda d: FRIM + CY - 1 + d), (below, lambda d: FRIM - d)):
         for b, (n, c, i) in enumerate(FORCE_BLOCKS):
             adjoints[n][c, layer_of(i + 1), PAD : PAD + CX, :] = unpack(piece[b * PACKED : b * PACKED + PACKED, :])
@@ -574,57 +630,14 @@
         for row, (n, c, dist, side, k) in enumerate(FORCE_CORNERS):
             x = (PAD - k, PAD + CX - 1 + k)[side]
             adjoints[n][c, layer_of(dist), x : x + 1, :] = piece[base + row : base + row + 1, :]
-
-    def pull(field, source, target, low, high, first_row, chunks, add):
-        def layer(i, carry):
-            y = i + low
-            keep = layer_mask(y, places[2], places[3])
-            done = []
-            for t in range(chunks):
-                r = first_row + 8 * t
-                here, ahead, behind = pl.ds(r, 8), pl.ds(r + 1, 8), pl.ds(r - 1, 8)
-                v = [field[c, y + RIM, here, :] for c in range(3)]
-                v_ahead = [field[c, y + RIM, ahead, :] for c in range(3)]
-                v_behind = [field[c, y + RIM, behind, :] for c in range(3)]
-                v_next = [field[c, y + RIM + 1, here, :] for c in range(3)]
-                v_last = [field[c, y + RIM - 1, here, :] for c in range(3)]
-                a = [source[c, y + FRIM, here, :] for c in range(3)]
-                scaled = [0.1 * f for f in a]
-                bends = [None] * 3
-                for d, (up, down) in enumerate(((v_ahead, v_behind), (v_next, v_last), (None, None))):
-                    for c in range(3):
-                        u, w = (up[c], down[c]) if d < 2 else (next_level(v[c]), last_level(v[c]))
-                        part = (u - w) * scaled[c]
-                        bends[d] = part if bends[d] is None else bends[d] + part
-                x_ahead = 0.1 + 0.1 * v_ahead[0]
-                x_behind = 0.1 - 0.1 * v_behind[0]
-                y_next = 0.1 + 0.1 * v_next[1]
-                y_last = 0.1 - 0.1 * v_last[1]
-                inside = mask[here, :] * keep
-                for c in range(3):
-                    total = 0.4 * a[c] - bends[c]
-                    total = total + (
-                        x_ahead * source[c, y + FRIM, ahead, :] + x_behind * source[c, y + FRIM, behind, :]
-                    )
-                    total = total + (
-                        y_next * source[c, y + FRIM + 1, here, :] + y_last * source[c, y + FRIM - 1, here, :]
-                    )
-                    product = v[2] * scaled[c]
-                    total = total + (next_level(scaled[c] + product) + last_level(scaled[c] - product))
-                    if add:
-                        total = total + target[c, y + FRIM, here, :]
-                    done.append((c, here, total * inside))
-            for c, here, total in done:
-                target[c, y + FRIM, here, :] = total
-            return carry
-
-        lax.fori_loop(0, high - low, layer, 0, unroll=UNROLL)
-
-    pull(s2, a3, a2, -2, CY + 2, 4, 5, True)
-    pull(s1, a2, a1, -1, CY + 1, 4, 5, True)
-    pull(s0, a1, a0, 0, CY, PAD, 4, False)
+    for low in (-2, CY - 1):
+        pull(s2, a3, a2, low, low + 3, 4, 5, True, mask, places)
+    for low in (-1, CY - 2):
+        pull(s1, a2, a1, low, low + 3, 4, 5, True, mask, places)
+    for low in (0, CY - 3):
+        pull(s0, a1, a0, low, low + 3, PAD, 4, False, mask, places)
     for c in range(3):
-        for y in range(CY):
+        for y in (0, 1, 2, CY - 3, CY - 2, CY - 1):
             out[c, :, NZ * y : NZ * y + NZ] = a0[c, FRIM + y, PAD : PAD + CX, 0:NZ]
 
 
@@ -641,9 +654,19 @@
     beams = beam_dir.shape[1]
     rows = peers * capacity // LANES
     x_rim = (16, CY * NZ)
-    near, far = call(
-        state_rows_kernel, (shape(*x_rim), shape(*x_rim)), [pltpu.VMEM(x_rim, F32)] * 2, limit=60, ins=1
-    )(initial_state)
+    edge = (3, ROWS, CY * NZ)
+    near, far = pl.pallas_call(
+        state_rows_kernel,
+        out_shape=(shape(*x_rim), shape(*x_rim)),
+        in_specs=[
+            pl.BlockSpec(edge, lambda i: (0, 0, 0)),
+            pl.BlockSpec(edge, lambda i: (0, GROUPS - 1, 0)),
+        ],
+        out_specs=(pl.BlockSpec(x_rim, lambda i: (0, 0)), pl.BlockSpec(x_rim, lambda i: (0, 0))),
+        grid=(1,),
+        scratch_shapes=[pltpu.VMEM(x_rim, F32)] * 2,
+        compiler_params=pltpu.CompilerParams(vmem_limit_bytes=60 * MIB),
+    )(initial_state, initial_state)
     x_near, x_far = swap(near, far, "gx")
     lists = (peers, 8, capacity)
     slots = call(
@@ -665,7 +688,7 @@
     )(slots)
     field = shape(3, YH, XH, LANES)
     bulk = shape(3 * RIM * PACKED, LANES)
-    wide, bulk_first, bulk_last = call(layout_kernel, (field, bulk, bulk), ins=1, micros=2)(initial_state)
+    bulk_first, bulk_last = call(state_layers_kernel, (bulk, bulk), ins=1)(initial_state)
     y_rim = (STATE_PIECE, LANES)
     near, far = call(
         state_corner_kernel,
@@ -674,18 +697,17 @@
         ins=4,
     )(bulk_first, bulk_last, x_near, x_far)
     y_near, y_far = swap(near, far, "gy")
-    lines = -(-STEPS * beams * peers // LANES // 8) * 8
     mask = pltpu.VMEM((XH, LANES), F32)
     seen, sums, s0, s1, s2 = call(
         functools.partial(forward_kernel, beams),
-        (shape(STEPS, rows, LANES), shape(peers, lines, LANES), field, field, field),
+        (shape(STEPS, rows, LANES), shape(peers, 1, STEPS * beams * peers), field, field, field),
         [pltpu.VMEM(field.shape, F32), pltpu.VMEM((GROUPS, 2 * FIELDS * NZ, GROUP), BF16), mask]
         + [pltpu.VMEM(y_rim, F32)] * 2
         + [pltpu.VMEM(x_rim, F32)] * 2,
         limit=32,
         ins=7,
         scalar_in=(0,),
-    )(every_work, wide, x_near, x_far, y_near, y_far, slots)
+    )(every_work, initial_state, x_near, x_far, y_near, y_far, slots)
     sums = lax.all_to_all(sums, AXES, split_axis=0, concat_axis=0, tiled=True)
     x_rim = (len(FORCE_BLOCKS), PACKED, LANES)
     part = shape(FIELDS, 2, CY, ROWS, LANES)
@@ -710,16 +732,20 @@
         ins=4,
     )(outer, inner, x_near, x_far)
     y_near, y_far = swap(near, far, "gy")
+    edges = shape(3, 2, EDGE, XH, LANES)
+    adjoint = pltpu.VMEM((3, FH, XH, LANES), F32)
+    whole = shape(*initial_state.shape)
+    part, e1, e2, e3 = call(
+        inner_backward_kernel,
+        (whole, edges, edges, edges),
+        [adjoint] * 4 + [mask] + [pltpu.VMEM(x_rim, F32)] * 2,
+        limit=32,
+        ins=7,
+        micros=8,
+    )(outer, inner, x_near, x_far, s0, s1, s2)
     return call(
-        backward_kernel,
-        shape(*initial_state.shape),
-        [pltpu.VMEM((3, FH, XH, LANES), F32)] * 4
-        + [mask]
-        + [pltpu.VMEM(y_rim, F32)] * 2
-        + [pltpu.VMEM(x_rim, F32)] * 2,
-        limit=32,
-        ins=9,
-    )(outer, inner, x_near, x_far, y_near, y_far, s0, s1, s2)
+        backward_kernel, whole, [adjoint] * 4 + [mask] + [pltpu.VMEM(y_rim, F32)] * 2, limit=32, ins=9
+    )(part, e1, e2, e3, y_near, y_far, s0, s1, s2)
 
 
 def solution(mesh):

time: 93.7 us -> 84.3 us (0.90); the launches traced: 93 us -> 84.8 us
  waiting for transfers between devices: 7.65 us -> 3.7 us
  Pallas kernels: 49.1 us -> 45.8 us
  local copies, waits for them, and re-layouts: 1.27 us -> 0.01 us
  starting transfers between devices: 22.3 us -> 23.5 us
    ppermute x4, waiting for transfers between devices: 7.02 us -> 1.31 us  [swap(): lax.ppermute(far, axis, pairs(1))]
    ppermute x4, starting transfers between devices: 10.9 us -> 12.9 us  [swap(): lax.ppermute(far, axis, pairs(1))]
    all_to_all x1, waiting for transfers between devices: 0.63 us -> 2.38 us  [local(): slots = lax.all_to_all(slots, AXES, split_axis=0, concat_axis=0, tiled=True)]
    pallas_call x1, Pallas kernels: 15.5 us -> 13.9 us  [local(): call(functools.partial(forward_kernel, beams), (shape(STEPS, rows, LANES)...]
    unnamed x2, local copies, waits for them, and re-layouts: 1.27 us -> 0.01 us
    pallas_call x3 -> x4, Pallas kernels: 13.2 us -> 13.2 us  [the longest x1 7.76 us: local(): call(inner_backward_kernel, (whole, edges, edges, edges), [adjoint] * 4 +...]
  transfers between devices with their start and end apart: 9 -> 9, of which waited for: 3 -> 3; matrix products, arithmetic and copies ran while one was open for 0% -> 0% of each run, Pallas kernels for 15% -> 24%
where the time goes in v5:
time: 84.3 us; the launch traced here: 84.8 us
  Pallas kernels  45.8 us (54%)
  starting transfers between devices  23.5 us (28%)
  blocking collectives  11.7 us (14%)
  waiting for transfers between devices  3.7 us (4%)
    pallas_call x1, Pallas kernels, local(): call(functools.partial(forward_kernel, beams), (shape(STEPS, rows, LANES)...  13.9 us
    ppermute x4, starting transfers between devices, swap(): lax.ppermute(far, axis, pairs(1))  12.9 us
    all_to_all x1, blocking collectives, local(): sums = lax.all_to_all(sums, AXES, split_axis=0, concat_axis=0, tiled=True)  11.7 us
    pallas_call x1, Pallas kernels, local(): call(inner_backward_kernel, (whole, edges, edges, edges), [adjoint] * 4 +...  7.76 us
    pallas_call x1, Pallas kernels, local(): call(functools.partial(outer_force_kernel, beams), (part, shape(FIELDS, r...  7.22 us
    all_to_all x1, starting transfers between devices, local(): slots = lax.all_to_all(slots, AXES, split_axis=0, concat_axis=0, tiled=True)  7.22 us
    pallas_call x1, Pallas kernels, local(): call(inner_force_kernel, part, [total], limit=24, ins=3, scalar_in=(0,),...  7.07 us
    ppermute x4, starting transfers between devices, swap(): lax.ppermute(near, axis, pairs(0))  3.36 us
  transfers between devices with their start and end apart: 9, of which 3 were waited for; matrix products, arithmetic and copies ran while one was open for 0% of the time, Pallas kernels for 24%

profile of v5, /device:TPU:5, one launch (start us, length us, event | category | flops | bytes accessed | tf_op | source)
XLA Modules:
  0.0 84.8 jit_solution(4210553166943478036)
XLA Ops:
  0.0 0.0 copy-start
  0.0 2.0 %shard_map.57 = (f32[16,3072]{1,0:T(8,128)}, f32[16,3072]{1,0:T(8,128)}) custom-call(f32[3,32,3072]{2,1,0:T(8,128)} %state.3, f32[3,32,3072]{2,1,0:T(8,128)} %state.3), custom_call_target="tpu_custom_call" | custom-call | tf_op jit(solution)/shard_map/pallas_call | solution.py:658
  2.0 1.2 %collective-permute-start = (f32[16,3072]{1,0:T(8,128)}, f32[16,3072]{1,0:T(8,128)S(1)}, u32[]{:S(2)}, u32[]{:S(2)}) collective-permute-start(f32[16,3072]{1,0:T(8,128)} %get-tuple-element.33), channel_id=1, source_target_pairs={{0,8},{16,24},{8,0},{24,16},{1,9},{17,25},{9,1},{25,17},{2,10},{18... | collective-permute-start | bytes 589832 | tf_op jit(solution)/shard_map/ppermute | solution.py:649
  3.2 1.9 %collective-permute-start.1 = (f32[16,3072]{1,0:T(8,128)}, f32[16,3072]{1,0:T(8,128)S(1)}, u32[]{:S(2)}, u32[]{:S(2)}) collective-permute-start(f32[16,3072]{1,0:T(8,128)} %get-tuple-element.34), channel_id=1, source_target_pairs={{8,16},{16,8},{9,17},{17,9},{10,18},{18,10},{11,19},{19,11},{12,20... | collective-permute-start | bytes 589832 | tf_op jit(solution)/shard_map/ppermute | solution.py:649
  5.1 2.7 %shard_map.55 = f32[32,8,128]{2,1,0:T(8,128)} custom-call(f32[3,4]{1,0:T(4,128)} %beam_dir.1, f32[3,1,32,128]{3,2,1,0:T(8,128)} %obs.1, s32[1,32,128]{2,1,0:T(8,128)} %beam.1, s32[1,32,128]{2,1,0:T(8,128)} %cell.1), custom_call_target="tpu_custom_call" | custom-call | bytes 3000000 | tf_op jit(solution)/shard_map/pallas_call | solution.py:672
  7.9 7.2 %all-to-all-start = ((f32[32,8,128]{2,1,0:T(8,128)}), f32[32,8,128]{2,1,0:T(8,128)S(1)}, u32[]{:S(2)}, u32[]{:S(2)}) async-start(f32[32,8,128]{2,1,0:T(8,128)} %shard_map.55), calls=%async_computation | async-start | bytes 262144 | tf_op jit(solution)/shard_map/all_to_all | solution.py:679
  15.1 0.0 copy-done
  15.1 0.9 %shard_map.58 = (f32[360,128]{1,0:T(8,128)S(1)}, f32[360,128]{1,0:T(8,128)S(1)}) custom-call(f32[3,32,3072]{2,1,0:T(8,128)S(1)} %copy-done), custom_call_target="tpu_custom_call" | custom-call | bytes 3000000 | tf_op jit(solution)/shard_map/pallas_call | solution.py:691
  16.0 0.0 collective-permute-done.x_near
  16.1 0.0 collective-permute-done.1.x_far
  16.1 0.2 shard_map.59
  16.2 0.4 collective-permute-start.2
  16.7 3.1 %collective-permute-start.3 = (f32[424,128]{1,0:T(8,128)S(1)}, f32[424,128]{1,0:T(8,128)S(1)}, u32[]{:S(2)}, u32[]{:S(2)}) collective-permute-start(f32[424,128]{1,0:T(8,128)S(1)} %get-tuple-element.38), channel_id=1, source_target_pairs={{1,2},{3,4},{5,6},{2,1},{4,3},{6,5},{9,10},{11,12},{13,14},{10,9},... | collective-permute-start | bytes 651272 | tf_op jit(solution)/shard_map/ppermute | solution.py:649
  19.8 2.4 %all-to-all-done.received = f32[32,8,128]{2,1,0:T(8,128)S(1)} async-done(((f32[32,8,128]{2,1,0:T(8,128)}), f32[32,8,128]{2,1,0:T(8,128)S(1)}, u32[]{:S(2)}, u32[]{:S(2)}) %all-to-all-start) | async-done | bytes 131104 | tf_op jit(solution)/shard_map/all_to_all | solution.py:679
  22.2 1.3 %shard_map.56 = (f32[32,8,128]{2,1,0:T(8,128)S(1)}, s32[128]{0:T(128)S(1)}, s32[128]{0:T(128)S(1)}, s32[128]{0:T(128)S(1)}) custom-call(f32[32,8,128]{2,1,0:T(8,128)S(1)} %all-to-all-done.received), custom_call_target="tpu_custom_call" | custom-call | bytes 6000000 | tf_op jit(solution)/shard_map/pallas_call | solution.py:681
  23.5 0.0 collective-permute-done.2.y_near
  23.5 0.4 collective-permute-done.3.y_far
  23.9 13.9 %shard_map.60 = (f32[3,32,128]{2,1,0:T(8,128)S(1)}, f32[32,1,384]{2,1,0:T(1,128)S(1)}, f32[3,42,48,128]{3,2,1,0:T(8,128)S(1)}, f32[3,42,48,128]{3,2,1,0:T(8,128)S(1)}, f32[3,42,48,128]{3,2,1,0:T(8,128)S(1)}) custom-call(s32[128]{0:T(128)S(1)} %get-tuple-element.32.work, f32[3,32,3072]{2,1,0:T(8,128)S(1)} %copy-done, ...), custom_call_target="tpu_custom_call" | custom-call | bytes 3000000 | tf_op jit(solution)/shard_map/pallas_call | solution.py:701
  37.7 11.7 %all_to_all.10.sums = f32[32,1,384]{2,1,0:T(1,128)S(1)} all-to-all(f32[32,1,384]{2,1,0:T(1,128)S(1)} %get-tuple-element.40), channel_id=1, replica_groups=mesh['gx'=4,'gy'=8] {'gx','gy'}, dimensions={0} | all-to-all | bytes 98304 | tf_op jit(solution)/shard_map/all_to_all | solution.py:711
  49.4 7.2 %shard_map.61 = (f32[9,2,32,8,128]{4,3,2,1,0:T(8,128)S(1)}, f32[9,32,128]{2,1,0:T(8,128)S(1)}, f32[18,24,128]{2,1,0:T(8,128)S(1)}, f32[18,24,128]{2,1,0:T(8,128)S(1)}) custom-call(s32[128]{0:T(128)S(1)} %get-tuple-element.30.work, f32[32,8,128]{2,1,0:T(8,128)S(1)} %get-tuple-element.31.slots, f32[3,32,128]{2,1,0:T(8,128)S(1)} %get-tuple-element.39.seen, ...), custom_call_target="tpu_custom_call" | custom-call | bytes 3000000 | tf_op jit(solution)/shard_map/pallas_call | solution.py:715
  56.6 0.4 collective-permute-start.4
  57.1 5.0 %collective-permute-start.5 = (f32[18,24,128]{2,1,0:T(8,128)S(1)}, f32[18,24,128]{2,1,0:T(8,128)S(1)}, u32[]{:S(2)}, u32[]{:S(2)}) collective-permute-start(f32[18,24,128]{2,1,0:T(8,128)S(1)} %get-tuple-element.45), channel_id=1, source_target_pairs={{8,16},{16,8},{9,17},{17,9},{10,18},{18,10},{11,19},{19,11},{12,20... | collective-permute-start | bytes 663560 | tf_op jit(solution)/shard_map/ppermute | solution.py:649
  62.0 7.1 %shard_map.62.inner = f32[9,2,32,8,128]{4,3,2,1,0:T(8,128)S(1)} custom-call(s32[128]{0:T(128)S(1)} %get-tuple-element.42.work, f32[32,8,128]{2,1,0:T(8,128)S(1)} %get-tuple-element.31.slots, f32[9,32,128]{2,1,0:T(8,128)S(1)} %get-tuple-element.43.weight), custom_call_target="tpu_custom_call" | custom-call | bytes 18000000 | tf_op jit(solution)/shard_map/pallas_call | solution.py:724
  69.1 0.0 collective-permute-done.4.x_near
  69.1 0.9 %collective-permute-done.5.x_far = f32[18,24,128]{2,1,0:T(8,128)S(1)} collective-permute-done((f32[18,24,128]{2,1,0:T(8,128)S(1)}, f32[18,24,128]{2,1,0:T(8,128)S(1)}, u32[]{:S(2)}, u32[]{:S(2)}) %collective-permute-start.5) | collective-permute-done | bytes 221216 | tf_op jit(solution)/shard_map/ppermute | solution.py:649
  70.0 0.3 shard_map.64
  70.3 1.3 %collective-permute-start.6 = (f32[456,128]{1,0:T(8,128)S(1)}, f32[456,128]{1,0:T(8,128)S(1)}, u32[]{:S(2)}, u32[]{:S(2)}) collective-permute-start(f32[456,128]{1,0:T(8,128)S(1)} %get-tuple-element.53), channel_id=1, source_target_pairs={{0,1},{2,3},{4,5},{6,7},{1,0},{3,2},{5,4},{7,6},{8,9},{10,11},{12,... | collective-permute-start | bytes 700424 | tf_op jit(solution)/shard_map/ppermute | solution.py:649
  71.6 2.9 %collective-permute-start.7 = (f32[456,128]{1,0:T(8,128)S(1)}, f32[456,128]{1,0:T(8,128)S(1)}, u32[]{:S(2)}, u32[]{:S(2)}) collective-permute-start(f32[456,128]{1,0:T(8,128)S(1)} %get-tuple-element.54), channel_id=1, source_target_pairs={{1,2},{3,4},{5,6},{2,1},{4,3},{6,5},{9,10},{11,12},{13,14},{10,9},... | collective-permute-start | bytes 700424 | tf_op jit(solution)/shard_map/ppermute | solution.py:649
  74.5 7.8 %shard_map.63 = (f32[3,32,3072]{2,1,0:T(8,128)S(1)}, f32[3,2,4,48,128]{4,3,2,1,0:T(8,128)S(1)}, f32[3,2,4,48,128]{4,3,2,1,0:T(8,128)S(1)}, f32[3,2,4,48,128]{4,3,2,1,0:T(8,128)S(1)}) custom-call(f32[9,2,32,8,128]{4,3,2,1,0:T(8,128)S(1)} %get-tuple-element.41.outer, f32[9,2,32,8,128]{4,3,2,1,0:T(8,128)S(1)} %shard_map.62.inner, ...), custom_call_target="tpu_custom_call" | custom-call | bytes 24000000 | tf_op jit(solution)/shard_map/pallas_call | solution.py:738
  82.3 0.0 collective-permute-done.6.y_near
  82.3 0.0 collective-permute-done.7.y_far
  82.3 2.5 %shard_map.65 = f32[3,32,3072]{2,1,0:T(8,128)} custom-call(f32[3,32,3072]{2,1,0:T(8,128)S(1)} %get-tuple-element.49.part, f32[3,2,4,48,128]{4,3,2,1,0:T(8,128)S(1)} %get-tuple-element.50.e1, f32[3,2,4,48,128]{4,3,2,1,0:T(8,128)S(1)} %get-tuple-element.51.e2, f32[3,2,4,48,128]{4,3,2,1,0:T(8,128)S(1)} %get-tuple-element.52.e3, ...), custom_call_target="tpu_custom_call" | custom-call | bytes 3000000 | tf_op jit(solution)/shard_map/pallas_call | solution.py:746
Async XLA Ops:
  0.0 15.1 %copy-start = (f32[3,32,3072]{2,1,0:T(8,128)S(1)}, f32[3,32,3072]{2,1,0:T(8,128)}, u32[]{:S(2)}) copy-start(f32[3,32,3072]{2,1,0:T(8,128)} %state.3) | copy-start | bytes 3538948
  2.0 14.0 %collective-permute-start = (f32[16,3072]{1,0:T(8,128)}, f32[16,3072]{1,0:T(8,128)S(1)}, u32[]{:S(2)}, u32[]{:S(2)}) collective-permute-start(f32[16,3072]{1,0:T(8,128)} %get-tuple-element.33), channel_id=1, source_target_pairs={{0,8},{16,24},{8,0},{24,16},{1,9},{17,25},{9,1},{25,17},{2,10},{18... | collective-permute-start | bytes 589832 | tf_op jit(solution)/shard_map/ppermute | solution.py:649
  3.2 12.8 %collective-permute-start.1 = (f32[16,3072]{1,0:T(8,128)}, f32[16,3072]{1,0:T(8,128)S(1)}, u32[]{:S(2)}, u32[]{:S(2)}) collective-permute-start(f32[16,3072]{1,0:T(8,128)} %get-tuple-element.34), channel_id=1, source_target_pairs={{8,16},{16,8},{9,17},{17,9},{10,18},{18,10},{11,19},{19,11},{12,20... | collective-permute-start | bytes 589832 | tf_op jit(solution)/shard_map/ppermute | solution.py:649
  7.9 14.3 %all-to-all-start = ((f32[32,8,128]{2,1,0:T(8,128)}), f32[32,8,128]{2,1,0:T(8,128)S(1)}, u32[]{:S(2)}, u32[]{:S(2)}) async-start(f32[32,8,128]{2,1,0:T(8,128)} %shard_map.55), calls=%async_computation | async-start | bytes 262144 | tf_op jit(solution)/shard_map/all_to_all | solution.py:679
  16.2 7.2 %collective-permute-start.2 = (f32[424,128]{1,0:T(8,128)S(1)}, f32[424,128]{1,0:T(8,128)S(1)}, u32[]{:S(2)}, u32[]{:S(2)}) collective-permute-start(f32[424,128]{1,0:T(8,128)S(1)} %get-tuple-element.37), channel_id=1, source_target_pairs={{0,1},{2,3},{4,5},{6,7},{1,0},{3,2},{5,4},{7,6},{8,9},{10,11},{12,... | collective-permute-start | bytes 651272 | tf_op jit(solution)/shard_map/ppermute | solution.py:649
  16.7 7.2 %collective-permute-start.3 = (f32[424,128]{1,0:T(8,128)S(1)}, f32[424,128]{1,0:T(8,128)S(1)}, u32[]{:S(2)}, u32[]{:S(2)}) collective-permute-start(f32[424,128]{1,0:T(8,128)S(1)} %get-tuple-element.38), channel_id=1, source_target_pairs={{1,2},{3,4},{5,6},{2,1},{4,3},{6,5},{9,10},{11,12},{13,14},{10,9},... | collective-permute-start | bytes 651272 | tf_op jit(solution)/shard_map/ppermute | solution.py:649
  56.6 12.5 %collective-permute-start.4 = (f32[18,24,128]{2,1,0:T(8,128)S(1)}, f32[18,24,128]{2,1,0:T(8,128)S(1)}, u32[]{:S(2)}, u32[]{:S(2)}) collective-permute-start(f32[18,24,128]{2,1,0:T(8,128)S(1)} %get-tuple-element.44), channel_id=1, source_target_pairs={{0,8},{16,24},{8,0},{24,16},{1,9},{17,25},{9,1},{25,17},{2,10},{18... | collective-permute-start | bytes 663560 | tf_op jit(solution)/shard_map/ppermute | solution.py:649
  57.1 13.0 %collective-permute-start.5 = (f32[18,24,128]{2,1,0:T(8,128)S(1)}, f32[18,24,128]{2,1,0:T(8,128)S(1)}, u32[]{:S(2)}, u32[]{:S(2)}) collective-permute-start(f32[18,24,128]{2,1,0:T(8,128)S(1)} %get-tuple-element.45), channel_id=1, source_target_pairs={{8,16},{16,8},{9,17},{17,9},{10,18},{18,10},{11,19},{19,11},{12,20... | collective-permute-start | bytes 663560 | tf_op jit(solution)/shard_map/ppermute | solution.py:649
  70.3 12.0 %collective-permute-start.6 = (f32[456,128]{1,0:T(8,128)S(1)}, f32[456,128]{1,0:T(8,128)S(1)}, u32[]{:S(2)}, u32[]{:S(2)}) collective-permute-start(f32[456,128]{1,0:T(8,128)S(1)} %get-tuple-element.53), channel_id=1, source_target_pairs={{0,1},{2,3},{4,5},{6,7},{1,0},{3,2},{5,4},{7,6},{8,9},{10,11},{12,... | collective-permute-start | bytes 700424 | tf_op jit(solution)/shard_map/ppermute | solution.py:649
  71.6 10.7 %collective-permute-start.7 = (f32[456,128]{1,0:T(8,128)S(1)}, f32[456,128]{1,0:T(8,128)S(1)}, u32[]{:S(2)}, u32[]{:S(2)}) collective-permute-start(f32[456,128]{1,0:T(8,128)S(1)} %get-tuple-element.54), channel_id=1, source_target_pairs={{1,2},{3,4},{5,6},{2,1},{4,3},{6,5},{9,10},{11,12},{13,14},{10,9},... | collective-permute-start | bytes 700424 | tf_op jit(solution)/shard_map/ppermute | solution.py:649

commit v6 on v5

--- a/solution.py
+++ b/solution.py
@@ -25,12 +25,15 @@
 FIELDS = 3 * STEPS
 UNROLL = 8
 ROWS = 8
+TURN = 4
 GROUPS = CX // ROWS
 GROUP = ROWS * CY
 BLOCK = 256
 BLOCK_ROWS = BLOCK // LANES
-TOGETHER = 4
+PAIR = 2
+GATHERS, OUTERS, INNERS = 2, 1, 1
 WORK = 128
+BLANK = 256
 F32 = jnp.float32
 BF16 = jnp.bfloat16
 AXES = ("gx", "gy")
@@ -131,6 +134,11 @@
     to_partners("gx", first_rows, last_rows, near, far)
 
 
+def cell_group(cell):
+    x = ((cell + 0.5) * (1.0 / (CY * NZ))).astype(jnp.int32)
+    return lax.shift_right_logical((x + TURN) & (CX - 1), 3)
+
+
 def arrange_kernel(beam_dir, obs, beam, cell, slots, values, places):
     beams = beam_dir.shape[1]
     owned = beam[0]
@@ -154,7 +162,7 @@
     for c in range(3):
         values[:, 5 + c, :] = spread([beam_dir[c : c + 1, k : k + 1] for k in range(beams)])
 
-    group = ((cells + 0.5) * (1.0 / (GROUP * NZ))).astype(jnp.int32)
+    group = cell_group(cells)
     row = lax.broadcasted_iota(jnp.int32, (capacity, capacity), 0)
     column = lax.broadcasted_iota(jnp.int32, (capacity, capacity), 1)
     ahead = jnp.where(row <= column, 1.0, 0.0).astype(BF16)
@@ -201,24 +209,27 @@
             line = line + pltpu.roll(turned[pl.ds(k, rows, stride=apart), :], k * owners, axis=1)
         slots[:, j, :] = line
     cell = slots[:, 0, :]
-    group = ((cell - 0.5) * (1.0 / (GROUP * NZ))).astype(jnp.int32).astype(F32)
+    group = cell_group(cell - 1.0).astype(F32)
     low = jnp.where(cell > 0.5, group, float(GROUPS))
     high = jnp.where(cell > 0.5, group, -1.0)
-    counts = [jnp.int32(0)] * 3
-    works = (every_work, outer_work, inner_work)
-    for block in range(rows // BLOCK_ROWS):
-        span = slice(block * BLOCK_ROWS, block * BLOCK_ROWS + BLOCK_ROWS)
-        first = jnp.min(low[span]).astype(jnp.int32)
-        last = jnp.max(high[span]).astype(jnp.int32)
-        for g in range(GROUPS):
-            hit = ((first <= g) & (last >= g)).astype(jnp.int32)
-            for w in (0, 1 if g in (0, GROUPS - 1) else 2):
-                works[w][counts[w]] = block * GROUPS + g
-                counts[w] = counts[w] + hit
-    for w in range(3):
-        for k in range(TOGETHER):
-            works[w][counts[w] + k] = 0
-        works[w][WORK - 1] = counts[w]
+    spans = [slice(BLOCK_ROWS * b, BLOCK_ROWS * b + BLOCK_ROWS) for b in range(rows // BLOCK_ROWS)]
+    firsts = [jnp.min(low[span]).astype(jnp.int32) for span in spans]
+    lasts = [jnp.max(high[span]).astype(jnp.int32) for span in spans]
+    for work, groups in (
+        (outer_work, (0,)),
+        (inner_work, tuple(range(1, GROUPS))),
+        (every_work, tuple(range(GROUPS))),
+    ):
+        count = jnp.int32(0)
+        for g in groups:
+            for b in range(len(spans)):
+                work[count] = b * GROUPS + g
+                count = count + ((firsts[b] <= g) & (lasts[b] >= g)).astype(jnp.int32)
+            work[count] = BLANK + g
+            count = count + (count & 1)
+        for k in range(2 * PAIR):
+            work[count + k] = BLANK + groups[0]
+        work[WORK - 1] = count
 
 
 def state_layers_kernel(state, first_layers, last_layers):
@@ -314,8 +325,9 @@
     x = ((cell + 0.5) * (1.0 / (CY * NZ))).astype(jnp.int32)
     rest = cell.astype(jnp.int32) - x * (CY * NZ)
     y = ((rest.astype(F32) + 0.5) * (1.0 / NZ)).astype(jnp.int32)
-    high = x // ROWS
-    return high * (GROUP - ROWS) + y * ROWS + x, rest - y * NZ
+    turned = (x + TURN) & (CX - 1)
+    high = lax.shift_right_logical(turned, 3)
+    return high * (GROUP - ROWS) + y * ROWS + turned, rest - y * NZ
 
 
 def column_hits(columns):
@@ -323,17 +335,16 @@
     return jnp.where(place == columns, 1.0, 0.0).astype(BF16)
 
 
-def block_places(slots, block):
-    rows = [slot_columns(slots, block * BLOCK_ROWS + r) for r in range(BLOCK_ROWS)]
-    columns = jnp.concatenate([r[0] for r in rows], axis=1)
-    level = jnp.concatenate([r[1] for r in rows], axis=1)
-    here = lax.broadcasted_iota(jnp.int32, (NZ, BLOCK), 0) == level
-    return columns, here
-
-
-def block_values(slots, block, which):
-    rows = [slots[block * BLOCK_ROWS + r, which : which + 1, :] for r in range(BLOCK_ROWS)]
-    return jnp.concatenate(rows, axis=1)
+def pair_rows(blocks):
+    return [block * BLOCK_ROWS + r for block in blocks for r in range(BLOCK_ROWS)]
+
+
+def pair_places(slots, blocks, offsets):
+    places = [slot_columns(slots, row) for row in pair_rows(blocks)]
+    columns = [p[0] - offsets[k // BLOCK_ROWS] for k, p in enumerate(places)]
+    level = jnp.concatenate([p[1] for p in places], axis=1)
+    here = lax.broadcasted_iota(jnp.int32, (NZ, PAIR * BLOCK), 0) == level
+    return jnp.concatenate(columns, axis=1), here
 
 
 def each_product(work, together, body):
@@ -341,14 +352,21 @@
 
     def some(i, carry):
         for k in range(together):
-            item = i * together + k
-            code = work[item]
-            group = code & (GROUPS - 1)
-            offset = jnp.where(item < count, group * GROUP, -(1 << 20))
-            body(lax.shift_right_logical(code, GROUPS // 2), group, offset)
+            item = (i * together + k) * PAIR
+            codes = [work[item + p] for p in range(PAIR)]
+            group = codes[0] & (GROUPS - 1)
+            blocks = [lax.shift_right_logical(code & (BLANK - 1), GROUPS // 2) for code in codes]
+            live = [(item < count) & (code < BLANK) for code in codes]
+            body(blocks, group, [jnp.where(l, group * GROUP, -(1 << 20)) for l in live])
         return carry
 
-    lax.fori_loop(0, lax.shift_right_logical(count + together - 1, together // 2), some, 0)
+    lax.fori_loop(0, lax.shift_right_logical(count + PAIR * together - 1, together), some, 0)
+
+
+def group_rows(g):
+    if g == 0:
+        return ((CX - TURN, 0, TURN), (0, TURN, ROWS - TURN))
+    return ((ROWS * g - TURN, 0, ROWS),)
 
 
 def fold(owners, line):
@@ -412,7 +430,9 @@
         for c in range(3):
             base = (3 * n + c) * NZ
             for g in range(GROUPS):
-                rows = field[c, RIM : RIM + CY, PAD + ROWS * g : PAD + ROWS * g + ROWS, :]
+                layers = slice(RIM, RIM + CY)
+                parts = [field[c, layers, PAD + x : PAD + x + count, :] for x, _, count in group_rows(g)]
+                rows = parts[0] if len(parts) == 1 else jnp.concatenate(parts, axis=1)
                 turned = rows.reshape(GROUP, LANES).T[0:NZ]
                 high = turned.astype(BF16)
                 table[g, base : base + NZ, :] = high
@@ -420,21 +440,24 @@
 
     seen[...] = jnp.zeros(seen.shape, F32)
 
-    def gather(block, group, offset):
-        columns, here = block_places(slots, block)
-        found = jnp.dot(table[group], column_hits(columns - offset), preferred_element_type=F32)
-        weights = [block_values(slots, block, 5 + c) for c in range(3)]
+    def gather(blocks, group, offsets):
+        columns, here = pair_places(slots, blocks, offsets)
+        found = jnp.dot(table[group], column_hits(columns), preferred_element_type=F32)
+        lines = pair_rows(blocks)
+        weights = [
+            jnp.concatenate([slots[line, 5 + c : 6 + c, :] for line in lines], axis=1) for c in range(3)
+        ]
         for n in range(STEPS):
-            total = jnp.zeros((1, BLOCK), F32)
+            total = jnp.zeros((1, PAIR * BLOCK), F32)
             for c in range(3):
                 base = (3 * n + c) * NZ
                 both = found[base : base + NZ] + found[half + base : half + base + NZ]
                 value = jnp.sum(jnp.where(here, both, 0.0), axis=0, keepdims=True)
                 total = total + weights[c] * value
-            for r in range(BLOCK_ROWS):
-                seen[n, pl.ds(block * BLOCK_ROWS + r, 1), :] += total[:, LANES * r : LANES * r + LANES]
-
-    each_product(work, TOGETHER, gather)
+            for r, line in enumerate(lines):
+                seen[n, pl.ds(line, 1), :] += total[:, LANES * r : LANES * r + LANES]
+
+    each_product(work, GATHERS, gather)
 
     owners = sums.shape[0]
     apart = LANES // owners
@@ -452,30 +475,29 @@
         sums[:, :, span] = jnp.broadcast_to(total[None], (owners, 1, LANES))
 
 
-def scatter_slots(part_of, together, work, slots, weight, total, force):
+def scatter_slots(first_group, together, work, slots, weight, total, force):
     total[...] = jnp.zeros(total.shape, F32)
     half = FIELDS * NZ
 
-    def scatter(block, group, offset):
-        columns, here = block_places(slots, block)
+    def scatter(blocks, group, offsets):
+        columns, here = pair_places(slots, blocks, offsets)
+        lines = pair_rows(blocks)
         high_rows, low_rows = [], []
         for f in range(FIELDS):
-            value = jnp.concatenate(
-                [weight[f, pl.ds(block * BLOCK_ROWS + r, 1), :] for r in range(BLOCK_ROWS)], axis=1
-            )
+            value = jnp.concatenate([weight[f, pl.ds(line, 1), :] for line in lines], axis=1)
             high = value.astype(BF16).astype(F32)
             high_rows.append(jnp.where(here, high, 0.0).astype(BF16))
             low_rows.append(jnp.where(here, value - high, 0.0).astype(BF16))
         table = jnp.concatenate(high_rows + low_rows, axis=0)
-        hits = column_hits(columns - offset)
+        hits = column_hits(columns)
         added = lax.dot_general(table, hits, (((1,), (1,)), ((), ())), preferred_element_type=F32)
-        part = part_of(group)
+        part = group - first_group
         for f in range(FIELDS):
             total[part, f, 0:NZ, :] += added[NZ * f : NZ * f + NZ] + added[half + NZ * f : half + NZ * f + NZ]
 
     each_product(work, together, scatter)
     for f in range(FIELDS):
-        for k in range(2):
+        for k in range(force.shape[1]):
             force[f, k] = total[k, f].T.reshape(CY, ROWS, LANES)
 
 
@@ -497,19 +519,19 @@
         misfit = seen[n] - mean - slots[:, 2 + n, :]
         for c in range(3):
             weight[3 * n + c] = slots[:, 5 + c, :] * misfit
-    scatter_slots(lambda g: (g == GROUPS - 1).astype(jnp.int32), 2, work, slots, weight, total, force)
-    for out, k, row_of in ((first_rows, 0, lambda i: i), (last_rows, 1, lambda i: ROWS - 1 - i)):
+    scatter_slots(0, OUTERS, work, slots, weight, total, force)
+    for out, row_of in ((first_rows, lambda i: TURN + i), (last_rows, lambda i: TURN - 1 - i)):
         for b, (n, c, i) in enumerate(FORCE_BLOCKS):
 
             def put(row, rows, b=b, out=out):
                 out[b, row : row + 8, :] = rows
 
-            pack(put, force[3 * n + c, k, :, row_of(i), :])
+            pack(put, force[3 * n + c, 0, :, row_of(i), :])
     to_partners("gx", first_rows, last_rows, near, far)
 
 
 def inner_force_kernel(work, slots, weight, force, total):
-    scatter_slots(lambda g: (g == 2).astype(jnp.int32), TOGETHER, work, slots, weight, total, force)
+    scatter_slots(1, INNERS, work, slots, weight, total, force)
 
 
 def force_rim_kernel(outer, inner, x_near, x_far, near, far, first_layers, last_layers, before, after):
@@ -522,7 +544,9 @@
                 out[b * PACKED + row : b * PACKED + row + 8, :] = rows
 
             f, y = 3 * n + c, layer_of(i + 1)
-            pack(put, jnp.concatenate([outer[f, 0, y], inner[f, 0, y], inner[f, 1, y], outer[f, 1, y]], axis=0))
+            ends = outer[f, 0, y]
+            middle = [inner[f, k, y] for k in range(GROUPS - 1)]
+            pack(put, jnp.concatenate([ends[TURN:ROWS]] + middle + [ends[0:TURN]], axis=0))
         base = len(FORCE_BLOCKS) * PACKED
         for row, (n, c, dist, side, k) in enumerate(FORCE_CORNERS):
             piece = (before, after)[side]
@@ -593,9 +617,10 @@
     for n in range(STEPS):
         adjoints[n][...] = jnp.zeros(adjoints[n].shape, F32)
         for c in range(3):
-            for g, (force, k) in enumerate(((outer, 0), (inner, 0), (inner, 1), (outer, 1))):
-                row = PAD + ROWS * g
-                adjoints[n][c, FRIM : FRIM + CY, row : row + ROWS, :] = force[3 * n + c, k]
+            for g in range(GROUPS):
+                force = outer[3 * n + c, 0] if g == 0 else inner[3 * n + c, g - 1]
+                for x, row, count in group_rows(g):
+                    adjoints[n][c, FRIM : FRIM + CY, PAD + x : PAD + x + count, :] = force[:, row : row + count]
     for b, (n, c, i) in enumerate(FORCE_BLOCKS):
         adjoints[n][c, FRIM : FRIM + CY, PAD - 1 - i, :] = unpack(before[b])
         adjoints[n][c, FRIM : FRIM + CY, PAD + CX + i, :] = unpack(after[b])
@@ -710,18 +735,18 @@
     )(every_work, initial_state, x_near, x_far, y_near, y_far, slots)
     sums = lax.all_to_all(sums, AXES, split_axis=0, concat_axis=0, tiled=True)
     x_rim = (len(FORCE_BLOCKS), PACKED, LANES)
-    part = shape(FIELDS, 2, CY, ROWS, LANES)
-    total = pltpu.VMEM((2, FIELDS, LANES, GROUP), F32)
+    parts = [shape(FIELDS, count, CY, ROWS, LANES) for count in (1, GROUPS - 1)]
+    totals = [pltpu.VMEM((count, FIELDS, LANES, GROUP), F32) for count in (1, GROUPS - 1)]
     outer, weight, near, far = call(
         functools.partial(outer_force_kernel, beams),
-        (part, shape(FIELDS, rows, LANES), shape(*x_rim), shape(*x_rim)),
-        [pltpu.VMEM(x_rim, F32)] * 2 + [total],
+        (parts[0], shape(FIELDS, rows, LANES), shape(*x_rim), shape(*x_rim)),
+        [pltpu.VMEM(x_rim, F32)] * 2 + [totals[0]],
         limit=24,
         ins=4,
         scalar_in=(0,),
     )(outer_work, slots, seen, sums)
     x_near, x_far = swap(near, far, "gx")
-    inner = call(inner_force_kernel, part, [total], limit=24, ins=3, scalar_in=(0,), micros=6)(
+    inner = call(inner_force_kernel, parts[1], [totals[1]], limit=24, ins=3, scalar_in=(0,), micros=6)(
         inner_work, slots, weight
     )
     y_rim = (FORCE_PIECE, LANES)

time: 84.3 us -> 82 us (0.973)
  Pallas kernels: 45.8 us -> 49.3 us
  starting transfers between devices: 23.5 us -> 20.4 us
  blocking collectives: 11.7 us -> 9.44 us
  waiting for transfers between devices: 3.7 us -> 2.7 us
    pallas_call x1, Pallas kernels: 13.9 us -> 17.1 us  [local(): call(functools.partial(forward_kernel, beams), (shape(STEPS, rows, LANES)...]
    all_to_all x1, blocking collectives: 11.7 us -> 9.44 us  [local(): sums = lax.all_to_all(sums, AXES, split_axis=0, concat_axis=0, tiled=True)]
    ppermute x4, starting transfers between devices: 12.9 us -> 11.1 us  [swap(): lax.ppermute(far, axis, pairs(1))]
    ppermute x4, starting transfers between devices: 3.36 us -> 2.14 us  [swap(): lax.ppermute(near, axis, pairs(0))]
    ppermute x4, waiting for transfers between devices: 1.31 us -> 0.32 us  [swap(): lax.ppermute(far, axis, pairs(1))]
  transfers between devices with their start and end apart: 9 -> 9, of which waited for: 3 -> 2; matrix products, arithmetic and copies ran while one was open for 0% -> 0% of each run, Pallas kernels for 24% -> 29%
where the time goes in v6:
time: 82 us
  Pallas kernels  49.3 us (60%)
  starting transfers between devices  20.4 us (25%)
  blocking collectives  9.44 us (12%)
  waiting for transfers between devices  2.7 us (3%)
    pallas_call x1, Pallas kernels, local(): call(functools.partial(forward_kernel, beams), (shape(STEPS, rows, LANES)...  17.1 us
    ppermute x4, starting transfers between devices, swap(): lax.ppermute(far, axis, pairs(1))  11.1 us
    pallas_call x1, Pallas kernels, local(): call(inner_force_kernel, parts[1], [totals[1]], limit=24, ins=3, scalar_i...  10.3 us
    all_to_all x1, blocking collectives, local(): sums = lax.all_to_all(sums, AXES, split_axis=0, concat_axis=0, tiled=True)  9.44 us
    pallas_call x1, Pallas kernels, local(): call(inner_backward_kernel, (whole, edges, edges, edges), [adjoint] * 4 +...  8.13 us
    all_to_all x1, starting transfers between devices, local(): slots = lax.all_to_all(slots, AXES, split_axis=0, concat_axis=0, tiled=True)  7.22 us
    pallas_call x1, Pallas kernels, local(): call(functools.partial(outer_force_kernel, beams), (parts[0], shape(FIELD...  3.78 us
    pallas_call x1, Pallas kernels, local(): call(arrange_kernel, shape(*lists), [pltpu.VMEM(lists, F32), pltpu.VMEM((...  2.72 us
  transfers between devices with their start and end apart: 9, of which 2 were waited for; matrix products, arithmetic and copies ran while one was open for 0% of the time, Pallas kernels for 29%

profile of v6, /device:TPU:5, one launch (start us, length us, event | category | flops | bytes accessed | tf_op | source)
XLA Modules:
  0.0 82.0 jit_solution(247510772822899851)
XLA Ops:
  0.0 0.0 copy-start
  0.0 2.0 %shard_map.57 = (f32[16,3072]{1,0:T(8,128)}, f32[16,3072]{1,0:T(8,128)}) custom-call(f32[3,32,3072]{2,1,0:T(8,128)} %state.3, f32[3,32,3072]{2,1,0:T(8,128)} %state.3), custom_call_target="tpu_custom_call" | custom-call | tf_op jit(solution)/shard_map/pallas_call | solution.py:683
  2.0 1.2 %collective-permute-start = (f32[16,3072]{1,0:T(8,128)}, f32[16,3072]{1,0:T(8,128)S(1)}, u32[]{:S(2)}, u32[]{:S(2)}) collective-permute-start(f32[16,3072]{1,0:T(8,128)} %get-tuple-element.33), channel_id=1, source_target_pairs={{0,8},{16,24},{8,0},{24,16},{1,9},{17,25},{9,1},{25,17},{2,10},{18... | collective-permute-start | bytes 589832 | tf_op jit(solution)/shard_map/ppermute | solution.py:674
  3.2 1.9 %collective-permute-start.1 = (f32[16,3072]{1,0:T(8,128)}, f32[16,3072]{1,0:T(8,128)S(1)}, u32[]{:S(2)}, u32[]{:S(2)}) collective-permute-start(f32[16,3072]{1,0:T(8,128)} %get-tuple-element.34), channel_id=1, source_target_pairs={{8,16},{16,8},{9,17},{17,9},{10,18},{18,10},{11,19},{19,11},{12,20... | collective-permute-start | bytes 589832 | tf_op jit(solution)/shard_map/ppermute | solution.py:674
  5.1 2.7 %shard_map.55 = f32[32,8,128]{2,1,0:T(8,128)} custom-call(f32[3,4]{1,0:T(4,128)} %beam_dir.1, f32[3,1,32,128]{3,2,1,0:T(8,128)} %obs.1, s32[1,32,128]{2,1,0:T(8,128)} %beam.1, s32[1,32,128]{2,1,0:T(8,128)} %cell.1), custom_call_target="tpu_custom_call" | custom-call | bytes 3000000 | tf_op jit(solution)/shard_map/pallas_call | solution.py:697
  7.9 7.2 %all-to-all-start = ((f32[32,8,128]{2,1,0:T(8,128)}), f32[32,8,128]{2,1,0:T(8,128)S(1)}, u32[]{:S(2)}, u32[]{:S(2)}) async-start(f32[32,8,128]{2,1,0:T(8,128)} %shard_map.55), calls=%async_computation | async-start | bytes 262144 | tf_op jit(solution)/shard_map/all_to_all | solution.py:704
  15.1 0.0 copy-done
  15.1 0.9 %shard_map.58 = (f32[360,128]{1,0:T(8,128)S(1)}, f32[360,128]{1,0:T(8,128)S(1)}) custom-call(f32[3,32,3072]{2,1,0:T(8,128)S(1)} %copy-done), custom_call_target="tpu_custom_call" | custom-call | bytes 3000000 | tf_op jit(solution)/shard_map/pallas_call | solution.py:716
  16.0 0.0 collective-permute-done.x_near
  16.1 0.0 collective-permute-done.1.x_far
  16.1 0.2 shard_map.59
  16.2 0.4 collective-permute-start.2
  16.7 3.1 %collective-permute-start.3 = (f32[424,128]{1,0:T(8,128)S(1)}, f32[424,128]{1,0:T(8,128)S(1)}, u32[]{:S(2)}, u32[]{:S(2)}) collective-permute-start(f32[424,128]{1,0:T(8,128)S(1)} %get-tuple-element.38), channel_id=1, source_target_pairs={{1,2},{3,4},{5,6},{2,1},{4,3},{6,5},{9,10},{11,12},{13,14},{10,9},... | collective-permute-start | bytes 651272 | tf_op jit(solution)/shard_map/ppermute | solution.py:674
  19.8 2.4 %all-to-all-done.received = f32[32,8,128]{2,1,0:T(8,128)S(1)} async-done(((f32[32,8,128]{2,1,0:T(8,128)}), f32[32,8,128]{2,1,0:T(8,128)S(1)}, u32[]{:S(2)}, u32[]{:S(2)}) %all-to-all-start) | async-done | bytes 131104 | tf_op jit(solution)/shard_map/all_to_all | solution.py:704
  22.2 1.4 %shard_map.56 = (f32[32,8,128]{2,1,0:T(8,128)S(1)}, s32[128]{0:T(128)S(1)}, s32[128]{0:T(128)S(1)}, s32[128]{0:T(128)S(1)}) custom-call(f32[32,8,128]{2,1,0:T(8,128)S(1)} %all-to-all-done.received), custom_call_target="tpu_custom_call" | custom-call | bytes 6000000 | tf_op jit(solution)/shard_map/pallas_call | solution.py:706
  23.6 0.0 collective-permute-done.2.y_near
  23.6 0.3 collective-permute-done.3.y_far
  23.9 17.1 %shard_map.60 = (f32[3,32,128]{2,1,0:T(8,128)S(1)}, f32[32,1,384]{2,1,0:T(1,128)S(1)}, f32[3,42,48,128]{3,2,1,0:T(8,128)S(1)}, f32[3,42,48,128]{3,2,1,0:T(8,128)S(1)}, f32[3,42,48,128]{3,2,1,0:T(8,128)S(1)}) custom-call(s32[128]{0:T(128)S(1)} %get-tuple-element.32.work, f32[3,32,3072]{2,1,0:T(8,128)S(1)} %copy-done, ...), custom_call_target="tpu_custom_call" | custom-call | bytes 3000000 | tf_op jit(solution)/shard_map/pallas_call | solution.py:726
  40.9 9.4 %all_to_all.10.sums = f32[32,1,384]{2,1,0:T(1,128)S(1)} all-to-all(f32[32,1,384]{2,1,0:T(1,128)S(1)} %get-tuple-element.40), channel_id=1, replica_groups=mesh['gx'=4,'gy'=8] {'gx','gy'}, dimensions={0} | all-to-all | bytes 98304 | tf_op jit(solution)/shard_map/all_to_all | solution.py:736
  50.4 3.8 %shard_map.61 = (f32[9,1,32,8,128]{4,3,2,1,0:T(8,128)S(1)}, f32[9,32,128]{2,1,0:T(8,128)S(1)}, f32[18,24,128]{2,1,0:T(8,128)S(1)}, f32[18,24,128]{2,1,0:T(8,128)S(1)}) custom-call(s32[128]{0:T(128)S(1)} %get-tuple-element.30.work, f32[32,8,128]{2,1,0:T(8,128)S(1)} %get-tuple-element.31.slots, f32[3,32,128]{2,1,0:T(8,128)S(1)} %get-tuple-element.39.seen, ...), custom_call_target="tpu_custom_call" | custom-call | bytes 3000000 | tf_op jit(solution)/shard_map/pallas_call | solution.py:740
  54.2 0.4 collective-permute-start.4
  54.6 3.9 %collective-permute-start.5 = (f32[18,24,128]{2,1,0:T(8,128)S(1)}, f32[18,24,128]{2,1,0:T(8,128)S(1)}, u32[]{:S(2)}, u32[]{:S(2)}) collective-permute-start(f32[18,24,128]{2,1,0:T(8,128)S(1)} %get-tuple-element.45), channel_id=1, source_target_pairs={{8,16},{16,8},{9,17},{17,9},{10,18},{18,10},{11,19},{19,11},{12,20... | collective-permute-start | bytes 663560 | tf_op jit(solution)/shard_map/ppermute | solution.py:674
  58.5 10.3 %shard_map.62.inner = f32[9,3,32,8,128]{4,3,2,1,0:T(8,128)S(1)} custom-call(s32[128]{0:T(128)S(1)} %get-tuple-element.42.work, f32[32,8,128]{2,1,0:T(8,128)S(1)} %get-tuple-element.31.slots, f32[9,32,128]{2,1,0:T(8,128)S(1)} %get-tuple-element.43.weight), custom_call_target="tpu_custom_call" | custom-call | bytes 18000000 | tf_op jit(solution)/shard_map/pallas_call | solution.py:749
  68.8 0.0 collective-permute-done.4.x_near
  68.9 0.0 collective-permute-done.5.x_far
  68.9 0.3 shard_map.64
  69.1 0.1 collective-permute-start.6
  69.2 2.1 %collective-permute-start.7 = (f32[456,128]{1,0:T(8,128)S(1)}, f32[456,128]{1,0:T(8,128)S(1)}, u32[]{:S(2)}, u32[]{:S(2)}) collective-permute-start(f32[456,128]{1,0:T(8,128)S(1)} %get-tuple-element.54), channel_id=1, source_target_pairs={{1,2},{3,4},{5,6},{2,1},{4,3},{6,5},{9,10},{11,12},{13,14},{10,9},... | collective-permute-start | bytes 700424 | tf_op jit(solution)/shard_map/ppermute | solution.py:674
  71.3 8.1 %shard_map.63 = (f32[3,32,3072]{2,1,0:T(8,128)S(1)}, f32[3,2,4,48,128]{4,3,2,1,0:T(8,128)S(1)}, f32[3,2,4,48,128]{4,3,2,1,0:T(8,128)S(1)}, f32[3,2,4,48,128]{4,3,2,1,0:T(8,128)S(1)}) custom-call(f32[9,1,32,8,128]{4,3,2,1,0:T(8,128)S(1)} %get-tuple-element.41.outer, f32[9,3,32,8,128]{4,3,2,1,0:T(8,128)S(1)} %shard_map.62.inner, ...), custom_call_target="tpu_custom_call" | custom-call | bytes 24000000 | tf_op jit(solution)/shard_map/pallas_call | solution.py:763
  79.5 0.0 collective-permute-done.6.y_near
  79.5 0.0 collective-permute-done.7.y_far
  79.5 2.5 %shard_map.65 = f32[3,32,3072]{2,1,0:T(8,128)} custom-call(f32[3,32,3072]{2,1,0:T(8,128)S(1)} %get-tuple-element.49.part, f32[3,2,4,48,128]{4,3,2,1,0:T(8,128)S(1)} %get-tuple-element.50.e1, f32[3,2,4,48,128]{4,3,2,1,0:T(8,128)S(1)} %get-tuple-element.51.e2, f32[3,2,4,48,128]{4,3,2,1,0:T(8,128)S(1)} %get-tuple-element.52.e3, ...), custom_call_target="tpu_custom_call" | custom-call | bytes 3000000 | tf_op jit(solution)/shard_map/pallas_call | solution.py:771
Async XLA Ops:
  0.0 15.1 %copy-start = (f32[3,32,3072]{2,1,0:T(8,128)S(1)}, f32[3,32,3072]{2,1,0:T(8,128)}, u32[]{:S(2)}) copy-start(f32[3,32,3072]{2,1,0:T(8,128)} %state.3) | copy-start | bytes 3538948
  2.0 14.0 %collective-permute-start = (f32[16,3072]{1,0:T(8,128)}, f32[16,3072]{1,0:T(8,128)S(1)}, u32[]{:S(2)}, u32[]{:S(2)}) collective-permute-start(f32[16,3072]{1,0:T(8,128)} %get-tuple-element.33), channel_id=1, source_target_pairs={{0,8},{16,24},{8,0},{24,16},{1,9},{17,25},{9,1},{25,17},{2,10},{18... | collective-permute-start | bytes 589832 | tf_op jit(solution)/shard_map/ppermute | solution.py:674
  3.2 12.8 %collective-permute-start.1 = (f32[16,3072]{1,0:T(8,128)}, f32[16,3072]{1,0:T(8,128)S(1)}, u32[]{:S(2)}, u32[]{:S(2)}) collective-permute-start(f32[16,3072]{1,0:T(8,128)} %get-tuple-element.34), channel_id=1, source_target_pairs={{8,16},{16,8},{9,17},{17,9},{10,18},{18,10},{11,19},{19,11},{12,20... | collective-permute-start | bytes 589832 | tf_op jit(solution)/shard_map/ppermute | solution.py:674
  7.9 14.3 %all-to-all-start = ((f32[32,8,128]{2,1,0:T(8,128)}), f32[32,8,128]{2,1,0:T(8,128)S(1)}, u32[]{:S(2)}, u32[]{:S(2)}) async-start(f32[32,8,128]{2,1,0:T(8,128)} %shard_map.55), calls=%async_computation | async-start | bytes 262144 | tf_op jit(solution)/shard_map/all_to_all | solution.py:704
  16.2 7.3 %collective-permute-start.2 = (f32[424,128]{1,0:T(8,128)S(1)}, f32[424,128]{1,0:T(8,128)S(1)}, u32[]{:S(2)}, u32[]{:S(2)}) collective-permute-start(f32[424,128]{1,0:T(8,128)S(1)} %get-tuple-element.37), channel_id=1, source_target_pairs={{0,1},{2,3},{4,5},{6,7},{1,0},{3,2},{5,4},{7,6},{8,9},{10,11},{12,... | collective-permute-start | bytes 651272 | tf_op jit(solution)/shard_map/ppermute | solution.py:674
  16.7 7.2 %collective-permute-start.3 = (f32[424,128]{1,0:T(8,128)S(1)}, f32[424,128]{1,0:T(8,128)S(1)}, u32[]{:S(2)}, u32[]{:S(2)}) collective-permute-start(f32[424,128]{1,0:T(8,128)S(1)} %get-tuple-element.38), channel_id=1, source_target_pairs={{1,2},{3,4},{5,6},{2,1},{4,3},{6,5},{9,10},{11,12},{13,14},{10,9},... | collective-permute-start | bytes 651272 | tf_op jit(solution)/shard_map/ppermute | solution.py:674
  54.2 14.7 %collective-permute-start.4 = (f32[18,24,128]{2,1,0:T(8,128)S(1)}, f32[18,24,128]{2,1,0:T(8,128)S(1)}, u32[]{:S(2)}, u32[]{:S(2)}) collective-permute-start(f32[18,24,128]{2,1,0:T(8,128)S(1)} %get-tuple-element.44), channel_id=1, source_target_pairs={{0,8},{16,24},{8,0},{24,16},{1,9},{17,25},{9,1},{25,17},{2,10},{18... | collective-permute-start | bytes 663560 | tf_op jit(solution)/shard_map/ppermute | solution.py:674
  54.6 14.3 %collective-permute-start.5 = (f32[18,24,128]{2,1,0:T(8,128)S(1)}, f32[18,24,128]{2,1,0:T(8,128)S(1)}, u32[]{:S(2)}, u32[]{:S(2)}) collective-permute-start(f32[18,24,128]{2,1,0:T(8,128)S(1)} %get-tuple-element.45), channel_id=1, source_target_pairs={{8,16},{16,8},{9,17},{17,9},{10,18},{18,10},{11,19},{19,11},{12,20... | collective-permute-start | bytes 663560 | tf_op jit(solution)/shard_map/ppermute | solution.py:674
  69.1 10.3 %collective-permute-start.6 = (f32[456,128]{1,0:T(8,128)S(1)}, f32[456,128]{1,0:T(8,128)S(1)}, u32[]{:S(2)}, u32[]{:S(2)}) collective-permute-start(f32[456,128]{1,0:T(8,128)S(1)} %get-tuple-element.53), channel_id=1, source_target_pairs={{0,1},{2,3},{4,5},{6,7},{1,0},{3,2},{5,4},{7,6},{8,9},{10,11},{12,... | collective-permute-start | bytes 700424 | tf_op jit(solution)/shard_map/ppermute | solution.py:674
  69.2 10.3 %collective-permute-start.7 = (f32[456,128]{1,0:T(8,128)S(1)}, f32[456,128]{1,0:T(8,128)S(1)}, u32[]{:S(2)}, u32[]{:S(2)}) collective-permute-start(f32[456,128]{1,0:T(8,128)S(1)} %get-tuple-element.54), channel_id=1, source_target_pairs={{1,2},{3,4},{5,6},{2,1},{4,3},{6,5},{9,10},{11,12},{13,14},{10,9},... | collective-permute-start | bytes 700424 | tf_op jit(solution)/shard_map/ppermute | solution.py:674

commit v7 on v6

--- a/solution.py
+++ b/solution.py
@@ -23,7 +23,6 @@
 FH = CY + 2 * FRIM
 EDGE = 4
 FIELDS = 3 * STEPS
-UNROLL = 8
 ROWS = 8
 TURN = 4
 GROUPS = CX // ROWS
@@ -308,7 +307,7 @@
             dst[c, y + RIM, here, :] = total
         return carry
 
-    lax.fori_loop(0, high - low, layer, 0, unroll=UNROLL)
+    lax.fori_loop(0, high - low, layer, 0, unroll=True)
 
 
 def mesh_places():
@@ -477,7 +476,6 @@
 
 def scatter_slots(first_group, together, work, slots, weight, total, force):
     total[...] = jnp.zeros(total.shape, F32)
-    half = FIELDS * NZ
 
     def scatter(blocks, group, offsets):
         columns, here = pair_places(slots, blocks, offsets)
@@ -488,12 +486,15 @@
             high = value.astype(BF16).astype(F32)
             high_rows.append(jnp.where(here, high, 0.0).astype(BF16))
             low_rows.append(jnp.where(here, value - high, 0.0).astype(BF16))
-        table = jnp.concatenate(high_rows + low_rows, axis=0)
+        table = jnp.concatenate(
+            [jnp.concatenate(high_rows, axis=0), jnp.concatenate(low_rows, axis=0)], axis=1
+        )
         hits = column_hits(columns)
+        hits = jnp.concatenate([hits, hits], axis=1)
         added = lax.dot_general(table, hits, (((1,), (1,)), ((), ())), preferred_element_type=F32)
         part = group - first_group
         for f in range(FIELDS):
-            total[part, f, 0:NZ, :] += added[NZ * f : NZ * f + NZ] + added[half + NZ * f : half + NZ * f + NZ]
+            total[part, f, 0:NZ, :] += added[NZ * f : NZ * f + NZ]
 
     each_product(work, together, scatter)
     for f in range(FIELDS):
@@ -599,7 +600,7 @@
             target[c, y + FRIM, here, :] = total
         return carry
 
-    lax.fori_loop(0, high - low, layer, 0, unroll=min(UNROLL, high - low))
+    lax.fori_loop(0, high - low, layer, 0, unroll=True)
 
 
 def edge_layers(side):
@@ -615,7 +616,9 @@
     mask[...] = row_mask(places[0], places[1])
     adjoints = (a1, a2, a3)
     for n in range(STEPS):
-        adjoints[n][...] = jnp.zeros(adjoints[n].shape, F32)
+        layers = slice(FRIM, FRIM + CY)
+        adjoints[n][:, layers, 0:PAD] = jnp.zeros((3, CY, PAD, LANES), F32)
+        adjoints[n][:, layers, PAD + CX : XH] = jnp.zeros((3, CY, PAD, LANES), F32)
         for c in range(3):
             for g in range(GROUPS):
                 force = outer[3 * n + c, 0] if g == 0 else inner[3 * n + c, g - 1]

time: 82 us -> 78.8 us (0.961)
  Pallas kernels: 49.3 us -> 41.2 us
  blocking collectives: 9.44 us -> 11.6 us
  starting transfers between devices: 20.4 us -> 22.2 us
    pallas_call x1, Pallas kernels: 10.3 us -> 7.13 us  [local(): call(inner_force_kernel, parts[1], [totals[1]], limit=24, ins=3, scalar_i...]
    pallas_call x1, Pallas kernels: 17.1 us -> 14 us  [local(): call(functools.partial(forward_kernel, beams), (shape(STEPS, rows, LANES)...]
    all_to_all x1, blocking collectives: 9.44 us -> 11.6 us  [local(): sums = lax.all_to_all(sums, AXES, split_axis=0, concat_axis=0, tiled=True)]
    pallas_call x1, Pallas kernels: 8.13 us -> 6.39 us  [local(): call(inner_backward_kernel, (whole, edges, edges, edges), [adjoint] * 4 +...]
    ppermute x4, starting transfers between devices: 2.14 us -> 3.36 us  [swap(): lax.ppermute(near, axis, pairs(0))]
  transfers between devices with their start and end apart: 9 -> 9, of which waited for: 2 -> 3; matrix products, arithmetic and copies ran while one was open for 0% -> 0% of each run, Pallas kernels for 29% -> 24%
where the time goes in v7:
time: 78.8 us; the launch traced here: 78.5 us
  Pallas kernels  41.2 us (52%)
  starting transfers between devices  22.2 us (28%)
  blocking collectives  11.6 us (15%)
  waiting for transfers between devices  3.36 us (4%)
    pallas_call x1, Pallas kernels, local(): call(functools.partial(forward_kernel, beams), (shape(STEPS, rows, LANES)...  14 us
    all_to_all x1, blocking collectives, local(): sums = lax.all_to_all(sums, AXES, split_axis=0, concat_axis=0, tiled=True)  11.6 us
    ppermute x4, starting transfers between devices, swap(): lax.ppermute(far, axis, pairs(1))  11.6 us
    all_to_all x1, starting transfers between devices, local(): slots = lax.all_to_all(slots, AXES, split_axis=0, concat_axis=0, tiled=True)  7.22 us
    pallas_call x1, Pallas kernels, local(): call(inner_force_kernel, parts[1], [totals[1]], limit=24, ins=3, scalar_i...  7.13 us
    pallas_call x1, Pallas kernels, local(): call(inner_backward_kernel, (whole, edges, edges, edges), [adjoint] * 4 +...  6.39 us
    pallas_call x1, Pallas kernels, local(): call(functools.partial(outer_force_kernel, beams), (parts[0], shape(FIELD...  3.66 us
    ppermute x4, starting transfers between devices, swap(): lax.ppermute(near, axis, pairs(0))  3.36 us
  transfers between devices with their start and end apart: 9, of which 3 were waited for; matrix products, arithmetic and copies ran while one was open for 0% of the time, Pallas kernels for 24%

profile of v7, /device:TPU:5, one launch (start us, length us, event | category | flops | bytes accessed | tf_op | source)
XLA Modules:
  0.0 78.5 jit_solution(14891089272446492815)
XLA Ops:
  0.0 0.0 copy-start
  0.0 2.0 %shard_map.57 = (f32[16,3072]{1,0:T(8,128)}, f32[16,3072]{1,0:T(8,128)}) custom-call(f32[3,32,3072]{2,1,0:T(8,128)} %state.3, f32[3,32,3072]{2,1,0:T(8,128)} %state.3), custom_call_target="tpu_custom_call" | custom-call | tf_op jit(solution)/shard_map/pallas_call | solution.py:686
  2.0 1.2 %collective-permute-start = (f32[16,3072]{1,0:T(8,128)}, f32[16,3072]{1,0:T(8,128)S(1)}, u32[]{:S(2)}, u32[]{:S(2)}) collective-permute-start(f32[16,3072]{1,0:T(8,128)} %get-tuple-element.33), channel_id=1, source_target_pairs={{0,8},{16,24},{8,0},{24,16},{1,9},{17,25},{9,1},{25,17},{2,10},{18... | collective-permute-start | bytes 589832 | tf_op jit(solution)/shard_map/ppermute | solution.py:677
  3.2 1.9 %collective-permute-start.1 = (f32[16,3072]{1,0:T(8,128)}, f32[16,3072]{1,0:T(8,128)S(1)}, u32[]{:S(2)}, u32[]{:S(2)}) collective-permute-start(f32[16,3072]{1,0:T(8,128)} %get-tuple-element.34), channel_id=1, source_target_pairs={{8,16},{16,8},{9,17},{17,9},{10,18},{18,10},{11,19},{19,11},{12,20... | collective-permute-start | bytes 589832 | tf_op jit(solution)/shard_map/ppermute | solution.py:677
  5.1 2.7 %shard_map.55 = f32[32,8,128]{2,1,0:T(8,128)} custom-call(f32[3,4]{1,0:T(4,128)} %beam_dir.1, f32[3,1,32,128]{3,2,1,0:T(8,128)} %obs.1, s32[1,32,128]{2,1,0:T(8,128)} %beam.1, s32[1,32,128]{2,1,0:T(8,128)} %cell.1), custom_call_target="tpu_custom_call" | custom-call | bytes 3000000 | tf_op jit(solution)/shard_map/pallas_call | solution.py:700
  7.9 7.2 %all-to-all-start = ((f32[32,8,128]{2,1,0:T(8,128)}), f32[32,8,128]{2,1,0:T(8,128)S(1)}, u32[]{:S(2)}, u32[]{:S(2)}) async-start(f32[32,8,128]{2,1,0:T(8,128)} %shard_map.55), calls=%async_computation | async-start | bytes 262144 | tf_op jit(solution)/shard_map/all_to_all | solution.py:707
  15.1 0.0 copy-done
  15.1 0.9 %shard_map.58 = (f32[360,128]{1,0:T(8,128)S(1)}, f32[360,128]{1,0:T(8,128)S(1)}) custom-call(f32[3,32,3072]{2,1,0:T(8,128)S(1)} %copy-done), custom_call_target="tpu_custom_call" | custom-call | bytes 3000000 | tf_op jit(solution)/shard_map/pallas_call | solution.py:719
  16.0 0.0 collective-permute-done.x_near
  16.1 0.0 collective-permute-done.1.x_far
  16.1 0.2 shard_map.59
  16.2 0.4 collective-permute-start.2
  16.7 3.1 %collective-permute-start.3 = (f32[424,128]{1,0:T(8,128)S(1)}, f32[424,128]{1,0:T(8,128)S(1)}, u32[]{:S(2)}, u32[]{:S(2)}) collective-permute-start(f32[424,128]{1,0:T(8,128)S(1)} %get-tuple-element.38), channel_id=1, source_target_pairs={{1,2},{3,4},{5,6},{2,1},{4,3},{6,5},{9,10},{11,12},{13,14},{10,9},... | collective-permute-start | bytes 651272 | tf_op jit(solution)/shard_map/ppermute | solution.py:677
  19.8 2.4 %all-to-all-done.received = f32[32,8,128]{2,1,0:T(8,128)S(1)} async-done(((f32[32,8,128]{2,1,0:T(8,128)}), f32[32,8,128]{2,1,0:T(8,128)S(1)}, u32[]{:S(2)}, u32[]{:S(2)}) %all-to-all-start) | async-done | bytes 131104 | tf_op jit(solution)/shard_map/all_to_all | solution.py:707
  22.2 1.4 %shard_map.56 = (f32[32,8,128]{2,1,0:T(8,128)S(1)}, s32[128]{0:T(128)S(1)}, s32[128]{0:T(128)S(1)}, s32[128]{0:T(128)S(1)}) custom-call(f32[32,8,128]{2,1,0:T(8,128)S(1)} %all-to-all-done.received), custom_call_target="tpu_custom_call" | custom-call | bytes 6000000 | tf_op jit(solution)/shard_map/pallas_call | solution.py:709
  23.6 0.0 collective-permute-done.2.y_near
  23.6 0.3 collective-permute-done.3.y_far
  23.9 14.0 %shard_map.60 = (f32[3,32,128]{2,1,0:T(8,128)S(1)}, f32[32,1,384]{2,1,0:T(1,128)S(1)}, f32[3,42,48,128]{3,2,1,0:T(8,128)S(1)}, f32[3,42,48,128]{3,2,1,0:T(8,128)S(1)}, f32[3,42,48,128]{3,2,1,0:T(8,128)S(1)}) custom-call(s32[128]{0:T(128)S(1)} %get-tuple-element.32.work, f32[3,32,3072]{2,1,0:T(8,128)S(1)} %copy-done, ...), custom_call_target="tpu_custom_call" | custom-call | bytes 3000000 | tf_op jit(solution)/shard_map/pallas_call | solution.py:729
  37.8 11.6 %all_to_all.10.sums = f32[32,1,384]{2,1,0:T(1,128)S(1)} all-to-all(f32[32,1,384]{2,1,0:T(1,128)S(1)} %get-tuple-element.40), channel_id=1, replica_groups=mesh['gx'=4,'gy'=8] {'gx','gy'}, dimensions={0} | all-to-all | bytes 98304 | tf_op jit(solution)/shard_map/all_to_all | solution.py:739
  49.5 3.7 %shard_map.61 = (f32[9,1,32,8,128]{4,3,2,1,0:T(8,128)S(1)}, f32[9,32,128]{2,1,0:T(8,128)S(1)}, f32[18,24,128]{2,1,0:T(8,128)S(1)}, f32[18,24,128]{2,1,0:T(8,128)S(1)}) custom-call(s32[128]{0:T(128)S(1)} %get-tuple-element.30.work, f32[32,8,128]{2,1,0:T(8,128)S(1)} %get-tuple-element.31.slots, f32[3,32,128]{2,1,0:T(8,128)S(1)} %get-tuple-element.39.seen, ...), custom_call_target="tpu_custom_call" | custom-call | bytes 3000000 | tf_op jit(solution)/shard_map/pallas_call | solution.py:743
  53.1 0.4 collective-permute-start.4
  53.6 4.1 %collective-permute-start.5 = (f32[18,24,128]{2,1,0:T(8,128)S(1)}, f32[18,24,128]{2,1,0:T(8,128)S(1)}, u32[]{:S(2)}, u32[]{:S(2)}) collective-permute-start(f32[18,24,128]{2,1,0:T(8,128)S(1)} %get-tuple-element.45), channel_id=1, source_target_pairs={{8,16},{16,8},{9,17},{17,9},{10,18},{18,10},{11,19},{19,11},{12,20... | collective-permute-start | bytes 663560 | tf_op jit(solution)/shard_map/ppermute | solution.py:677
  57.7 7.1 %shard_map.62.inner = f32[9,3,32,8,128]{4,3,2,1,0:T(8,128)S(1)} custom-call(s32[128]{0:T(128)S(1)} %get-tuple-element.42.work, f32[32,8,128]{2,1,0:T(8,128)S(1)} %get-tuple-element.31.slots, f32[9,32,128]{2,1,0:T(8,128)S(1)} %get-tuple-element.43.weight), custom_call_target="tpu_custom_call" | custom-call | bytes 18000000 | tf_op jit(solution)/shard_map/pallas_call | solution.py:752
  64.8 0.0 collective-permute-done.4.x_near
  64.8 0.7 collective-permute-done.5.x_far
  65.5 0.3 shard_map.64
  65.8 1.3 %collective-permute-start.6 = (f32[456,128]{1,0:T(8,128)S(1)}, f32[456,128]{1,0:T(8,128)S(1)}, u32[]{:S(2)}, u32[]{:S(2)}) collective-permute-start(f32[456,128]{1,0:T(8,128)S(1)} %get-tuple-element.53), channel_id=1, source_target_pairs={{0,1},{2,3},{4,5},{6,7},{1,0},{3,2},{5,4},{7,6},{8,9},{10,11},{12,... | collective-permute-start | bytes 700424 | tf_op jit(solution)/shard_map/ppermute | solution.py:677
  67.1 2.4 %collective-permute-start.7 = (f32[456,128]{1,0:T(8,128)S(1)}, f32[456,128]{1,0:T(8,128)S(1)}, u32[]{:S(2)}, u32[]{:S(2)}) collective-permute-start(f32[456,128]{1,0:T(8,128)S(1)} %get-tuple-element.54), channel_id=1, source_target_pairs={{1,2},{3,4},{5,6},{2,1},{4,3},{6,5},{9,10},{11,12},{13,14},{10,9},... | collective-permute-start | bytes 700424 | tf_op jit(solution)/shard_map/ppermute | solution.py:677
  69.5 6.4 %shard_map.63 = (f32[3,32,3072]{2,1,0:T(8,128)S(1)}, f32[3,2,4,48,128]{4,3,2,1,0:T(8,128)S(1)}, f32[3,2,4,48,128]{4,3,2,1,0:T(8,128)S(1)}, f32[3,2,4,48,128]{4,3,2,1,0:T(8,128)S(1)}) custom-call(f32[9,1,32,8,128]{4,3,2,1,0:T(8,128)S(1)} %get-tuple-element.41.outer, f32[9,3,32,8,128]{4,3,2,1,0:T(8,128)S(1)} %shard_map.62.inner, ...), custom_call_target="tpu_custom_call" | custom-call | bytes 24000000 | tf_op jit(solution)/shard_map/pallas_call | solution.py:766
  75.9 0.0 collective-permute-done.6.y_near
  75.9 0.0 collective-permute-done.7.y_far
  75.9 2.5 %shard_map.65 = f32[3,32,3072]{2,1,0:T(8,128)} custom-call(f32[3,32,3072]{2,1,0:T(8,128)S(1)} %get-tuple-element.49.part, f32[3,2,4,48,128]{4,3,2,1,0:T(8,128)S(1)} %get-tuple-element.50.e1, f32[3,2,4,48,128]{4,3,2,1,0:T(8,128)S(1)} %get-tuple-element.51.e2, f32[3,2,4,48,128]{4,3,2,1,0:T(8,128)S(1)} %get-tuple-element.52.e3, ...), custom_call_target="tpu_custom_call" | custom-call | bytes 3000000 | tf_op jit(solution)/shard_map/pallas_call | solution.py:774
Async XLA Ops:
  0.0 15.1 %copy-start = (f32[3,32,3072]{2,1,0:T(8,128)S(1)}, f32[3,32,3072]{2,1,0:T(8,128)}, u32[]{:S(2)}) copy-start(f32[3,32,3072]{2,1,0:T(8,128)} %state.3) | copy-start | bytes 3538948
  2.0 14.0 %collective-permute-start = (f32[16,3072]{1,0:T(8,128)}, f32[16,3072]{1,0:T(8,128)S(1)}, u32[]{:S(2)}, u32[]{:S(2)}) collective-permute-start(f32[16,3072]{1,0:T(8,128)} %get-tuple-element.33), channel_id=1, source_target_pairs={{0,8},{16,24},{8,0},{24,16},{1,9},{17,25},{9,1},{25,17},{2,10},{18... | collective-permute-start | bytes 589832 | tf_op jit(solution)/shard_map/ppermute | solution.py:677
  3.2 12.8 %collective-permute-start.1 = (f32[16,3072]{1,0:T(8,128)}, f32[16,3072]{1,0:T(8,128)S(1)}, u32[]{:S(2)}, u32[]{:S(2)}) collective-permute-start(f32[16,3072]{1,0:T(8,128)} %get-tuple-element.34), channel_id=1, source_target_pairs={{8,16},{16,8},{9,17},{17,9},{10,18},{18,10},{11,19},{19,11},{12,20... | collective-permute-start | bytes 589832 | tf_op jit(solution)/shard_map/ppermute | solution.py:677
  7.9 14.3 %all-to-all-start = ((f32[32,8,128]{2,1,0:T(8,128)}), f32[32,8,128]{2,1,0:T(8,128)S(1)}, u32[]{:S(2)}, u32[]{:S(2)}) async-start(f32[32,8,128]{2,1,0:T(8,128)} %shard_map.55), calls=%async_computation | async-start | bytes 262144 | tf_op jit(solution)/shard_map/all_to_all | solution.py:707
  16.2 7.3 %collective-permute-start.2 = (f32[424,128]{1,0:T(8,128)S(1)}, f32[424,128]{1,0:T(8,128)S(1)}, u32[]{:S(2)}, u32[]{:S(2)}) collective-permute-start(f32[424,128]{1,0:T(8,128)S(1)} %get-tuple-element.37), channel_id=1, source_target_pairs={{0,1},{2,3},{4,5},{6,7},{1,0},{3,2},{5,4},{7,6},{8,9},{10,11},{12,... | collective-permute-start | bytes 651272 | tf_op jit(solution)/shard_map/ppermute | solution.py:677
  16.7 7.2 %collective-permute-start.3 = (f32[424,128]{1,0:T(8,128)S(1)}, f32[424,128]{1,0:T(8,128)S(1)}, u32[]{:S(2)}, u32[]{:S(2)}) collective-permute-start(f32[424,128]{1,0:T(8,128)S(1)} %get-tuple-element.38), channel_id=1, source_target_pairs={{1,2},{3,4},{5,6},{2,1},{4,3},{6,5},{9,10},{11,12},{13,14},{10,9},... | collective-permute-start | bytes 651272 | tf_op jit(solution)/shard_map/ppermute | solution.py:677
  53.1 11.7 %collective-permute-start.4 = (f32[18,24,128]{2,1,0:T(8,128)S(1)}, f32[18,24,128]{2,1,0:T(8,128)S(1)}, u32[]{:S(2)}, u32[]{:S(2)}) collective-permute-start(f32[18,24,128]{2,1,0:T(8,128)S(1)} %get-tuple-element.44), channel_id=1, source_target_pairs={{0,8},{16,24},{8,0},{24,16},{1,9},{17,25},{9,1},{25,17},{2,10},{18... | collective-permute-start | bytes 663560 | tf_op jit(solution)/shard_map/ppermute | solution.py:677
  53.6 11.9 %collective-permute-start.5 = (f32[18,24,128]{2,1,0:T(8,128)S(1)}, f32[18,24,128]{2,1,0:T(8,128)S(1)}, u32[]{:S(2)}, u32[]{:S(2)}) collective-permute-start(f32[18,24,128]{2,1,0:T(8,128)S(1)} %get-tuple-element.45), channel_id=1, source_target_pairs={{8,16},{16,8},{9,17},{17,9},{10,18},{18,10},{11,19},{19,11},{12,20... | collective-permute-start | bytes 663560 | tf_op jit(solution)/shard_map/ppermute | solution.py:677
  65.8 10.1 %collective-permute-start.6 = (f32[456,128]{1,0:T(8,128)S(1)}, f32[456,128]{1,0:T(8,128)S(1)}, u32[]{:S(2)}, u32[]{:S(2)}) collective-permute-start(f32[456,128]{1,0:T(8,128)S(1)} %get-tuple-element.53), channel_id=1, source_target_pairs={{0,1},{2,3},{4,5},{6,7},{1,0},{3,2},{5,4},{7,6},{8,9},{10,11},{12,... | collective-permute-start | bytes 700424 | tf_op jit(solution)/shard_map/ppermute | solution.py:677
  67.1 8.9 %collective-permute-start.7 = (f32[456,128]{1,0:T(8,128)S(1)}, f32[456,128]{1,0:T(8,128)S(1)}, u32[]{:S(2)}, u32[]{:S(2)}) collective-permute-start(f32[456,128]{1,0:T(8,128)S(1)} %get-tuple-element.54), channel_id=1, source_target_pairs={{1,2},{3,4},{5,6},{2,1},{4,3},{6,5},{9,10},{11,12},{13,14},{10,9},... | collective-permute-start | bytes 700424 | tf_op jit(solution)/shard_map/ppermute | solution.py:677

commit v8 on v7

--- a/solution.py
+++ b/solution.py
@@ -111,7 +111,8 @@
 
 
 STATE_CORNERS, STATE_CORNER_ROWS = corner_rows(RIM)
-STATE_PIECE = 3 * RIM * PACKED + 64
+STRIP = -(-RIM * NZ // LANES)
+STATE_PIECE = 3 * STRIP * CX + 64
 FORCE_BLOCKS = [(n, c, i) for n in range(STEPS) for c in range(3) for i in range(n + 1)]
 FORCE_CORNERS = [
     (n, c, dist, side, k)
@@ -189,7 +190,7 @@
         slots[i] = moved[0:8] + moved[8:16] + moved[16:24]
         return carry
 
-    lax.fori_loop(0, lists, move, 0, unroll=8)
+    lax.fori_loop(0, lists, move, 0, unroll=16)
 
 
 def regroup_kernel(received, slots, every_work, outer_work, inner_work, turned):
@@ -231,28 +232,17 @@
         work[WORK - 1] = count
 
 
-def state_layers_kernel(state, first_layers, last_layers):
-    blank = jnp.zeros((CX, LANES - NZ), F32)
-    for out, layer_of in ((first_layers, lambda d: d - 1), (last_layers, lambda d: CY - d)):
+def state_corner_kernel(state, x_near, x_far, near, far, first, last, before, after):
+    from_partners("gx", x_near, x_far, before, after)
+    base = 3 * STRIP * CX
+    for start, out, layer_of in (
+        (0, first, lambda d: d - 1),
+        (CY * NZ - STRIP * LANES, last, lambda d: CY - d),
+    ):
         for c in range(3):
-            for dist in range(1, RIM + 1):
-                base = (c * RIM + dist - 1) * PACKED
-                y = layer_of(dist)
-
-                def put(row, rows, base=base, out=out):
-                    out[base + row : base + row + 8, :] = rows
-
-                pack(put, jnp.concatenate([state[c, :, NZ * y : NZ * y + NZ], blank], axis=1))
-
-
-def state_corner_kernel(bulk_first, bulk_last, x_near, x_far, near, far, first, last, before, after):
-    from_partners("gx", x_near, x_far, before, after)
-    base = 3 * RIM * PACKED
-    for bulk, out, layer_of in (
-        (bulk_first, first, lambda d: d - 1),
-        (bulk_last, last, lambda d: CY - d),
-    ):
-        out[0:base, :] = bulk[...]
+            for j in range(STRIP):
+                lanes = slice(start + LANES * j, start + LANES * j + LANES)
+                out[(c * STRIP + j) * CX : (c * STRIP + j + 1) * CX, :] = state[c, :, lanes]
         out[base : base + 64, :] = jnp.zeros((64, LANES), F32)
         for c, dist, row, side in STATE_CORNERS:
             lanes = slice(NZ * layer_of(dist), NZ * layer_of(dist) + NZ)
@@ -409,12 +399,17 @@
             s0[c, RIM + y, PAD : PAD + CX, 0:NZ] = state[c, :, lanes]
             s0[c, RIM + y, PAD - RIM : PAD, 0:NZ] = before[RIM * c : RIM * c + RIM, lanes]
             s0[c, RIM + y, PAD + CX : PAD + CX + RIM, 0:NZ] = after[RIM * c : RIM * c + RIM, lanes]
-    for piece, layer_of in ((above, lambda d: RIM + CY - 1 + d), (below, lambda d: RIM - d)):
+    for piece, layer_of, lane_of_layer in (
+        (above, lambda d: RIM + CY - 1 + d, lambda d: NZ * (d - 1)),
+        (below, lambda d: RIM - d, lambda d: STRIP * LANES - NZ * d),
+    ):
         for c in range(3):
+            tiles = [piece[(c * STRIP + j) * CX : (c * STRIP + j + 1) * CX, :] for j in range(STRIP)]
+            strip = jnp.concatenate(tiles, axis=1)
             for dist in range(1, RIM + 1):
-                base = (c * RIM + dist - 1) * PACKED
-                s0[c, layer_of(dist), PAD : PAD + CX, :] = unpack(piece[base : base + PACKED, :])
-        base = 3 * RIM * PACKED
+                lane = lane_of_layer(dist)
+                s0[c, layer_of(dist), PAD : PAD + CX, 0:NZ] = strip[:, lane : lane + NZ]
+        base = 3 * STRIP * CX
         for c, dist, row, side in STATE_CORNERS:
             s0[c, layer_of(dist), PAD - side : PAD, :] = piece[base + row : base + row + side, :]
             s0[c, layer_of(dist), PAD + CX : PAD + CX + side, :] = piece[
@@ -693,7 +688,7 @@
         out_specs=(pl.BlockSpec(x_rim, lambda i: (0, 0)), pl.BlockSpec(x_rim, lambda i: (0, 0))),
         grid=(1,),
         scratch_shapes=[pltpu.VMEM(x_rim, F32)] * 2,
-        compiler_params=pltpu.CompilerParams(vmem_limit_bytes=60 * MIB),
+        compiler_params=pltpu.CompilerParams(vmem_limit_bytes=8 * MIB),
     )(initial_state, initial_state)
     x_near, x_far = swap(near, far, "gx")
     lists = (peers, 8, capacity)
@@ -715,15 +710,13 @@
         micros=2,
     )(slots)
     field = shape(3, YH, XH, LANES)
-    bulk = shape(3 * RIM * PACKED, LANES)
-    bulk_first, bulk_last = call(state_layers_kernel, (bulk, bulk), ins=1)(initial_state)
     y_rim = (STATE_PIECE, LANES)
     near, far = call(
         state_corner_kernel,
         (shape(*y_rim), shape(*y_rim)),
         [pltpu.VMEM(y_rim, F32)] * 2 + [pltpu.VMEM(x_rim, F32)] * 2,
-        ins=4,
-    )(bulk_first, bulk_last, x_near, x_far)
+        ins=3,
+    )(initial_state, x_near, x_far)
     y_near, y_far = swap(near, far, "gy")
     mask = pltpu.VMEM((XH, LANES), F32)
     seen, sums, s0, s1, s2 = call(

time: 78.8 us -> 77.7 us (0.986)
  Pallas kernels: 41.2 us -> 39.2 us
  local copies, waits for them, and re-layouts: 0.01 us -> 1.27 us
    pallas_call x1, Pallas kernels: 2 us -> 0.14 us  [local(): pl.pallas_call(state_rows_kernel, out_shape=(shape(*x_rim), shape(*x_rim)...]
    unnamed x2 -> x4, local copies, waits for them, and re-layouts: 0.01 us -> 1.27 us
    ppermute x4, waiting for transfers between devices: 0.97 us -> 0.01 us  [swap(): lax.ppermute(far, axis, pairs(1))]
    ppermute x4, starting transfers between devices: 11.6 us -> 10.6 us  [swap(): lax.ppermute(far, axis, pairs(1))]
    all_to_all x1, waiting for transfers between devices: 2.38 us -> 3.33 us  [local(): slots = lax.all_to_all(slots, AXES, split_axis=0, concat_axis=0, tiled=True)]
    pallas_call x1 -> x0, Pallas kernels: 0.95 us -> none  [local(): call(state_layers_kernel, (bulk, bulk), ins=1)(initial_state)]
    pallas_call x1, Pallas kernels: 7.13 us -> 7.98 us  [local(): call(inner_force_kernel, parts[1], [totals[1]], limit=24, ins=3, scalar_i...]
  transfers between devices with their start and end apart: 9 -> 9, of which waited for: 3 -> 1; matrix products, arithmetic and copies ran while one was open for 0% -> 0% of each run, Pallas kernels for 24% -> 24%
where the time goes in v8:
time: 77.7 us; the launch traced here: 76.7 us
  Pallas kernels  39.2 us (50%)
  starting transfers between devices  21.6 us (28%)
  blocking collectives  11.1 us (14%)
  waiting for transfers between devices  3.35 us (4%)
  local copies, waits for them, and re-layouts  1.27 us (2%)
    pallas_call x1, Pallas kernels, local(): call(functools.partial(forward_kernel, beams), (shape(STEPS, rows, LANES)...  14.3 us
    all_to_all x1, blocking collectives, local(): sums = lax.all_to_all(sums, AXES, split_axis=0, concat_axis=0, tiled=True)  11.1 us
    ppermute x4, starting transfers between devices, swap(): lax.ppermute(far, axis, pairs(1))  10.6 us
    pallas_call x1, Pallas kernels, local(): call(inner_force_kernel, parts[1], [totals[1]], limit=24, ins=3, scalar_i...  7.98 us
    all_to_all x1, starting transfers between devices, local(): slots = lax.all_to_all(slots, AXES, split_axis=0, concat_axis=0, tiled=True)  7.13 us
    pallas_call x1, Pallas kernels, local(): call(inner_backward_kernel, (whole, edges, edges, edges), [adjoint] * 4 +...  6.34 us
    ppermute x4, starting transfers between devices, swap(): lax.ppermute(near, axis, pairs(0))  3.84 us
    pallas_call x1, Pallas kernels, local(): call(functools.partial(outer_force_kernel, beams), (parts[0], shape(FIELD...  3.65 us
  transfers between devices with their start and end apart: 9, of which 1 were waited for; matrix products, arithmetic and copies ran while one was open for 0% of the time, Pallas kernels for 24%

profile of v8, /device:TPU:5, one launch (start us, length us, event | category | flops | bytes accessed | tf_op | source)
XLA Modules:
  0.0 76.7 jit_solution(12941665048243701863)
XLA Ops:
  0.0 0.0 copy-start
  0.0 1.3 %copy-done = f32[3,32,3072]{2,1,0:T(8,128)S(1)} copy-done((f32[3,32,3072]{2,1,0:T(8,128)S(1)}, f32[3,32,3072]{2,1,0:T(8,128)}, u32[]{:S(2)}) %copy-start) | copy-done | bytes 1179672
  1.3 0.0 copy-start.1
  1.3 0.1 shard_map.57
  1.4 1.3 %collective-permute-start = (f32[16,3072]{1,0:T(8,128)S(1)}, f32[16,3072]{1,0:T(8,128)S(1)}, u32[]{:S(2)}, u32[]{:S(2)}) collective-permute-start(f32[16,3072]{1,0:T(8,128)S(1)} %get-tuple-element.31), channel_id=1, source_target_pairs={{0,8},{16,24},{8,0},{24,16},{1,9},{17,25},{9,1},{25,17},{2,10},{18... | collective-permute-start | bytes 589832 | tf_op jit(solution)/shard_map/ppermute | solution.py:672
  2.7 2.0 %collective-permute-start.1 = (f32[16,3072]{1,0:T(8,128)S(1)}, f32[16,3072]{1,0:T(8,128)S(1)}, u32[]{:S(2)}, u32[]{:S(2)}) collective-permute-start(f32[16,3072]{1,0:T(8,128)S(1)} %get-tuple-element.32), channel_id=1, source_target_pairs={{8,16},{16,8},{9,17},{17,9},{10,18},{18,10},{11,19},{19,11},{12,20... | collective-permute-start | bytes 589832 | tf_op jit(solution)/shard_map/ppermute | solution.py:672
  4.7 2.5 %shard_map.55 = f32[32,8,128]{2,1,0:T(8,128)} custom-call(f32[3,4]{1,0:T(4,128)} %beam_dir.1, f32[3,1,32,128]{3,2,1,0:T(8,128)} %obs.1, s32[1,32,128]{2,1,0:T(8,128)} %beam.1, s32[1,32,128]{2,1,0:T(8,128)} %cell.1), custom_call_target="tpu_custom_call" | custom-call | bytes 3000000 | tf_op jit(solution)/shard_map/pallas_call | solution.py:695
  7.2 7.1 %all-to-all-start = ((f32[32,8,128]{2,1,0:T(8,128)}), f32[32,8,128]{2,1,0:T(8,128)S(1)}, u32[]{:S(2)}, u32[]{:S(2)}) async-start(f32[32,8,128]{2,1,0:T(8,128)} %shard_map.55), calls=%async_computation | async-start | bytes 262144 | tf_op jit(solution)/shard_map/all_to_all | solution.py:702
  14.3 0.0 collective-permute-done.x_near
  14.3 0.0 collective-permute-done.1.x_far
  14.3 0.0 copy-done.1
  14.4 0.2 shard_map.58
  14.5 0.4 collective-permute-start.2
  15.0 3.1 %collective-permute-start.3 = (f32[448,128]{1,0:T(8,128)S(1)}, f32[448,128]{1,0:T(8,128)S(1)}, u32[]{:S(2)}, u32[]{:S(2)}) collective-permute-start(f32[448,128]{1,0:T(8,128)S(1)} %get-tuple-element.34), channel_id=1, source_target_pairs={{1,2},{3,4},{5,6},{2,1},{4,3},{6,5},{9,10},{11,12},{13,14},{10,9},... | collective-permute-start | bytes 688136 | tf_op jit(solution)/shard_map/ppermute | solution.py:672
  18.1 3.3 %all-to-all-done.received = f32[32,8,128]{2,1,0:T(8,128)S(1)} async-done(((f32[32,8,128]{2,1,0:T(8,128)}), f32[32,8,128]{2,1,0:T(8,128)S(1)}, u32[]{:S(2)}, u32[]{:S(2)}) %all-to-all-start) | async-done | bytes 131104 | tf_op jit(solution)/shard_map/all_to_all | solution.py:702
  21.4 1.4 %shard_map.56 = (f32[32,8,128]{2,1,0:T(8,128)S(1)}, s32[128]{0:T(128)S(1)}, s32[128]{0:T(128)S(1)}, s32[128]{0:T(128)S(1)}) custom-call(f32[32,8,128]{2,1,0:T(8,128)S(1)} %all-to-all-done.received), custom_call_target="tpu_custom_call" | custom-call | bytes 6000000 | tf_op jit(solution)/shard_map/pallas_call | solution.py:704
  22.8 0.0 collective-permute-done.2.y_near
  22.8 0.0 collective-permute-done.3.y_far
  22.8 14.3 %shard_map.59 = (f32[3,32,128]{2,1,0:T(8,128)S(1)}, f32[32,1,384]{2,1,0:T(1,128)S(1)}, f32[3,42,48,128]{3,2,1,0:T(8,128)S(1)}, f32[3,42,48,128]{3,2,1,0:T(8,128)S(1)}, f32[3,42,48,128]{3,2,1,0:T(8,128)S(1)}) custom-call(s32[128]{0:T(128)S(1)} %get-tuple-element.30.work, f32[3,32,3072]{2,1,0:T(8,128)S(1)} %copy-done.1, ...), custom_call_target="tpu_custom_call" | custom-call | bytes 3000000 | tf_op jit(solution)/shard_map/pallas_call | solution.py:722
  37.1 11.1 %all_to_all.10.sums = f32[32,1,384]{2,1,0:T(1,128)S(1)} all-to-all(f32[32,1,384]{2,1,0:T(1,128)S(1)} %get-tuple-element.36), channel_id=1, replica_groups=mesh['gx'=4,'gy'=8] {'gx','gy'}, dimensions={0} | all-to-all | bytes 98304 | tf_op jit(solution)/shard_map/all_to_all | solution.py:732
  48.2 3.7 %shard_map.60 = (f32[9,1,32,8,128]{4,3,2,1,0:T(8,128)S(1)}, f32[9,32,128]{2,1,0:T(8,128)S(1)}, f32[18,24,128]{2,1,0:T(8,128)S(1)}, f32[18,24,128]{2,1,0:T(8,128)S(1)}) custom-call(s32[128]{0:T(128)S(1)} %get-tuple-element.28.work, f32[32,8,128]{2,1,0:T(8,128)S(1)} %get-tuple-element.29.slots, f32[3,32,128]{2,1,0:T(8,128)S(1)} %get-tuple-element.35.seen, ...), custom_call_target="tpu_custom_call" | custom-call | bytes 3000000 | tf_op jit(solution)/shard_map/pallas_call | solution.py:736
  51.9 0.4 collective-permute-start.4
  52.3 3.3 %collective-permute-start.5 = (f32[18,24,128]{2,1,0:T(8,128)S(1)}, f32[18,24,128]{2,1,0:T(8,128)S(1)}, u32[]{:S(2)}, u32[]{:S(2)}) collective-permute-start(f32[18,24,128]{2,1,0:T(8,128)S(1)} %get-tuple-element.41), channel_id=1, source_target_pairs={{8,16},{16,8},{9,17},{17,9},{10,18},{18,10},{11,19},{19,11},{12,20... | collective-permute-start | bytes 663560 | tf_op jit(solution)/shard_map/ppermute | solution.py:672
  55.6 8.0 %shard_map.61.inner = f32[9,3,32,8,128]{4,3,2,1,0:T(8,128)S(1)} custom-call(s32[128]{0:T(128)S(1)} %get-tuple-element.38.work, f32[32,8,128]{2,1,0:T(8,128)S(1)} %get-tuple-element.29.slots, f32[9,32,128]{2,1,0:T(8,128)S(1)} %get-tuple-element.39.weight), custom_call_target="tpu_custom_call" | custom-call | bytes 18000000 | tf_op jit(solution)/shard_map/pallas_call | solution.py:745
  63.6 0.0 collective-permute-done.4.x_near
  63.6 0.0 collective-permute-done.5.x_far
  63.6 0.3 shard_map.63
  63.8 1.7 %collective-permute-start.6 = (f32[456,128]{1,0:T(8,128)S(1)}, f32[456,128]{1,0:T(8,128)S(1)}, u32[]{:S(2)}, u32[]{:S(2)}) collective-permute-start(f32[456,128]{1,0:T(8,128)S(1)} %get-tuple-element.49), channel_id=1, source_target_pairs={{0,1},{2,3},{4,5},{6,7},{1,0},{3,2},{5,4},{7,6},{8,9},{10,11},{12,... | collective-permute-start | bytes 700424 | tf_op jit(solution)/shard_map/ppermute | solution.py:672
  65.5 2.3 %collective-permute-start.7 = (f32[456,128]{1,0:T(8,128)S(1)}, f32[456,128]{1,0:T(8,128)S(1)}, u32[]{:S(2)}, u32[]{:S(2)}) collective-permute-start(f32[456,128]{1,0:T(8,128)S(1)} %get-tuple-element.50), channel_id=1, source_target_pairs={{1,2},{3,4},{5,6},{2,1},{4,3},{6,5},{9,10},{11,12},{13,14},{10,9},... | collective-permute-start | bytes 700424 | tf_op jit(solution)/shard_map/ppermute | solution.py:672
  67.8 6.3 %shard_map.62 = (f32[3,32,3072]{2,1,0:T(8,128)S(1)}, f32[3,2,4,48,128]{4,3,2,1,0:T(8,128)S(1)}, f32[3,2,4,48,128]{4,3,2,1,0:T(8,128)S(1)}, f32[3,2,4,48,128]{4,3,2,1,0:T(8,128)S(1)}) custom-call(f32[9,1,32,8,128]{4,3,2,1,0:T(8,128)S(1)} %get-tuple-element.37.outer, f32[9,3,32,8,128]{4,3,2,1,0:T(8,128)S(1)} %shard_map.61.inner, ...), custom_call_target="tpu_custom_call" | custom-call | bytes 24000000 | tf_op jit(solution)/shard_map/pallas_call | solution.py:759
  74.2 0.0 collective-permute-done.6.y_near
  74.2 0.0 collective-permute-done.7.y_far
  74.2 2.5 %shard_map.64 = f32[3,32,3072]{2,1,0:T(8,128)} custom-call(f32[3,32,3072]{2,1,0:T(8,128)S(1)} %get-tuple-element.45.part, f32[3,2,4,48,128]{4,3,2,1,0:T(8,128)S(1)} %get-tuple-element.46.e1, f32[3,2,4,48,128]{4,3,2,1,0:T(8,128)S(1)} %get-tuple-element.47.e2, f32[3,2,4,48,128]{4,3,2,1,0:T(8,128)S(1)} %get-tuple-element.48.e3, ...), custom_call_target="tpu_custom_call" | custom-call | bytes 3000000 | tf_op jit(solution)/shard_map/pallas_call | solution.py:767
Async XLA Ops:
  0.0 1.3 %copy-start = (f32[3,32,3072]{2,1,0:T(8,128)S(1)}, f32[3,32,3072]{2,1,0:T(8,128)}, u32[]{:S(2)}) copy-start(f32[3,32,3072]{2,1,0:T(8,128)} %state.3) | copy-start | bytes 3538948
  1.3 13.1 %copy-start.1 = (f32[3,32,3072]{2,1,0:T(8,128)S(1)}, f32[3,32,3072]{2,1,0:T(8,128)}, u32[]{:S(2)}) copy-start(f32[3,32,3072]{2,1,0:T(8,128)} %state.3) | copy-start | bytes 3538948
  1.4 12.9 %collective-permute-start = (f32[16,3072]{1,0:T(8,128)S(1)}, f32[16,3072]{1,0:T(8,128)S(1)}, u32[]{:S(2)}, u32[]{:S(2)}) collective-permute-start(f32[16,3072]{1,0:T(8,128)S(1)} %get-tuple-element.31), channel_id=1, source_target_pairs={{0,8},{16,24},{8,0},{24,16},{1,9},{17,25},{9,1},{25,17},{2,10},{18... | collective-permute-start | bytes 589832 | tf_op jit(solution)/shard_map/ppermute | solution.py:672
  2.7 11.6 %collective-permute-start.1 = (f32[16,3072]{1,0:T(8,128)S(1)}, f32[16,3072]{1,0:T(8,128)S(1)}, u32[]{:S(2)}, u32[]{:S(2)}) collective-permute-start(f32[16,3072]{1,0:T(8,128)S(1)} %get-tuple-element.32), channel_id=1, source_target_pairs={{8,16},{16,8},{9,17},{17,9},{10,18},{18,10},{11,19},{19,11},{12,20... | collective-permute-start | bytes 589832 | tf_op jit(solution)/shard_map/ppermute | solution.py:672
  7.2 14.2 %all-to-all-start = ((f32[32,8,128]{2,1,0:T(8,128)}), f32[32,8,128]{2,1,0:T(8,128)S(1)}, u32[]{:S(2)}, u32[]{:S(2)}) async-start(f32[32,8,128]{2,1,0:T(8,128)} %shard_map.55), calls=%async_computation | async-start | bytes 262144 | tf_op jit(solution)/shard_map/all_to_all | solution.py:702
  14.5 8.3 %collective-permute-start.2 = (f32[448,128]{1,0:T(8,128)S(1)}, f32[448,128]{1,0:T(8,128)S(1)}, u32[]{:S(2)}, u32[]{:S(2)}) collective-permute-start(f32[448,128]{1,0:T(8,128)S(1)} %get-tuple-element.33), channel_id=1, source_target_pairs={{0,1},{2,3},{4,5},{6,7},{1,0},{3,2},{5,4},{7,6},{8,9},{10,11},{12,... | collective-permute-start | bytes 688136 | tf_op jit(solution)/shard_map/ppermute | solution.py:672
  15.0 7.8 %collective-permute-start.3 = (f32[448,128]{1,0:T(8,128)S(1)}, f32[448,128]{1,0:T(8,128)S(1)}, u32[]{:S(2)}, u32[]{:S(2)}) collective-permute-start(f32[448,128]{1,0:T(8,128)S(1)} %get-tuple-element.34), channel_id=1, source_target_pairs={{1,2},{3,4},{5,6},{2,1},{4,3},{6,5},{9,10},{11,12},{13,14},{10,9},... | collective-permute-start | bytes 688136 | tf_op jit(solution)/shard_map/ppermute | solution.py:672
  51.9 11.7 %collective-permute-start.4 = (f32[18,24,128]{2,1,0:T(8,128)S(1)}, f32[18,24,128]{2,1,0:T(8,128)S(1)}, u32[]{:S(2)}, u32[]{:S(2)}) collective-permute-start(f32[18,24,128]{2,1,0:T(8,128)S(1)} %get-tuple-element.40), channel_id=1, source_target_pairs={{0,8},{16,24},{8,0},{24,16},{1,9},{17,25},{9,1},{25,17},{2,10},{18... | collective-permute-start | bytes 663560 | tf_op jit(solution)/shard_map/ppermute | solution.py:672
  52.3 11.3 %collective-permute-start.5 = (f32[18,24,128]{2,1,0:T(8,128)S(1)}, f32[18,24,128]{2,1,0:T(8,128)S(1)}, u32[]{:S(2)}, u32[]{:S(2)}) collective-permute-start(f32[18,24,128]{2,1,0:T(8,128)S(1)} %get-tuple-element.41), channel_id=1, source_target_pairs={{8,16},{16,8},{9,17},{17,9},{10,18},{18,10},{11,19},{19,11},{12,20... | collective-permute-start | bytes 663560 | tf_op jit(solution)/shard_map/ppermute | solution.py:672
  63.8 10.3 %collective-permute-start.6 = (f32[456,128]{1,0:T(8,128)S(1)}, f32[456,128]{1,0:T(8,128)S(1)}, u32[]{:S(2)}, u32[]{:S(2)}) collective-permute-start(f32[456,128]{1,0:T(8,128)S(1)} %get-tuple-element.49), channel_id=1, source_target_pairs={{0,1},{2,3},{4,5},{6,7},{1,0},{3,2},{5,4},{7,6},{8,9},{10,11},{12,... | collective-permute-start | bytes 700424 | tf_op jit(solution)/shard_map/ppermute | solution.py:672
  65.5 8.6 %collective-permute-start.7 = (f32[456,128]{1,0:T(8,128)S(1)}, f32[456,128]{1,0:T(8,128)S(1)}, u32[]{:S(2)}, u32[]{:S(2)}) collective-permute-start(f32[456,128]{1,0:T(8,128)S(1)} %get-tuple-element.50), channel_id=1, source_target_pairs={{1,2},{3,4},{5,6},{2,1},{4,3},{6,5},{9,10},{11,12},{13,14},{10,9},... | collective-permute-start | bytes 700424 | tf_op jit(solution)/shard_map/ppermute | solution.py:672

commit v9 on v8

--- a/solution.py
+++ b/solution.py
@@ -281,18 +281,17 @@
             r = first_row + 8 * t
             here, ahead, behind = pl.ds(r, 8), pl.ds(r + 1, 8), pl.ds(r - 1, 8)
             centre = [src[c, y + RIM, here, :] for c in range(3)]
-            scaled = [0.1 * v for v in centre]
-            plus = [0.1 - v for v in scaled]
-            minus = [0.1 + v for v in scaled]
-            inside = mask[here, :] * keep
+            plus = [1.0 - v for v in centre]
+            minus = [1.0 + v for v in centre]
+            tenth = mask[here, :] * (0.1 * keep)
             for c in range(3):
                 v = centre[c]
-                total = 0.4 * v + (plus[2] * next_level(v) + minus[2] * last_level(v))
+                total = 4.0 * v + (plus[2] * next_level(v) + minus[2] * last_level(v))
                 total = total + (plus[0] * src[c, y + RIM, ahead, :] + minus[0] * src[c, y + RIM, behind, :])
                 total = total + (
                     plus[1] * src[c, y + RIM + 1, here, :] + minus[1] * src[c, y + RIM - 1, here, :]
                 )
-                done.append((c, here, total * inside))
+                done.append((c, here, total * tenth))
         for c, here, total in done:
             dst[c, y + RIM, here, :] = total
         return carry
@@ -566,31 +565,31 @@
             v_next = [field[c, y + RIM + 1, here, :] for c in range(3)]
             v_last = [field[c, y + RIM - 1, here, :] for c in range(3)]
             a = [source[c, y + FRIM, here, :] for c in range(3)]
-            scaled = [0.1 * f for f in a]
             bends = [None] * 3
             for d, (up, down) in enumerate(((v_ahead, v_behind), (v_next, v_last), (None, None))):
                 for c in range(3):
                     u, w = (up[c], down[c]) if d < 2 else (next_level(v[c]), last_level(v[c]))
-                    part = (u - w) * scaled[c]
+                    part = (u - w) * a[c]
                     bends[d] = part if bends[d] is None else bends[d] + part
-            x_ahead = 0.1 + 0.1 * v_ahead[0]
-            x_behind = 0.1 - 0.1 * v_behind[0]
-            y_next = 0.1 + 0.1 * v_next[1]
-            y_last = 0.1 - 0.1 * v_last[1]
-            inside = mask[here, :] * keep
+            x_ahead = 1.0 + v_ahead[0]
+            x_behind = 1.0 - v_behind[0]
+            y_next = 1.0 + v_next[1]
+            y_last = 1.0 - v_last[1]
+            tenth = mask[here, :] * (0.1 * keep)
             for c in range(3):
-                total = 0.4 * a[c] - bends[c]
+                total = 4.0 * a[c] - bends[c]
                 total = total + (
                     x_ahead * source[c, y + FRIM, ahead, :] + x_behind * source[c, y + FRIM, behind, :]
                 )
                 total = total + (
                     y_next * source[c, y + FRIM + 1, here, :] + y_last * source[c, y + FRIM - 1, here, :]
                 )
-                product = v[2] * scaled[c]
-                total = total + (next_level(scaled[c] + product) + last_level(scaled[c] - product))
+                product = v[2] * a[c]
+                total = total + (next_level(a[c] + product) + last_level(a[c] - product))
+                total = total * tenth
                 if add:
                     total = total + target[c, y + FRIM, here, :]
-                done.append((c, here, total * inside))
+                done.append((c, here, total))
         for c, here, total in done:
             target[c, y + FRIM, here, :] = total
         return carry

time: 77.7 us -> 76.9 us (0.990)
  Pallas kernels: 39.2 us -> 41.6 us
  starting transfers between devices: 21.6 us -> 20.2 us
  blocking collectives: 11.1 us -> 10 us
    ppermute x4, starting transfers between devices: 3.84 us -> 2.47 us  [swap(): lax.ppermute(near, axis, pairs(0))]
    pallas_call x1, Pallas kernels: 7.98 us -> 9.33 us  [local(): call(inner_force_kernel, parts[1], [totals[1]], limit=24, ins=3, scalar_i...]
    all_to_all x1, blocking collectives: 11.1 us -> 10 us  [local(): sums = lax.all_to_all(sums, AXES, split_axis=0, concat_axis=0, tiled=True)]
    pallas_call x1, Pallas kernels: 14.3 us -> 15.2 us  [local(): call(functools.partial(forward_kernel, beams), (shape(STEPS, rows, LANES)...]
  transfers between devices with their start and end apart: 9 -> 9, of which waited for: 1 -> 1; matrix products, arithmetic and copies ran while one was open for 0% -> 0% of each run, Pallas kernels for 24% -> 26%
where the time goes in v9:
time: 76.9 us; the launch traced here: 76.7 us
  Pallas kernels  41.6 us (54%)
  starting transfers between devices  20.2 us (26%)
  blocking collectives  10 us (13%)
  waiting for transfers between devices  3.35 us (4%)
  local copies, waits for them, and re-layouts  1.27 us (2%)
    pallas_call x1, Pallas kernels, local(): call(functools.partial(forward_kernel, beams), (shape(STEPS, rows, LANES)...  15.2 us
    ppermute x4, starting transfers between devices, swap(): lax.ppermute(far, axis, pairs(1))  10.6 us
    all_to_all x1, blocking collectives, local(): sums = lax.all_to_all(sums, AXES, split_axis=0, concat_axis=0, tiled=True)  10 us
    pallas_call x1, Pallas kernels, local(): call(inner_force_kernel, parts[1], [totals[1]], limit=24, ins=3, scalar_i...  9.33 us
    all_to_all x1, starting transfers between devices, local(): slots = lax.all_to_all(slots, AXES, split_axis=0, concat_axis=0, tiled=True)  7.13 us
    pallas_call x1, Pallas kernels, local(): call(inner_backward_kernel, (whole, edges, edges, edges), [adjoint] * 4 +...  6.4 us
    pallas_call x1, Pallas kernels, local(): call(functools.partial(outer_force_kernel, beams), (parts[0], shape(FIELD...  3.66 us
    all_to_all x1, waiting for transfers between devices, local(): slots = lax.all_to_all(slots, AXES, split_axis=0, concat_axis=0, tiled=True)  3.33 us
  transfers between devices with their start and end apart: 9, of which 1 were waited for; matrix products, arithmetic and copies ran while one was open for 0% of the time, Pallas kernels for 26%

profile of v9, /device:TPU:5, one launch (start us, length us, event | category | flops | bytes accessed | tf_op | source)
XLA Modules:
  0.0 76.7 jit_solution(15945347245174218484)
XLA Ops:
  0.0 0.0 copy-start
  0.0 1.3 %copy-done = f32[3,32,3072]{2,1,0:T(8,128)S(1)} copy-done((f32[3,32,3072]{2,1,0:T(8,128)S(1)}, f32[3,32,3072]{2,1,0:T(8,128)}, u32[]{:S(2)}) %copy-start) | copy-done | bytes 1179672
  1.3 0.0 copy-start.1
  1.3 0.1 shard_map.57
  1.4 1.3 %collective-permute-start = (f32[16,3072]{1,0:T(8,128)S(1)}, f32[16,3072]{1,0:T(8,128)S(1)}, u32[]{:S(2)}, u32[]{:S(2)}) collective-permute-start(f32[16,3072]{1,0:T(8,128)S(1)} %get-tuple-element.31), channel_id=1, source_target_pairs={{0,8},{16,24},{8,0},{24,16},{1,9},{17,25},{9,1},{25,17},{2,10},{18... | collective-permute-start | bytes 589832 | tf_op jit(solution)/shard_map/ppermute | solution.py:671
  2.7 2.0 %collective-permute-start.1 = (f32[16,3072]{1,0:T(8,128)S(1)}, f32[16,3072]{1,0:T(8,128)S(1)}, u32[]{:S(2)}, u32[]{:S(2)}) collective-permute-start(f32[16,3072]{1,0:T(8,128)S(1)} %get-tuple-element.32), channel_id=1, source_target_pairs={{8,16},{16,8},{9,17},{17,9},{10,18},{18,10},{11,19},{19,11},{12,20... | collective-permute-start | bytes 589832 | tf_op jit(solution)/shard_map/ppermute | solution.py:671
  4.7 2.5 %shard_map.55 = f32[32,8,128]{2,1,0:T(8,128)} custom-call(f32[3,4]{1,0:T(4,128)} %beam_dir.1, f32[3,1,32,128]{3,2,1,0:T(8,128)} %obs.1, s32[1,32,128]{2,1,0:T(8,128)} %beam.1, s32[1,32,128]{2,1,0:T(8,128)} %cell.1), custom_call_target="tpu_custom_call" | custom-call | bytes 3000000 | tf_op jit(solution)/shard_map/pallas_call | solution.py:694
  7.2 7.1 %all-to-all-start = ((f32[32,8,128]{2,1,0:T(8,128)}), f32[32,8,128]{2,1,0:T(8,128)S(1)}, u32[]{:S(2)}, u32[]{:S(2)}) async-start(f32[32,8,128]{2,1,0:T(8,128)} %shard_map.55), calls=%async_computation | async-start | bytes 262144 | tf_op jit(solution)/shard_map/all_to_all | solution.py:701
  14.3 0.0 collective-permute-done.x_near
  14.3 0.0 collective-permute-done.1.x_far
  14.3 0.0 copy-done.1
  14.4 0.2 shard_map.58
  14.5 0.4 collective-permute-start.2
  15.0 3.1 %collective-permute-start.3 = (f32[448,128]{1,0:T(8,128)S(1)}, f32[448,128]{1,0:T(8,128)S(1)}, u32[]{:S(2)}, u32[]{:S(2)}) collective-permute-start(f32[448,128]{1,0:T(8,128)S(1)} %get-tuple-element.34), channel_id=1, source_target_pairs={{1,2},{3,4},{5,6},{2,1},{4,3},{6,5},{9,10},{11,12},{13,14},{10,9},... | collective-permute-start | bytes 688136 | tf_op jit(solution)/shard_map/ppermute | solution.py:671
  18.1 3.3 %all-to-all-done.received = f32[32,8,128]{2,1,0:T(8,128)S(1)} async-done(((f32[32,8,128]{2,1,0:T(8,128)}), f32[32,8,128]{2,1,0:T(8,128)S(1)}, u32[]{:S(2)}, u32[]{:S(2)}) %all-to-all-start) | async-done | bytes 131104 | tf_op jit(solution)/shard_map/all_to_all | solution.py:701
  21.4 1.4 %shard_map.56 = (f32[32,8,128]{2,1,0:T(8,128)S(1)}, s32[128]{0:T(128)S(1)}, s32[128]{0:T(128)S(1)}, s32[128]{0:T(128)S(1)}) custom-call(f32[32,8,128]{2,1,0:T(8,128)S(1)} %all-to-all-done.received), custom_call_target="tpu_custom_call" | custom-call | bytes 6000000 | tf_op jit(solution)/shard_map/pallas_call | solution.py:703
  22.8 0.0 collective-permute-done.2.y_near
  22.8 0.0 collective-permute-done.3.y_far
  22.8 15.2 %shard_map.59 = (f32[3,32,128]{2,1,0:T(8,128)S(1)}, f32[32,1,384]{2,1,0:T(1,128)S(1)}, f32[3,42,48,128]{3,2,1,0:T(8,128)S(1)}, f32[3,42,48,128]{3,2,1,0:T(8,128)S(1)}, f32[3,42,48,128]{3,2,1,0:T(8,128)S(1)}) custom-call(s32[128]{0:T(128)S(1)} %get-tuple-element.30.work, f32[3,32,3072]{2,1,0:T(8,128)S(1)} %copy-done.1, ...), custom_call_target="tpu_custom_call" | custom-call | bytes 3000000 | tf_op jit(solution)/shard_map/pallas_call | solution.py:721
  38.1 10.0 %all_to_all.10.sums = f32[32,1,384]{2,1,0:T(1,128)S(1)} all-to-all(f32[32,1,384]{2,1,0:T(1,128)S(1)} %get-tuple-element.36), channel_id=1, replica_groups=mesh['gx'=4,'gy'=8] {'gx','gy'}, dimensions={0} | all-to-all | bytes 98304 | tf_op jit(solution)/shard_map/all_to_all | solution.py:731
  48.1 3.7 %shard_map.60 = (f32[9,1,32,8,128]{4,3,2,1,0:T(8,128)S(1)}, f32[9,32,128]{2,1,0:T(8,128)S(1)}, f32[18,24,128]{2,1,0:T(8,128)S(1)}, f32[18,24,128]{2,1,0:T(8,128)S(1)}) custom-call(s32[128]{0:T(128)S(1)} %get-tuple-element.28.work, f32[32,8,128]{2,1,0:T(8,128)S(1)} %get-tuple-element.29.slots, f32[3,32,128]{2,1,0:T(8,128)S(1)} %get-tuple-element.35.seen, ...), custom_call_target="tpu_custom_call" | custom-call | bytes 3000000 | tf_op jit(solution)/shard_map/pallas_call | solution.py:735
  51.8 0.4 collective-permute-start.4
  52.2 3.3 %collective-permute-start.5 = (f32[18,24,128]{2,1,0:T(8,128)S(1)}, f32[18,24,128]{2,1,0:T(8,128)S(1)}, u32[]{:S(2)}, u32[]{:S(2)}) collective-permute-start(f32[18,24,128]{2,1,0:T(8,128)S(1)} %get-tuple-element.41), channel_id=1, source_target_pairs={{8,16},{16,8},{9,17},{17,9},{10,18},{18,10},{11,19},{19,11},{12,20... | collective-permute-start | bytes 663560 | tf_op jit(solution)/shard_map/ppermute | solution.py:671
  55.4 9.3 %shard_map.61.inner = f32[9,3,32,8,128]{4,3,2,1,0:T(8,128)S(1)} custom-call(s32[128]{0:T(128)S(1)} %get-tuple-element.38.work, f32[32,8,128]{2,1,0:T(8,128)S(1)} %get-tuple-element.29.slots, f32[9,32,128]{2,1,0:T(8,128)S(1)} %get-tuple-element.39.weight), custom_call_target="tpu_custom_call" | custom-call | bytes 18000000 | tf_op jit(solution)/shard_map/pallas_call | solution.py:744
  64.8 0.0 collective-permute-done.4.x_near
  64.8 0.0 collective-permute-done.5.x_far
  64.8 0.3 shard_map.63
  65.1 0.3 collective-permute-start.6
  65.4 2.3 %collective-permute-start.7 = (f32[456,128]{1,0:T(8,128)S(1)}, f32[456,128]{1,0:T(8,128)S(1)}, u32[]{:S(2)}, u32[]{:S(2)}) collective-permute-start(f32[456,128]{1,0:T(8,128)S(1)} %get-tuple-element.50), channel_id=1, source_target_pairs={{1,2},{3,4},{5,6},{2,1},{4,3},{6,5},{9,10},{11,12},{13,14},{10,9},... | collective-permute-start | bytes 700424 | tf_op jit(solution)/shard_map/ppermute | solution.py:671
  67.7 6.4 %shard_map.62 = (f32[3,32,3072]{2,1,0:T(8,128)S(1)}, f32[3,2,4,48,128]{4,3,2,1,0:T(8,128)S(1)}, f32[3,2,4,48,128]{4,3,2,1,0:T(8,128)S(1)}, f32[3,2,4,48,128]{4,3,2,1,0:T(8,128)S(1)}) custom-call(f32[9,1,32,8,128]{4,3,2,1,0:T(8,128)S(1)} %get-tuple-element.37.outer, f32[9,3,32,8,128]{4,3,2,1,0:T(8,128)S(1)} %shard_map.61.inner, ...), custom_call_target="tpu_custom_call" | custom-call | bytes 24000000 | tf_op jit(solution)/shard_map/pallas_call | solution.py:758
  74.1 0.0 collective-permute-done.6.y_near
  74.1 0.0 collective-permute-done.7.y_far
  74.1 2.5 %shard_map.64 = f32[3,32,3072]{2,1,0:T(8,128)} custom-call(f32[3,32,3072]{2,1,0:T(8,128)S(1)} %get-tuple-element.45.part, f32[3,2,4,48,128]{4,3,2,1,0:T(8,128)S(1)} %get-tuple-element.46.e1, f32[3,2,4,48,128]{4,3,2,1,0:T(8,128)S(1)} %get-tuple-element.47.e2, f32[3,2,4,48,128]{4,3,2,1,0:T(8,128)S(1)} %get-tuple-element.48.e3, ...), custom_call_target="tpu_custom_call" | custom-call | bytes 3000000 | tf_op jit(solution)/shard_map/pallas_call | solution.py:766
Async XLA Ops:
  0.0 1.3 %copy-start = (f32[3,32,3072]{2,1,0:T(8,128)S(1)}, f32[3,32,3072]{2,1,0:T(8,128)}, u32[]{:S(2)}) copy-start(f32[3,32,3072]{2,1,0:T(8,128)} %state.3) | copy-start | bytes 3538948
  1.3 13.1 %copy-start.1 = (f32[3,32,3072]{2,1,0:T(8,128)S(1)}, f32[3,32,3072]{2,1,0:T(8,128)}, u32[]{:S(2)}) copy-start(f32[3,32,3072]{2,1,0:T(8,128)} %state.3) | copy-start | bytes 3538948
  1.4 12.9 %collective-permute-start = (f32[16,3072]{1,0:T(8,128)S(1)}, f32[16,3072]{1,0:T(8,128)S(1)}, u32[]{:S(2)}, u32[]{:S(2)}) collective-permute-start(f32[16,3072]{1,0:T(8,128)S(1)} %get-tuple-element.31), channel_id=1, source_target_pairs={{0,8},{16,24},{8,0},{24,16},{1,9},{17,25},{9,1},{25,17},{2,10},{18... | collective-permute-start | bytes 589832 | tf_op jit(solution)/shard_map/ppermute | solution.py:671
  2.7 11.6 %collective-permute-start.1 = (f32[16,3072]{1,0:T(8,128)S(1)}, f32[16,3072]{1,0:T(8,128)S(1)}, u32[]{:S(2)}, u32[]{:S(2)}) collective-permute-start(f32[16,3072]{1,0:T(8,128)S(1)} %get-tuple-element.32), channel_id=1, source_target_pairs={{8,16},{16,8},{9,17},{17,9},{10,18},{18,10},{11,19},{19,11},{12,20... | collective-permute-start | bytes 589832 | tf_op jit(solution)/shard_map/ppermute | solution.py:671
  7.2 14.2 %all-to-all-start = ((f32[32,8,128]{2,1,0:T(8,128)}), f32[32,8,128]{2,1,0:T(8,128)S(1)}, u32[]{:S(2)}, u32[]{:S(2)}) async-start(f32[32,8,128]{2,1,0:T(8,128)} %shard_map.55), calls=%async_computation | async-start | bytes 262144 | tf_op jit(solution)/shard_map/all_to_all | solution.py:701
  14.5 8.3 %collective-permute-start.2 = (f32[448,128]{1,0:T(8,128)S(1)}, f32[448,128]{1,0:T(8,128)S(1)}, u32[]{:S(2)}, u32[]{:S(2)}) collective-permute-start(f32[448,128]{1,0:T(8,128)S(1)} %get-tuple-element.33), channel_id=1, source_target_pairs={{0,1},{2,3},{4,5},{6,7},{1,0},{3,2},{5,4},{7,6},{8,9},{10,11},{12,... | collective-permute-start | bytes 688136 | tf_op jit(solution)/shard_map/ppermute | solution.py:671
  15.0 7.8 %collective-permute-start.3 = (f32[448,128]{1,0:T(8,128)S(1)}, f32[448,128]{1,0:T(8,128)S(1)}, u32[]{:S(2)}, u32[]{:S(2)}) collective-permute-start(f32[448,128]{1,0:T(8,128)S(1)} %get-tuple-element.34), channel_id=1, source_target_pairs={{1,2},{3,4},{5,6},{2,1},{4,3},{6,5},{9,10},{11,12},{13,14},{10,9},... | collective-permute-start | bytes 688136 | tf_op jit(solution)/shard_map/ppermute | solution.py:671
  51.8 13.0 %collective-permute-start.4 = (f32[18,24,128]{2,1,0:T(8,128)S(1)}, f32[18,24,128]{2,1,0:T(8,128)S(1)}, u32[]{:S(2)}, u32[]{:S(2)}) collective-permute-start(f32[18,24,128]{2,1,0:T(8,128)S(1)} %get-tuple-element.40), channel_id=1, source_target_pairs={{0,8},{16,24},{8,0},{24,16},{1,9},{17,25},{9,1},{25,17},{2,10},{18... | collective-permute-start | bytes 663560 | tf_op jit(solution)/shard_map/ppermute | solution.py:671
  52.2 12.6 %collective-permute-start.5 = (f32[18,24,128]{2,1,0:T(8,128)S(1)}, f32[18,24,128]{2,1,0:T(8,128)S(1)}, u32[]{:S(2)}, u32[]{:S(2)}) collective-permute-start(f32[18,24,128]{2,1,0:T(8,128)S(1)} %get-tuple-element.41), channel_id=1, source_target_pairs={{8,16},{16,8},{9,17},{17,9},{10,18},{18,10},{11,19},{19,11},{12,20... | collective-permute-start | bytes 663560 | tf_op jit(solution)/shard_map/ppermute | solution.py:671
  65.1 9.0 %collective-permute-start.6 = (f32[456,128]{1,0:T(8,128)S(1)}, f32[456,128]{1,0:T(8,128)S(1)}, u32[]{:S(2)}, u32[]{:S(2)}) collective-permute-start(f32[456,128]{1,0:T(8,128)S(1)} %get-tuple-element.49), channel_id=1, source_target_pairs={{0,1},{2,3},{4,5},{6,7},{1,0},{3,2},{5,4},{7,6},{8,9},{10,11},{12,... | collective-permute-start | bytes 700424 | tf_op jit(solution)/shard_map/ppermute | solution.py:671
  65.4 8.7 %collective-permute-start.7 = (f32[456,128]{1,0:T(8,128)S(1)}, f32[456,128]{1,0:T(8,128)S(1)}, u32[]{:S(2)}, u32[]{:S(2)}) collective-permute-start(f32[456,128]{1,0:T(8,128)S(1)} %get-tuple-element.50), channel_id=1, source_target_pairs={{1,2},{3,4},{5,6},{2,1},{4,3},{6,5},{9,10},{11,12},{13,14},{10,9},... | collective-permute-start | bytes 700424 | tf_op jit(solution)/shard_map/ppermute | solution.py:671
